TPU v7x, 32 devices: a whole 2x2x4 slice. The times are simulated.
32 devices in a mesh: gauss: 8 (over z, x), view: 4 (over y, core).
Axes of the slice: x: 2, y: 2, z: 4, core: 2. Of those that a mesh axis runs over, the one named last changes fastest.
Arguments:
- params: bfloat16 [64, 8192], P(None, 'gauss'), may hold values from -5 to 2, as said below
- lists: int32 [128, 128], P(('gauss', 'view')), may hold values from -1 to 8191, as said below
- tile_pos: int32 [128], P(('gauss', 'view')), may hold values from 0 to 255
- cam_index: int32 [128], P(('gauss', 'view')), may hold values from 0 to 15
- cams: float32 [28, 16], replicated, may hold values from -1 to 1100, as said below
- targets: float32 [3, 128, 256], P(None, ('gauss', 'view')), may hold values from 0 to 1
Outputs:
- rendered: float32 [3, 128, 256], P(None, ('gauss', 'view'))
- grads: float32 [64, 8192], P(None, 'gauss')
Inputs may be any that keep to these rules, and one draw needn't show every extreme that they name: `lists`: within each tile the entries that are not -1 come first. The entries of one device's 4 tiles that are not -1 name at most 64 times Gaussians of one gauss index (blocks of 1024 consecutive Gaussians), and in every draw some gauss index is named exactly 64 times by the tiles of every device; the number of entries that are not -1 differs from device to device. `cams`: columns are cameras: rows 0-8 a rotation matrix, 9-11 a translation putting every Gaussian mean at depth 2.4 or more, row 12 the focal length, rows 13-27 appearance weights. `params`: rows 6-9 are quaternions whose first component is 1 or more.
All inputs are finite; a program needn't handle non-finite values.
Results may differ from a plain program's by a relative error of at most 0.0003.
Values may be sent and summed in bfloat16 or wider, within the bound.
No kernel may reach another device: no remote copies, remote signals or barrier semaphores. Data moves between devices by JAX's collectives and lax.ppermute only.
A program may use at most 64 MiB of HBM per device.

v0:
```python
import functools
import math

import jax
import jax.numpy as jnp
from jax import lax
from jax.experimental import pallas as pl
from jax.experimental.pallas import tpu as pltpu
from jax.sharding import PartitionSpec as P

WIN = 16
SIDE = 16
LANES = 128
LOG2E = math.log2(math.e)
F32 = jnp.float32
BF16 = jnp.bfloat16
VMEM_LIMIT = 24 * 2**20
SENT = 32


def sh_terms(x, y, z):
    xx, yy, zz = x * x, y * y, z * z
    xy = x * y
    diff = xx - yy
    five = 5.0 * zz - 1.0
    return [
        x,
        y,
        z,
        xy,
        y * z,
        x * z,
        diff,
        3.0 * zz - 1.0,
        x * (xx - 3.0 * yy),
        xy * z,
        y * (3.0 * xx - yy),
        z * diff,
        x * five,
        y * five,
        z * (5.0 * zz - 3.0),
    ]


def project(rows, cam, live):
    mx, my, mz = rows[0], rows[1], rows[2]
    cam_x = cam[0] * mx + cam[1] * my + cam[2] * mz + cam[9]
    cam_y = cam[3] * mx + cam[4] * my + cam[5] * mz + cam[10]
    cam_z = cam[6] * mx + cam[7] * my + cam[8] * mz + cam[11]
    cam_z = jnp.where(live, cam_z, 1.0)
    inv_z = 1.0 / cam_z
    qw, qx, qy, qz = rows[6], rows[7], rows[8], rows[9]
    qw = jnp.where(live, qw, 1.0)
    inv_q = lax.rsqrt(qw * qw + qx * qx + qy * qy + qz * qz)
    qw, qx, qy, qz = qw * inv_q, qx * inv_q, qy * inv_q, qz * inv_q
    rot = [
        [
            1.0 - 2.0 * (qy * qy + qz * qz),
            2.0 * (qx * qy - qw * qz),
            2.0 * (qx * qz + qw * qy),
        ],
        [
            2.0 * (qx * qy + qw * qz),
            1.0 - 2.0 * (qx * qx + qz * qz),
            2.0 * (qy * qz - qw * qx),
        ],
        [
            2.0 * (qx * qz - qw * qy),
            2.0 * (qy * qz + qw * qx),
            1.0 - 2.0 * (qx * qx + qy * qy),
        ],
    ]
    mixed = [
        [
            cam[3 * i] * rot[0][k] + cam[3 * i + 1] * rot[1][k] + cam[3 * i + 2] * rot[2][k]
            for k in range(3)
        ]
        for i in range(3)
    ]
    scale = cam[12] * inv_z
    ray_x, ray_y = cam_x * inv_z, cam_y * inv_z
    proj_u = [scale * (mixed[0][k] - ray_x * mixed[2][k]) for k in range(3)]
    proj_v = [scale * (mixed[1][k] - ray_y * mixed[2][k]) for k in range(3)]
    var = [jnp.exp(2.0 * rows[3 + k]) for k in range(3)]
    uv = [proj_u[k] * var[k] for k in range(3)]
    cov_a = sum(uv[k] * proj_u[k] for k in range(3)) + 0.3
    cov_b = sum(uv[k] * proj_v[k] for k in range(3))
    cov_c = sum(proj_v[k] * proj_v[k] * var[k] for k in range(3)) + 0.3
    inv_det = 1.0 / (cov_a * cov_c - cov_b * cov_b)
    inv_dist = lax.rsqrt(cam_x * cam_x + cam_y * cam_y + cam_z * cam_z)
    terms = sh_terms(cam_x * inv_dist, cam_y * inv_dist, cam_z * inv_dist)
    geometry = [cam_x * scale, cam_y * scale, cov_c * inv_det, -cov_b * inv_det, cov_a * inv_det]
    return geometry + terms, (ray_x, ray_y)


def iota(shape, dim):
    return lax.broadcasted_iota(jnp.int32, shape, dim)


def one_hot(mask):
    return jnp.where(mask, 1.0, 0.0).astype(BF16)


def dot(lhs, rhs, lhs_dim=1, rhs_dim=0):
    return lax.dot_general(
        lhs, rhs, (((lhs_dim,), (rhs_dim,)), ((), ())), preferred_element_type=F32
    )


def split(x, parts):
    out = []
    for _ in range(parts):
        head = x.astype(BF16)
        out.append(head)
        x = x - head.astype(F32)
    return out


def ranks(mask, tiles):
    rows, length = mask.shape
    bits = one_hot(mask)
    earlier = one_hot(iota((length, length), 0) < iota((length, length), 1))
    within = dot(bits, earlier)
    count = dot(bits, jnp.ones((length, length), BF16)).astype(BF16)
    here, there = iota((rows, rows), 0), iota((rows, rows), 1)
    above = one_hot((there < here) & (there >= here - lax.rem(here, tiles)))
    return (within + dot(above, count)).astype(jnp.int32)


def find(ids, base, tiles, cap, g_dev):
    local = ids - base
    mine = (local >= 0) & (local < g_dev)
    key = jnp.where(mine, ranks(mine, tiles), -1)
    rows, length = ids.shape
    slot = iota((cap, length), 0)
    found = []
    for r in range(0, rows, tiles):
        total = jnp.zeros((cap, length), jnp.int32)
        for t in range(r, r + tiles):
            total = total + jnp.where(key[t : t + 1, :] == slot, local[t : t + 1, :], 0)
        found.append(jnp.sum(total, axis=1, keepdims=True))
    return jnp.concatenate(found, axis=0)


def pick_kernel(tiles, cap, lists_ref, params_ref, picked_ref):
    width, g_dev = params_ref.shape
    where = find(lists_ref[...], lax.axis_index("gauss") * g_dev, tiles, cap, g_dev)
    hot = one_hot(where == iota((where.shape[0], g_dev), 1))
    wide = jnp.concatenate([params_ref[...], jnp.zeros((LANES - width, g_dev), BF16)], axis=0)
    picked_ref[...] = dot(hot, wide, 1, 1).astype(BF16)


def pick_pair_kernel(cap, peers, *refs):
    lists_refs, refs = refs[:peers], refs[peers:]
    own_ref, other_ref = refs[:2]
    picked_refs, refs = refs[2 : 2 + peers], refs[2 + peers :]
    lists_scratch, picked_scratch = refs
    tiles, length = lists_refs[0].shape
    width, g_dev = own_ref.shape
    me = lax.axis_index("gauss")
    first = me % 2 == 0
    for k in range(peers):
        lists_scratch[(me // 2) ^ k] = lists_refs[k][...]
    ids = lists_scratch[...].reshape(peers * tiles, length)
    where_own = find(ids, me * g_dev, tiles, cap, g_dev)
    where_other = find(ids, (me ^ 1) * g_dev, tiles, cap, g_dev)
    own, other = own_ref[...], other_ref[...]
    blank = jnp.zeros((width, g_dev), BF16)
    lanes = iota((peers * cap, g_dev), 1)
    picked = dot(
        one_hot(where_own == lanes),
        jnp.concatenate([jnp.where(first, own, blank), jnp.where(first, blank, own)], axis=0),
        1,
        1,
    ) + dot(
        one_hot(where_other == lanes),
        jnp.concatenate([jnp.where(first, blank, other), jnp.where(first, other, blank)], axis=0),
        1,
        1,
    )
    picked_scratch[...] = picked.astype(BF16).reshape(peers, cap, 2 * width)
    for k in range(peers):
        picked_refs[k][...] = picked_scratch[(me // 2) ^ k]


def by_tile(values, row):
    out = jnp.full(row.shape, values[-1])
    for t in range(len(values) - 1):
        out = jnp.where(row == t, values[t], out)
    return out


def prepare_kernel(
    owners,
    cap,
    g_dev,
    tile_pos_ref,
    cam_index_ref,
    cams_ref,
    lists_ref,
    params_ref,
    hot_ref,
    local_ref,
    copy_ref,
    cam_ref,
    pixel_ref,
):
    tiles, length = lists_ref.shape
    share = LANES // tiles
    depth = SIDE * SIDE // share
    cam_ids = [cam_index_ref[t] for t in range(tiles)]
    tile_row = iota((tiles, length), 0)
    for j in range(cams_ref.shape[0]):
        cam_ref[j] = by_tile([cams_ref[j, cam_ids[t]] for t in range(tiles)], tile_row)
    pos = [tile_pos_ref[t] for t in range(tiles)]
    lane = iota((depth, LANES), 1)
    origin_x = [(SIDE * (lax.rem(p, WIN) - WIN // 2)).astype(F32) + 0.5 for p in pos]
    pixel_ref[0] = by_tile(origin_x, lane // share) + (lane % SIDE).astype(F32)
    origin_y = [(SIDE * (lax.div(p, WIN) - WIN // 2)).astype(F32) + 0.5 for p in pos]
    pixel_row = iota((depth, LANES), 0) * (share // SIDE) + (lane % share) // SIDE
    pixel_ref[1] = by_tile(origin_y, lane // share) + pixel_row.astype(F32)

    slots = owners * cap
    ids = lists_ref[...]
    masks = [(ids >= o * g_dev) & (ids < (o + 1) * g_dev) for o in range(owners)]
    rank = ranks(jnp.concatenate([m.astype(jnp.int32) for m in masks], axis=0) > 0, tiles)
    place = jnp.full((tiles, length), -1, jnp.int32)
    local = jnp.zeros((tiles, length), jnp.int32)
    for o in range(owners):
        place = jnp.where(masks[o], rank[o * tiles : (o + 1) * tiles] + o * cap, place)
        local = jnp.where(masks[o], ids - o * g_dev, local)
    slot_iota = iota((slots, length), 0)
    hot_ref[...] = jnp.concatenate(
        [one_hot(slot_iota == place[t : t + 1, :]) for t in range(tiles)], axis=1
    )
    local_ref[...] = local.astype(F32)
    copy_ref[...] = params_ref[...]


def render_kernel(pieces, width, *refs):
    recv_refs, refs = refs[:pieces], refs[pieces:]
    lists_ref, hot_ref, local_ref, cam_ref, pixel_ref, targets_ref = refs[:6]
    pictures_ref, send_ref, rows_ref, table_ref, alpha_ref, weight_ref, part_ref = refs[6:13]
    tiles, length = lists_ref.shape
    share = LANES // tiles
    depth = SIDE * SIDE // share
    live = lists_ref[...] >= 0
    hot = hot_ref[...]

    if pieces == 1:
        listed = dot(recv_refs[0][...], hot, 0, 0)[:width]
    else:
        (recv_scratch,) = refs[13:]
        cap = recv_refs[0].shape[0]
        place = lax.axis_index("gauss") // 2
        for k in range(pieces):
            recv_scratch[place ^ k] = recv_refs[k][...]
        received = recv_scratch[...].reshape(pieces * cap, 2 * width)
        halves = [
            jnp.concatenate(
                [hot[(2 * p + j) * cap : (2 * p + j + 1) * cap] for p in range(pieces)], axis=0
            )
            for j in range(2)
        ]
        listed = dot(received, halves[0], 0, 0)[:width] + dot(received, halves[1], 0, 0)[width:]
    for t in range(tiles):
        rows_ref[t * width : (t + 1) * width, :] = listed[:, t * length : (t + 1) * length]
    rows = [rows_ref[pl.ds(f, tiles, stride=width), :] for f in range(width)]

    cam = [cam_ref[j] for j in range(cam_ref.shape[0])]
    outs, pullback, rays = jax.vjp(lambda r: project(r, cam, live), rows[:10], has_aux=True)
    terms = outs[5:]
    colors = []
    for k in range(3):
        base = 11 + 16 * k
        shade = 0.5 + rows[base]
        for b in range(15):
            shade = shade + rows[base + 1 + b] * terms[b]
        for j in range(5):
            shade = shade + rows[59 + j] * cam[13 + 3 * j + k]
        colors.append(shade)
    opacity = jax.nn.sigmoid(rows[10])
    con_a, con_b, con_c = outs[2], outs[3], outs[4]

    attrs = [
        outs[0],
        outs[1],
        (-0.5 * LOG2E) * con_a,
        -LOG2E * con_b,
        (-0.5 * LOG2E) * con_c,
        jnp.where(live, opacity, 0.0),
    ] + colors
    count = len(attrs)
    blocks = []
    for value in attrs:
        parts = [p.astype(F32) for p in split(value, 3)]
        parts.append(jnp.zeros((16 - 3 * tiles, length), F32))
        blocks.append(jnp.concatenate(parts, axis=0))
    stacked = jnp.concatenate(blocks, axis=1)
    lane_tile = iota((16, LANES), 1) // share
    row_index = iota((16, LANES), 0)
    spread = one_hot((row_index % tiles == lane_tile) & (row_index < 3 * tiles))
    table = dot(stacked.T.astype(BF16), spread)
    pixel_x, pixel_y = pixel_ref[0, :1, :], pixel_ref[1]
    dx = pixel_x - table[:length]
    table_ref[0:length, :] = table[2 * length : 3 * length] * dx * dx
    table_ref[length : 2 * length, :] = table[3 * length : 4 * length] * dx
    table_ref[2 * length : 3 * length, :] = table[length : 2 * length]
    table_ref[3 * length :, :] = table[4 * length :]

    def row(index, l):
        return table_ref[pl.ds(index * length + l, 1), :]

    group = 16
    zero = jnp.zeros((depth, LANES), F32)

    def forward(chunk, carry):
        through, red, green, blue = carry
        for i in range(group):
            l = chunk * group + i
            dy = pixel_y - row(2, l)
            power = row(0, l) + dy * (row(1, l) + row(3, l) * dy)
            alpha = row(4, l) * jnp.exp2(power)
            weight = through * alpha
            red = red + weight * row(5, l)
            green = green + weight * row(6, l)
            blue = blue + weight * row(7, l)
            through = through - weight
            at = pl.ds(pl.multiple_of(l * depth, depth), depth)
            alpha_ref[at, :] = alpha
            weight_ref[at, :] = weight
        return through, red, green, blue

    start = (jnp.ones((depth, LANES), F32), zero, zero, zero)
    _, red, green, blue = lax.fori_loop(0, length // group, forward, start)
    pictures_ref[0] = red
    pictures_ref[1] = green
    pictures_ref[2] = blue
    res = [red - targets_ref[0], green - targets_ref[1], blue - targets_ref[2]]

    def backward(step, behind):
        chunk = length // group - 1 - step
        for i in reversed(range(group)):
            l = chunk * group + i
            at = pl.ds(pl.multiple_of(l * depth, depth), depth)
            alpha = alpha_ref[at, :]
            weight = weight_ref[at, :]
            dy = pixel_y - row(2, l)
            seen = row(5, l) * res[0] + row(6, l) * res[1] + row(7, l) * res[2]
            gap = seen - behind
            behind = behind + alpha * gap
            g = weight * gap
            gy = g * dy
            part_ref[0, at, :] = g
            part_ref[1, at, :] = gy
            part_ref[2, at, :] = gy * dy
            for k in range(3):
                part_ref[3 + k, at, :] = weight * res[k]
        return behind

    lax.fori_loop(0, length // group, backward, zero)

    def down(index):
        blocks = []
        for first in range(0, length, 8):
            parts = [
                part_ref[index, pl.ds(first * depth + s, 8, stride=depth), :] for s in range(depth)
            ]
            while len(parts) > 1:
                parts = [a + b for a, b in zip(parts[::2], parts[1::2])]
            blocks.append(parts[0])
        return jnp.concatenate(blocks, axis=0)

    sums = [down(index) for index in range(6)]
    g_x = sums[0] * dx
    sums = sums + [g_x, g_x * dx, sums[1] * dx]
    wide = jnp.concatenate([jnp.concatenate(split(s, 3), axis=1) for s in sums], axis=0)
    gather = one_hot(iota((8, 3 * LANES), 0) == (iota((8, 3 * LANES), 1) % LANES) // share)
    reduced = dot(gather, wide, 1, 1)
    g_0, g_y, g_yy, s_0, s_1, s_2, g_x, g_xx, g_xy = [
        reduced[:tiles, q * length : (q + 1) * length] for q in range(len(sums))
    ]

    d_colors = [s_0, s_1, s_2]
    d_terms = []
    for b in range(15):
        d_terms.append(sum(d_colors[k] * rows[12 + 16 * k + b] for k in range(3)))
    d_geometry = [
        con_a * g_x + con_b * g_y,
        con_b * g_x + con_c * g_y,
        -0.5 * g_xx,
        -g_xy,
        -0.5 * g_yy,
    ]
    (d_rows,) = pullback(d_geometry + d_terms)
    values = list(d_rows)
    values.append(g_0 * (1.0 - opacity))
    values.extend(d_colors)
    values.extend(rays)
    for j in range(5):
        values.append(sum(d_colors[k] * cam[13 + 3 * j + k] for k in range(3)))
    values.append(local_ref[...])
    values.extend([jnp.zeros((tiles, length), F32)] * (SENT - len(values)))
    for v in range(SENT):
        rows_ref[pl.ds(v, tiles, stride=width), :] = values[v]
    by_slot = jnp.concatenate(
        [
            jnp.concatenate(split(rows_ref[t * width : t * width + SENT, :], 3), axis=0)
            for t in range(tiles)
        ],
        axis=1,
    )
    by_slot = dot(by_slot, hot, 1, 1)
    by_slot = by_slot[:SENT] + by_slot[SENT : 2 * SENT] + by_slot[2 * SENT :]
    owners, copies, high, _ = send_ref.shape
    cap = hot.shape[0] // owners
    for o in range(owners):
        block = jnp.concatenate(
            [by_slot[r : r + high, o * cap : (o + 1) * cap] for r in range(0, SENT, high)], axis=1
        )
        for c in range(copies):
            send_ref[o, c] = block


def scatter_kernel(cap, recv_ref, out_ref, rows_ref):
    blocks, high, _ = recv_ref.shape
    width, g_dev = out_ref.shape

    def value(v):
        first = v // high * cap
        return recv_ref[:, v % high, first : first + cap]

    ray_x, ray_y = value(14), value(15)
    dir_z = lax.rsqrt(ray_x * ray_x + ray_y * ray_y + 1.0)
    terms = sh_terms(ray_x * dir_z, ray_y * dir_z, dir_z)
    features = [value(v) for v in range(11)]
    for k in range(3):
        color = value(11 + k)
        features.append(color)
        features.extend(color * term for term in terms)
    features.extend(value(v) for v in range(16, 21))
    for f in range(width):
        rows_ref[pl.ds(f, blocks, stride=width), :] = features[f]
    received = jnp.concatenate(
        [rows_ref[b * width : (b + 1) * width, :] for b in range(blocks)], axis=1
    )
    names = value(21).astype(jnp.int32)
    where = jnp.concatenate([names[b : b + 1, :] for b in range(blocks)], axis=1)
    hot = one_hot(iota((g_dev, blocks * cap), 0) == where)
    total = dot(jnp.concatenate(split(received, 2), axis=0), hot, 1, 1)
    out_ref[...] = total[:width] + total[width:]


def call(kernel, out_shape, args, scalars=0, scratch=()):
    in_specs = [pl.BlockSpec(memory_space=pltpu.SMEM)] * scalars
    in_specs += [pl.BlockSpec(memory_space=pltpu.VMEM)] * (len(args) - scalars)
    many = isinstance(out_shape, (list, tuple))
    spec = pl.BlockSpec(memory_space=pltpu.VMEM)
    return pl.pallas_call(
        kernel,
        out_shape=out_shape,
        in_specs=in_specs,
        out_specs=[spec] * len(out_shape) if many else spec,
        scratch_shapes=list(scratch),
        compiler_params=pltpu.CompilerParams(vmem_limit_bytes=VMEM_LIMIT),
    )(*args)


def swap(x, axis, k):
    return lax.ppermute(x, axis, [(i, i ^ k) for i in range(lax.axis_size(axis))])


def exchange(x):
    return lax.all_to_all(x, "gauss", split_axis=0, concat_axis=0, tiled=True)


def exchange_wide(x):
    owners, views = lax.axis_size("gauss"), lax.axis_size("view")
    blocks = x.reshape(owners * views // 2, *x.shape[2:])
    groups = [[i for i in range(owners * views) if i % 2 == c] for c in range(2)]
    return lax.all_to_all(
        blocks,
        ("gauss", "view"),
        split_axis=0,
        concat_axis=0,
        axis_index_groups=groups,
        tiled=True,
    )


def power_of_two(n):
    return n & (n - 1) == 0


def shape(dims, dtype):
    return jax.ShapeDtypeStruct(dims, dtype)


def on_device(params, lists, tile_pos, cam_index, cams, targets):
    owners = lax.axis_size("gauss")
    views = lax.axis_size("view")
    width, g_dev = params.shape
    tiles, length = lists.shape
    cap = max(tiles * length // owners, 16)
    slots = owners * cap
    share = LANES // tiles
    depth = SIDE * SIDE // share
    paired = 2 <= owners <= 16 and power_of_two(owners) and LANES == 2 * width
    peers = owners // 2 if paired else 1
    wide = views % 2 == 0 and owners * views <= 32

    if paired:
        other = swap(params, "gauss", 1)
        all_lists = [lists] + [swap(lists, "gauss", 2 * k) for k in range(1, peers)]
    hot, local, params_copy, cam, pixel = call(
        functools.partial(prepare_kernel, owners, cap, g_dev),
        [
            shape((slots, tiles * length), BF16),
            shape((tiles, length), F32),
            shape((width, g_dev), BF16),
            shape((cams.shape[0], tiles, length), F32),
            shape((2, depth, LANES), F32),
        ],
        (tile_pos, cam_index, cams, lists, params),
        scalars=3,
    )
    if paired:
        picked = call(
            functools.partial(pick_pair_kernel, cap, peers),
            [shape((cap, 2 * width), BF16)] * peers,
            (*all_lists, params_copy, other),
            scratch=(
                pltpu.VMEM((peers, tiles, length), jnp.int32),
                pltpu.VMEM((peers, cap, 2 * width), BF16),
            ),
        )
        returned = [picked[0]] + [swap(picked[k], "gauss", 2 * k) for k in range(1, peers)]
        recv_scratch = (pltpu.VMEM((peers, cap, 2 * width), BF16),)
    else:
        all_lists = exchange(jnp.broadcast_to(lists[None], (owners, tiles, length)))
        picked = call(
            functools.partial(pick_kernel, tiles, cap),
            shape((slots, LANES), BF16),
            (all_lists.reshape(owners * tiles, length), params_copy),
        )
        returned = [exchange(picked.reshape(owners, cap, LANES)).reshape(slots, LANES)]
        recv_scratch = ()
    spread_targets = (
        targets.reshape(3, tiles, depth, share).transpose(0, 2, 1, 3).reshape(3, depth, LANES)
    )
    copies = views // 2 if wide else 1
    high = SENT * cap // LANES
    pictures, sent = call(
        functools.partial(render_kernel, peers, width),
        [shape((3, depth, LANES), F32), shape((owners, copies, high, LANES), F32)],
        (*returned, lists, hot, local, cam, pixel, spread_targets),
        scratch=(
            pltpu.VMEM((tiles * width, length), F32),
            pltpu.VMEM((8 * length, LANES), F32),
            pltpu.VMEM((length * depth, LANES), F32),
            pltpu.VMEM((length * depth, LANES), F32),
            pltpu.VMEM((6, length * depth, LANES), F32),
        )
        + recv_scratch,
    )
    pictures = (
        pictures.reshape(3, depth, tiles, share)
        .transpose(0, 2, 1, 3)
        .reshape(3, tiles, SIDE * SIDE)
    )
    received = exchange_wide(sent) if wide else exchange(sent[:, 0])
    grads = call(
        functools.partial(scatter_kernel, cap),
        shape((width, g_dev), F32),
        (received,),
        scratch=(pltpu.VMEM((received.shape[0] * width, cap), F32),),
    )
    if wide:
        grads = grads + swap(grads, "view", 1)
    else:
        grads = lax.psum(grads, "view")
    return (pictures, grads)


def solution(mesh):
    return jax.shard_map(
        on_device,
        mesh=mesh,
        in_specs=(
            P(None, "gauss"),
            P(("gauss", "view"), None),
            P(("gauss", "view")),
            P(("gauss", "view")),
            P(),
            P(None, ("gauss", "view"), None),
        ),
        out_specs=(P(None, ("gauss", "view"), None), P(None, "gauss")),
        check_vma=False,
    )
```

profile of v0, /device:TPU:0, one launch (start us, length us, event | category | flops | bytes accessed | tf_op | source)
XLA Modules:
  0.0 40.9 jit_solution(15888751420219709766)
XLA Ops:
  0.6 0.0 copy-start.1
  0.6 0.0 copy-start.2
  0.7 0.0 copy-start.3
  0.7 3.0 %collective-permute-start.3 = (bf16[64,1024]{1,0:T(8,128)(2,1)}, bf16[64,1024]{1,0:T(8,128)(2,1)S(1)}, u32[]{:S(2)}, u32[]{:S(2)}) collective-permute-start(bf16[64,1024]{1,0:T(8,128)(2,1)} %params_ref.1), channel_id=1, source_target_pairs={{0,4},{4,0},{8,12},{12,8},{16,20},{20,16},{24,28},{28,24},{1,5},{5... | collective-permute-start | bytes 393224 | tf_op jit(solution)/shard_map/ppermute | solution.py:470
  3.7 1.6 %collective-permute-start = (s32[4,128]{1,0:T(4,128)}, s32[4,128]{1,0:T(4,128)S(1)}, u32[]{:S(2)}, u32[]{:S(2)}) collective-permute-start(s32[4,128]{1,0:T(4,128)} %refs_4_.1), channel_id=1, source_target_pairs={{0,8},{4,12},{8,0},{12,4},{16,24},{20,28},{24,16},{28,20},{1,9},{5... | collective-permute-start | bytes 6152 | tf_op jit(solution)/shard_map/ppermute | solution.py:470
  5.2 2.6 %collective-permute-start.1 = (s32[4,128]{1,0:T(4,128)}, s32[4,128]{1,0:T(4,128)S(1)}, u32[]{:S(2)}, u32[]{:S(2)}) collective-permute-start(s32[4,128]{1,0:T(4,128)} %refs_4_.1), channel_id=1, source_target_pairs={{0,16},{4,20},{8,24},{12,28},{16,0},{20,4},{24,8},{28,12},{1,17},{... | collective-permute-start | bytes 6152 | tf_op jit(solution)/shard_map/ppermute | solution.py:470
  7.8 0.2 collective-permute-start.2
  8.1 0.8 %copy.8.cams_ref = f32[28,16]{1,0:T(8,128)S(1)} copy(f32[28,16]{0,1:T(8,128)} %param.10) | data formatting | bytes 3584 | tf_op args[4]
  8.8 0.0 copy-done.1
  8.8 0.0 copy-done.2
  8.8 0.0 copy-done.3
  8.8 0.0 copy-start
  8.9 0.9 %copy-done = bf16[64,1024]{1,0:T(8,128)(2,1)S(1)} copy-done((bf16[64,1024]{1,0:T(8,128)(2,1)S(1)}, bf16[64,1024]{1,0:T(8,128)(2,1)}, u32[]{:S(2)}) %copy-start) | copy-done | bytes 131096
  9.8 1.3 %shard_map.77 = (bf16[512,512]{1,0:T(8,128)(2,1)S(1)}, f32[4,128]{1,0:T(4,128)S(1)}, bf16[64,1024]{1,0:T(8,128)(2,1)S(1)}, f32[28,4,128]{2,1,0:T(4,128)S(1)}, f32[2,8,128]{2,1,0:T(8,128)S(1)}) custom-call(s32[4]{0:T(128)S(1)} %copy-done.2, s32[4]{0:T(128)S(1)} %copy-done.3, f32[28,16]{1,0:T(8,128)S(1)} %copy.8.cams_ref, s32[4,128]{1,0:T(4,128)S(1)} %copy-done.1, ...), custom_call_target="tpu_custom_call" | custom-call | tf_op jit(solution)/shard_map/pallas_call | solution.py:459
  11.0 0.0 collective-permute-done.refs_1_
  11.1 0.0 collective-permute-done.1.refs_2_
  11.1 2.4 %collective-permute-done.2.refs_3_ = s32[4,128]{1,0:T(4,128)S(1)} collective-permute-done((s32[4,128]{1,0:T(4,128)}, s32[4,128]{1,0:T(4,128)S(1)}, u32[]{:S(2)}, u32[]{:S(2)}) %collective-permute-start.2) | collective-permute-done | bytes 2080 | tf_op jit(solution)/shard_map/ppermute | solution.py:470
  13.4 0.0 collective-permute-done.3.refs_5_
  13.4 0.0 copy-start.4
  13.4 1.0 %shard_map.78 = (bf16[64,128]{1,0:T(8,128)(2,1)S(1)}, bf16[64,128]{1,0:T(8,128)(2,1)S(1)}, bf16[64,128]{1,0:T(8,128)(2,1)S(1)}, bf16[64,128]{1,0:T(8,128)(2,1)S(1)}) custom-call(s32[4,128]{1,0:T(4,128)S(1)} %copy-done.1, s32[4,128]{1,0:T(4,128)S(1)} %collective-permute-done.refs_1_, s32[4,128]{1,0:T(4,128)S(1)} %collective-permute-done.1.refs_2_, ...), custom_call_target="tpu_custom_call" | custom-call | tf_op jit(solution)/shard_map/pallas_call | solution.py:459
  14.5 0.1 collective-permute-start.4
  14.5 1.8 %collective-permute-start.5 = (bf16[64,128]{1,0:T(8,128)(2,1)S(1)}, bf16[64,128]{1,0:T(8,128)(2,1)S(1)}, u32[]{:S(2)}, u32[]{:S(2)}) collective-permute-start(bf16[64,128]{1,0:T(8,128)(2,1)S(1)} %get-tuple-element.16), channel_id=1, source_target_pairs={{0,16},{4,20},{8,24},{12,28},{16,0},{20,4},{24,8},{28,12},{1,17},{... | collective-permute-start | bytes 49160 | tf_op jit(solution)/shard_map/ppermute | solution.py:470
  16.4 2.6 %collective-permute-start.6 = (bf16[64,128]{1,0:T(8,128)(2,1)S(1)}, bf16[64,128]{1,0:T(8,128)(2,1)S(1)}, u32[]{:S(2)}, u32[]{:S(2)}) collective-permute-start(bf16[64,128]{1,0:T(8,128)(2,1)S(1)} %get-tuple-element.17), channel_id=1, source_target_pairs={{0,24},{4,28},{8,16},{12,20},{16,8},{20,12},{24,0},{28,4},{1,25},{... | collective-permute-start | bytes 49160 | tf_op jit(solution)/shard_map/ppermute | solution.py:470
  18.9 0.0 copy-done.4
  18.9 0.1 reshape.19
  19.0 0.1 reshape.20.refs_9_
  19.1 0.0 collective-permute-done.4.refs_1_
  19.1 0.1 collective-permute-done.5.refs_2_
  19.3 2.6 %collective-permute-done.6.refs_3_ = bf16[64,128]{1,0:T(8,128)(2,1)S(1)} collective-permute-done((bf16[64,128]{1,0:T(8,128)(2,1)S(1)}, bf16[64,128]{1,0:T(8,128)(2,1)S(1)}, u32[]{:S(2)}, u32[]{:S(2)}) %collective-permute-start.6) | collective-permute-done | bytes 16416 | tf_op jit(solution)/shard_map/ppermute | solution.py:470
  21.9 2.6 %shard_map.79 = (f32[3,8,128]{2,1,0:T(8,128)S(1)}, f32[8,2,16,128]{3,2,1,0:T(8,128)S(1)}) custom-call(bf16[64,128]{1,0:T(8,128)(2,1)S(1)} %get-tuple-element.14.refs_0_, bf16[64,128]{1,0:T(8,128)(2,1)S(1)} %collective-permute-done.4.refs_1_, bf16[64,128]{1,0:T(8,128)(2,1)S(1)} %collective-permute-done.5.refs_2_, ...), custom_call_target="tpu_custom_call" | custom-call | tf_op jit(solution)/shard_map/pallas_call | solution.py:459
  24.6 12.5 %all_to_all.5.recv_ref = f32[16,16,128]{2,1,0:T(8,128)S(1)} all-to-all(f32[16,16,128]{2,1,0:T(8,128)S(1)} %bitcast.7), channel_id=1, replica_groups={{0,2,4,6,8,10,12,14,16,18,20,22,24,26,28,30},{1,3,5,7,9,11,13,15,17,19,..., dimensions={0} | all-to-all | bytes 262144 | tf_op jit(solution)/shard_map/all_to_all | solution.py:481
  37.0 1.6 %shard_map.80 = f32[64,1024]{1,0:T(8,128)S(1)} custom-call(f32[16,16,128]{2,1,0:T(8,128)S(1)} %all_to_all.5.recv_ref), custom_call_target="tpu_custom_call" | custom-call | tf_op jit(solution)/shard_map/pallas_call | solution.py:459
  38.6 0.1 collective-permute-start.7
  38.7 0.1 reshape.21
  38.8 0.7 %reshape.22 = f32[3,4,256]{2,1,0:T(4,128)} reshape(f32[3,4,8,32]{3,2,1,0:T(8,128)S(1)} %copy.10) | data formatting | bytes 24576 | tf_op jit(solution)/shard_map/reshape | solution.py:569
  39.5 0.7 %collective-permute-done.7 = f32[64,1024]{1,0:T(8,128)S(1)} collective-permute-done((f32[64,1024]{1,0:T(8,128)S(1)}, f32[64,1024]{1,0:T(8,128)S(1)}, u32[]{:S(2)}, u32[]{:S(2)}) %collective-permute-start.7) | collective-permute-done | bytes 262176 | tf_op jit(solution)/shard_map/ppermute | solution.py:470
  40.2 0.7 %add.3 = f32[64,1024]{1,0:T(8,128)} add(f32[64,1024]{1,0:T(8,128)S(1)} %shard_map.80, f32[64,1024]{1,0:T(8,128)S(1)} %collective-permute-done.7) | non-fusion elementwise | flops 65536 | bytes 786432 | tf_op jit(solution)/shard_map/add | solution.py:579
  (2 shorter events, 0.0 us)
Async XLA Ops:
  0.6 8.2 %copy-start.1 = (s32[4,128]{1,0:T(4,128)S(1)}, s32[4,128]{1,0:T(4,128)}, u32[]{:S(2)}) copy-start(s32[4,128]{1,0:T(4,128)} %refs_4_.1) | copy-start | bytes 6148
  0.6 8.2 %copy-start.2 = (s32[4]{0:T(128)S(1)}, s32[4]{0:T(128)}, u32[]{:S(2)}) copy-start(s32[4]{0:T(128)} %tile_pos_ref.1) | copy-start | bytes 52
  0.7 8.2 %copy-start.3 = (s32[4]{0:T(128)S(1)}, s32[4]{0:T(128)}, u32[]{:S(2)}) copy-start(s32[4]{0:T(128)} %cam_index_ref.1) | copy-start | bytes 52
  0.7 12.8 %collective-permute-start.3 = (bf16[64,1024]{1,0:T(8,128)(2,1)}, bf16[64,1024]{1,0:T(8,128)(2,1)S(1)}, u32[]{:S(2)}, u32[]{:S(2)}) collective-permute-start(bf16[64,1024]{1,0:T(8,128)(2,1)} %params_ref.1), channel_id=1, source_target_pairs={{0,4},{4,0},{8,12},{12,8},{16,20},{20,16},{24,28},{28,24},{1,5},{5... | collective-permute-start | bytes 393224 | tf_op jit(solution)/shard_map/ppermute | solution.py:470
  3.7 7.4 %collective-permute-start = (s32[4,128]{1,0:T(4,128)}, s32[4,128]{1,0:T(4,128)S(1)}, u32[]{:S(2)}, u32[]{:S(2)}) collective-permute-start(s32[4,128]{1,0:T(4,128)} %refs_4_.1), channel_id=1, source_target_pairs={{0,8},{4,12},{8,0},{12,4},{16,24},{20,28},{24,16},{28,20},{1,9},{5... | collective-permute-start | bytes 6152 | tf_op jit(solution)/shard_map/ppermute | solution.py:470
  5.2 5.8 %collective-permute-start.1 = (s32[4,128]{1,0:T(4,128)}, s32[4,128]{1,0:T(4,128)S(1)}, u32[]{:S(2)}, u32[]{:S(2)}) collective-permute-start(s32[4,128]{1,0:T(4,128)} %refs_4_.1), channel_id=1, source_target_pairs={{0,16},{4,20},{8,24},{12,28},{16,0},{20,4},{24,8},{28,12},{1,17},{... | collective-permute-start | bytes 6152 | tf_op jit(solution)/shard_map/ppermute | solution.py:470
  7.8 5.6 %collective-permute-start.2 = (s32[4,128]{1,0:T(4,128)}, s32[4,128]{1,0:T(4,128)S(1)}, u32[]{:S(2)}, u32[]{:S(2)}) collective-permute-start(s32[4,128]{1,0:T(4,128)} %refs_4_.1), channel_id=1, source_target_pairs={{0,24},{4,28},{8,16},{12,20},{16,8},{20,12},{24,0},{28,4},{1,25},{... | collective-permute-start | bytes 6152 | tf_op jit(solution)/shard_map/ppermute | solution.py:470
  8.8 0.9 %copy-start = (bf16[64,1024]{1,0:T(8,128)(2,1)S(1)}, bf16[64,1024]{1,0:T(8,128)(2,1)}, u32[]{:S(2)}) copy-start(bf16[64,1024]{1,0:T(8,128)(2,1)} %params_ref.1) | copy-start | bytes 393220
  13.4 5.5 %copy-start.4 = (f32[3,4,256]{2,1,0:T(4,128)S(1)}, f32[3,4,256]{2,1,0:T(4,128)}, u32[]{:S(2)}) copy-start(f32[3,4,256]{2,1,0:T(4,128)} %param.11) | copy-start | bytes 36868
  14.5 4.7 %collective-permute-start.4 = (bf16[64,128]{1,0:T(8,128)(2,1)S(1)}, bf16[64,128]{1,0:T(8,128)(2,1)S(1)}, u32[]{:S(2)}, u32[]{:S(2)}) collective-permute-start(bf16[64,128]{1,0:T(8,128)(2,1)S(1)} %get-tuple-element.15), channel_id=1, source_target_pairs={{0,8},{4,12},{8,0},{12,4},{16,24},{20,28},{24,16},{28,20},{1,9},{5... | collective-permute-start | bytes 49160 | tf_op jit(solution)/shard_map/ppermute | solution.py:470
  14.5 4.7 %collective-permute-start.5 = (bf16[64,128]{1,0:T(8,128)(2,1)S(1)}, bf16[64,128]{1,0:T(8,128)(2,1)S(1)}, u32[]{:S(2)}, u32[]{:S(2)}) collective-permute-start(bf16[64,128]{1,0:T(8,128)(2,1)S(1)} %get-tuple-element.16), channel_id=1, source_target_pairs={{0,16},{4,20},{8,24},{12,28},{16,0},{20,4},{24,8},{28,12},{1,17},{... | collective-permute-start | bytes 49160 | tf_op jit(solution)/shard_map/ppermute | solution.py:470
  16.4 5.5 %collective-permute-start.6 = (bf16[64,128]{1,0:T(8,128)(2,1)S(1)}, bf16[64,128]{1,0:T(8,128)(2,1)S(1)}, u32[]{:S(2)}, u32[]{:S(2)}) collective-permute-start(bf16[64,128]{1,0:T(8,128)(2,1)S(1)} %get-tuple-element.17), channel_id=1, source_target_pairs={{0,24},{4,28},{8,16},{12,20},{16,8},{20,12},{24,0},{28,4},{1,25},{... | collective-permute-start | bytes 49160 | tf_op jit(solution)/shard_map/ppermute | solution.py:470
  38.6 1.6 %collective-permute-start.7 = (f32[64,1024]{1,0:T(8,128)S(1)}, f32[64,1024]{1,0:T(8,128)S(1)}, u32[]{:S(2)}, u32[]{:S(2)}) collective-permute-start(f32[64,1024]{1,0:T(8,128)S(1)} %shard_map.80), channel_id=1, source_target_pairs={{0,1},{1,0},{2,3},{3,2},{4,5},{5,4},{6,7},{7,6},{8,9},{9,8},{10,11... | collective-permute-start | bytes 786440 | tf_op jit(solution)/shard_map/ppermute | solution.py:470
where the time goes:
time: 41.2 us; the launch traced here: 40.9 us
  blocking collectives  12.5 us (30%)
  starting transfers between devices  11.9 us (29%)
  Pallas kernels  6.51 us (16%)
  waiting for transfers between devices  5.89 us (14%)
  local copies, waits for them, and re-layouts  2.66 us (6%)
  between operations  0.76 us (2%)
  other arithmetic  0.73 us (2%)
    all_to_all x1, blocking collectives, exchange_wide(): lax.all_to_all(blocks, ('gauss', 'view'), split_axis=0, concat_axis=0, ax...  12.5 us
    ppermute x8, starting transfers between devices, swap(): lax.ppermute(x, axis, [(i, i ^ k) for i in range(lax.axis_size(axis))])  11.9 us
    pallas_call x4, Pallas kernels, call(): pl.pallas_call(kernel, out_shape=out_shape, in_specs=in_specs, out_specs=...  6.51 us
    ppermute x8, waiting for transfers between devices, swap(): lax.ppermute(x, axis, [(i, i ^ k) for i in range(lax.axis_size(axis))])  5.89 us
    unnamed x11, local copies, waits for them, and re-layouts  1.7 us
  transfers between devices with their start and end apart: 8, of which 4 were waited for; matrix products, arithmetic and copies ran while one was open for 4% of the time, Pallas kernels for 3%

commit v1 on v0

--- a/solution.py
+++ b/solution.py
@@ -160,7 +160,7 @@
     me = lax.axis_index("gauss")
     first = me % 2 == 0
     for k in range(peers):
-        lists_scratch[(me // 2) ^ k] = lists_refs[k][...]
+        lists_scratch[(me // 2) ^ k] = lists_refs[peers - 1 - k][...]
     ids = lists_scratch[...].reshape(peers * tiles, length)
     where_own = find(ids, me * g_dev, tiles, cap, g_dev)
     where_other = find(ids, (me ^ 1) * g_dev, tiles, cap, g_dev)
@@ -180,7 +180,7 @@
     )
     picked_scratch[...] = picked.astype(BF16).reshape(peers, cap, 2 * width)
     for k in range(peers):
-        picked_refs[k][...] = picked_scratch[(me // 2) ^ k]
+        picked_refs[peers - 1 - k][...] = picked_scratch[(me // 2) ^ k]
 
 
 def by_tile(values, row):
@@ -248,13 +248,13 @@
     hot = hot_ref[...]
 
     if pieces == 1:
-        listed = dot(recv_refs[0][...], hot, 0, 0)[:width]
+        listed = dot(recv_refs[0][...].reshape(-1, LANES), hot, 0, 0)[:width]
     else:
         (recv_scratch,) = refs[13:]
         cap = recv_refs[0].shape[0]
         place = lax.axis_index("gauss") // 2
         for k in range(pieces):
-            recv_scratch[place ^ k] = recv_refs[k][...]
+            recv_scratch[place ^ k] = recv_refs[pieces - 1 - k][...]
         received = recv_scratch[...].reshape(pieces * cap, 2 * width)
         halves = [
             jnp.concatenate(
@@ -422,33 +422,31 @@
             send_ref[o, c] = block
 
 
-def scatter_kernel(cap, recv_ref, out_ref, rows_ref):
-    blocks, high, _ = recv_ref.shape
-    width, g_dev = out_ref.shape
-
-    def value(v):
-        first = v // high * cap
-        return recv_ref[:, v % high, first : first + cap]
-
-    ray_x, ray_y = value(14), value(15)
+def scatter_kernel(cap, recv_ref, out_ref):
+    blocks, high, lanes = recv_ref.shape
+    g_dev = out_ref.shape[1]
+    values = jnp.concatenate(
+        [
+            jnp.concatenate(
+                [recv_ref[b, :, first : first + cap] for b in range(blocks)], axis=1
+            )
+            for first in range(0, SENT * cap // high, cap)
+        ],
+        axis=0,
+    )
+    ray_x, ray_y = values[14:15], values[15:16]
     dir_z = lax.rsqrt(ray_x * ray_x + ray_y * ray_y + 1.0)
     terms = sh_terms(ray_x * dir_z, ray_y * dir_z, dir_z)
-    features = [value(v) for v in range(11)]
-    for k in range(3):
-        color = value(11 + k)
-        features.append(color)
-        features.extend(color * term for term in terms)
-    features.extend(value(v) for v in range(16, 21))
-    for f in range(width):
-        rows_ref[pl.ds(f, blocks, stride=width), :] = features[f]
-    received = jnp.concatenate(
-        [rows_ref[b * width : (b + 1) * width, :] for b in range(blocks)], axis=1
-    )
-    names = value(21).astype(jnp.int32)
-    where = jnp.concatenate([names[b : b + 1, :] for b in range(blocks)], axis=1)
-    hot = one_hot(iota((g_dev, blocks * cap), 0) == where)
-    total = dot(jnp.concatenate(split(received, 2), axis=0), hot, 1, 1)
-    out_ref[...] = total[:width] + total[width:]
+    terms = jnp.concatenate([jnp.ones_like(dir_z)] + terms, axis=0)
+    rows = [values] + [terms * values[11 + k : 12 + k] for k in range(3)]
+    hot = one_hot(iota((g_dev, blocks * cap), 0) == values[21:22].astype(jnp.int32))
+    parts = split(jnp.concatenate(rows, axis=0), 2)
+    total = dot(jnp.concatenate(parts, axis=0), hot, 1, 1)
+    count = total.shape[0] // 2
+    total = total[:count] + total[count:]
+    out_ref[:11, :] = total[:11]
+    out_ref[11:59, :] = total[SENT:]
+    out_ref[59:, :] = total[16:21]
 
 
 def call(kernel, out_shape, args, scalars=0, scratch=()):
@@ -470,6 +468,11 @@
     return lax.ppermute(x, axis, [(i, i ^ k) for i in range(lax.axis_size(axis))])
 
 
+def far_first(blocks):
+    last = len(blocks) - 1
+    return [swap(b, "gauss", 2 * (last - i)) if i < last else b for i, b in enumerate(blocks)]
+
+
 def exchange(x):
     return lax.all_to_all(x, "gauss", split_axis=0, concat_axis=0, tiled=True)
 
@@ -511,7 +514,7 @@
 
     if paired:
         other = swap(params, "gauss", 1)
-        all_lists = [lists] + [swap(lists, "gauss", 2 * k) for k in range(1, peers)]
+        all_lists = far_first([lists] * peers)
     hot, local, params_copy, cam, pixel = call(
         functools.partial(prepare_kernel, owners, cap, g_dev),
         [
@@ -534,8 +537,7 @@
                 pltpu.VMEM((peers, cap, 2 * width), BF16),
             ),
         )
-        returned = [picked[0]] + [swap(picked[k], "gauss", 2 * k) for k in range(1, peers)]
-        recv_scratch = (pltpu.VMEM((peers, cap, 2 * width), BF16),)
+        returned = far_first(picked)
     else:
         all_lists = exchange(jnp.broadcast_to(lists[None], (owners, tiles, length)))
         picked = call(
@@ -543,8 +545,7 @@
             shape((slots, LANES), BF16),
             (all_lists.reshape(owners * tiles, length), params_copy),
         )
-        returned = [exchange(picked.reshape(owners, cap, LANES)).reshape(slots, LANES)]
-        recv_scratch = ()
+        returned = [exchange(picked.reshape(owners, cap, LANES))]
     spread_targets = (
         targets.reshape(3, tiles, depth, share).transpose(0, 2, 1, 3).reshape(3, depth, LANES)
     )
@@ -560,8 +561,8 @@
             pltpu.VMEM((length * depth, LANES), F32),
             pltpu.VMEM((length * depth, LANES), F32),
             pltpu.VMEM((6, length * depth, LANES), F32),
-        )
-        + recv_scratch,
+            pltpu.VMEM((peers, *returned[0].shape[-2:]), BF16),
+        ),
     )
     pictures = (
         pictures.reshape(3, depth, tiles, share)
@@ -573,7 +574,6 @@
         functools.partial(scatter_kernel, cap),
         shape((width, g_dev), F32),
         (received,),
-        scratch=(pltpu.VMEM((received.shape[0] * width, cap), F32),),
     )
     if wide:
         grads = grads + swap(grads, "view", 1)

time: 41.2 us -> 38.6 us (0.937)
  waiting for transfers between devices: 5.89 us -> 4.43 us
  Pallas kernels: 6.51 us -> 5.88 us
  blocking collectives: 12.5 us -> 12 us
    ppermute x8, waiting for transfers between devices: 5.89 us -> 4.43 us  [swap(): lax.ppermute(x, axis, [(i, i ^ k) for i in range(lax.axis_size(axis))])]
    pallas_call x4, Pallas kernels: 6.51 us -> 5.88 us  [call(): pl.pallas_call(kernel, out_shape=out_shape, in_specs=in_specs, out_specs=...]
    all_to_all x1, blocking collectives: 12.5 us -> 12 us  [exchange_wide(): lax.all_to_all(blocks, ('gauss', 'view'), split_axis=0, concat_axis=0, ax...]
  transfers between devices with their start and end apart: 8 -> 8, of which waited for: 4 -> 4; matrix products, arithmetic and copies ran while one was open for 4% -> 5% of each run, Pallas kernels for 3% -> 3%
where the time goes in v1:
time: 38.6 us; the launch traced here: 38.3 us
  blocking collectives  12 us (31%)
  starting transfers between devices  11.9 us (31%)
  Pallas kernels  5.88 us (15%)
  waiting for transfers between devices  4.43 us (11%)
  local copies, waits for them, and re-layouts  2.66 us (7%)
  between operations  0.74 us (2%)
  other arithmetic  0.73 us (2%)
    all_to_all x1, blocking collectives, exchange_wide(): lax.all_to_all(blocks, ('gauss', 'view'), split_axis=0, concat_axis=0, ax...  12 us
    ppermute x8, starting transfers between devices, swap(): lax.ppermute(x, axis, [(i, i ^ k) for i in range(lax.axis_size(axis))])  11.9 us
    pallas_call x4, Pallas kernels, call(): pl.pallas_call(kernel, out_shape=out_shape, in_specs=in_specs, out_specs=...  5.88 us
    ppermute x8, waiting for transfers between devices, swap(): lax.ppermute(x, axis, [(i, i ^ k) for i in range(lax.axis_size(axis))])  4.43 us
    unnamed x11, local copies, waits for them, and re-layouts  1.7 us
  transfers between devices with their start and end apart: 8, of which 4 were waited for; matrix products, arithmetic and copies ran while one was open for 5% of the time, Pallas kernels for 3%

profile of v1, /device:TPU:0, one launch (start us, length us, event | category | flops | bytes accessed | tf_op | source)
XLA Modules:
  0.0 38.3 jit_solution(7630966212429622606)
XLA Ops:
  0.6 0.0 copy-start.1
  0.6 0.0 copy-start.2
  0.7 0.0 copy-start.3
  0.7 3.0 %collective-permute-start.3 = (bf16[64,1024]{1,0:T(8,128)(2,1)}, bf16[64,1024]{1,0:T(8,128)(2,1)S(1)}, u32[]{:S(2)}, u32[]{:S(2)}) collective-permute-start(bf16[64,1024]{1,0:T(8,128)(2,1)} %params_ref.1), channel_id=1, source_target_pairs={{0,4},{4,0},{8,12},{12,8},{16,20},{20,16},{24,28},{28,24},{1,5},{5... | collective-permute-start | bytes 393224 | tf_op jit(solution)/shard_map/ppermute | solution.py:468
  3.7 3.6 %collective-permute-start = (s32[4,128]{1,0:T(4,128)}, s32[4,128]{1,0:T(4,128)S(1)}, u32[]{:S(2)}, u32[]{:S(2)}) collective-permute-start(s32[4,128]{1,0:T(4,128)} %refs_4_.1), channel_id=1, source_target_pairs={{0,24},{4,28},{8,16},{12,20},{16,8},{20,12},{24,0},{28,4},{1,25},{... | collective-permute-start | bytes 6152 | tf_op jit(solution)/shard_map/ppermute | solution.py:468
  7.3 0.0 collective-permute-start.1
  7.3 0.8 %collective-permute-start.2 = (s32[4,128]{1,0:T(4,128)}, s32[4,128]{1,0:T(4,128)S(1)}, u32[]{:S(2)}, u32[]{:S(2)}) collective-permute-start(s32[4,128]{1,0:T(4,128)} %refs_4_.1), channel_id=1, source_target_pairs={{0,8},{4,12},{8,0},{12,4},{16,24},{20,28},{24,16},{28,20},{1,9},{5... | collective-permute-start | bytes 6152 | tf_op jit(solution)/shard_map/ppermute | solution.py:468
  8.1 0.8 %copy.8.cams_ref = f32[28,16]{1,0:T(8,128)S(1)} copy(f32[28,16]{0,1:T(8,128)} %param.10) | data formatting | bytes 3584 | tf_op args[4]
  8.8 0.0 copy-done.1
  8.8 0.0 copy-done.2
  8.8 0.0 copy-done.3
  8.8 0.0 copy-start
  8.9 0.9 %copy-done = bf16[64,1024]{1,0:T(8,128)(2,1)S(1)} copy-done((bf16[64,1024]{1,0:T(8,128)(2,1)S(1)}, bf16[64,1024]{1,0:T(8,128)(2,1)}, u32[]{:S(2)}) %copy-start) | copy-done | bytes 131096
  9.8 1.3 %shard_map.77 = (bf16[512,512]{1,0:T(8,128)(2,1)S(1)}, f32[4,128]{1,0:T(4,128)S(1)}, bf16[64,1024]{1,0:T(8,128)(2,1)S(1)}, f32[28,4,128]{2,1,0:T(4,128)S(1)}, f32[2,8,128]{2,1,0:T(8,128)S(1)}) custom-call(s32[4]{0:T(128)S(1)} %copy-done.2, s32[4]{0:T(128)S(1)} %copy-done.3, f32[28,16]{1,0:T(8,128)S(1)} %copy.8.cams_ref, s32[4,128]{1,0:T(4,128)S(1)} %copy-done.1, ...), custom_call_target="tpu_custom_call" | custom-call | tf_op jit(solution)/shard_map/pallas_call | solution.py:457
  11.0 0.0 collective-permute-done.refs_0_
  11.1 0.9 %collective-permute-done.1.refs_1_ = s32[4,128]{1,0:T(4,128)S(1)} collective-permute-done((s32[4,128]{1,0:T(4,128)}, s32[4,128]{1,0:T(4,128)S(1)}, u32[]{:S(2)}, u32[]{:S(2)}) %collective-permute-start.1) | collective-permute-done | bytes 2080 | tf_op jit(solution)/shard_map/ppermute | solution.py:468
  12.0 0.0 collective-permute-done.2.refs_2_
  12.0 0.0 collective-permute-done.3.refs_5_
  12.0 0.0 copy-start.4
  12.0 1.0 %shard_map.78 = (bf16[64,128]{1,0:T(8,128)(2,1)S(1)}, bf16[64,128]{1,0:T(8,128)(2,1)S(1)}, bf16[64,128]{1,0:T(8,128)(2,1)S(1)}, bf16[64,128]{1,0:T(8,128)(2,1)S(1)}) custom-call(s32[4,128]{1,0:T(4,128)S(1)} %collective-permute-done.refs_0_, s32[4,128]{1,0:T(4,128)S(1)} %collective-permute-done.1.refs_1_, s32[4,128]{1,0:T(4,128)S(1)} %collective-permute-done.2.refs_2_, ...), custom_call_target="tpu_custom_call" | custom-call | tf_op jit(solution)/shard_map/pallas_call | solution.py:457
  13.0 2.8 %collective-permute-start.4 = (bf16[64,128]{1,0:T(8,128)(2,1)S(1)}, bf16[64,128]{1,0:T(8,128)(2,1)S(1)}, u32[]{:S(2)}, u32[]{:S(2)}) collective-permute-start(bf16[64,128]{1,0:T(8,128)(2,1)S(1)} %get-tuple-element.14), channel_id=1, source_target_pairs={{0,24},{4,28},{8,16},{12,20},{16,8},{20,12},{24,0},{28,4},{1,25},{... | collective-permute-start | bytes 49160 | tf_op jit(solution)/shard_map/ppermute | solution.py:468
  15.8 0.0 collective-permute-start.5
  15.8 1.7 %collective-permute-start.6 = (bf16[64,128]{1,0:T(8,128)(2,1)S(1)}, bf16[64,128]{1,0:T(8,128)(2,1)S(1)}, u32[]{:S(2)}, u32[]{:S(2)}) collective-permute-start(bf16[64,128]{1,0:T(8,128)(2,1)S(1)} %get-tuple-element.16), channel_id=1, source_target_pairs={{0,8},{4,12},{8,0},{12,4},{16,24},{20,28},{24,16},{28,20},{1,9},{5... | collective-permute-start | bytes 49160 | tf_op jit(solution)/shard_map/ppermute | solution.py:468
  17.5 0.0 copy-done.4
  17.5 0.1 reshape.19
  17.6 0.1 reshape.20.refs_9_
  17.7 1.0 %collective-permute-done.4.refs_0_ = bf16[64,128]{1,0:T(8,128)(2,1)S(1)} collective-permute-done((bf16[64,128]{1,0:T(8,128)(2,1)S(1)}, bf16[64,128]{1,0:T(8,128)(2,1)S(1)}, u32[]{:S(2)}, u32[]{:S(2)}) %collective-permute-start.4) | collective-permute-done | bytes 16416 | tf_op jit(solution)/shard_map/ppermute | solution.py:468
  18.6 1.8 %collective-permute-done.5.refs_1_ = bf16[64,128]{1,0:T(8,128)(2,1)S(1)} collective-permute-done((bf16[64,128]{1,0:T(8,128)(2,1)S(1)}, bf16[64,128]{1,0:T(8,128)(2,1)S(1)}, u32[]{:S(2)}, u32[]{:S(2)}) %collective-permute-start.5) | collective-permute-done | bytes 16416 | tf_op jit(solution)/shard_map/ppermute | solution.py:468
  20.4 0.0 collective-permute-done.6.refs_2_
  20.4 2.6 %shard_map.79 = (f32[3,8,128]{2,1,0:T(8,128)S(1)}, f32[8,2,16,128]{3,2,1,0:T(8,128)S(1)}) custom-call(bf16[64,128]{1,0:T(8,128)(2,1)S(1)} %collective-permute-done.4.refs_0_, bf16[64,128]{1,0:T(8,128)(2,1)S(1)} %collective-permute-done.5.refs_1_, bf16[64,128]{1,0:T(8,128)(2,1)S(1)} %collective-permute-done.6.refs_2_, ...), custom_call_target="tpu_custom_call" | custom-call | tf_op jit(solution)/shard_map/pallas_call | solution.py:457
  23.1 12.0 %all_to_all.5.recv_ref = f32[16,16,128]{2,1,0:T(8,128)S(1)} all-to-all(f32[16,16,128]{2,1,0:T(8,128)S(1)} %bitcast.7), channel_id=1, replica_groups={{0,2,4,6,8,10,12,14,16,18,20,22,24,26,28,30},{1,3,5,7,9,11,13,15,17,19,..., dimensions={0} | all-to-all | bytes 262144 | tf_op jit(solution)/shard_map/all_to_all | solution.py:484
  35.0 0.9 %shard_map.80 = f32[64,1024]{1,0:T(8,128)S(1)} custom-call(f32[16,16,128]{2,1,0:T(8,128)S(1)} %all_to_all.5.recv_ref), custom_call_target="tpu_custom_call" | custom-call | tf_op jit(solution)/shard_map/pallas_call | solution.py:457
  36.0 0.1 collective-permute-start.7
  36.1 0.1 reshape.21
  36.2 0.7 %reshape.22 = f32[3,4,256]{2,1,0:T(4,128)} reshape(f32[3,4,8,32]{3,2,1,0:T(8,128)S(1)} %copy.10) | data formatting | bytes 24576 | tf_op jit(solution)/shard_map/reshape | solution.py:570
  36.8 0.7 %collective-permute-done.7 = f32[64,1024]{1,0:T(8,128)S(1)} collective-permute-done((f32[64,1024]{1,0:T(8,128)S(1)}, f32[64,1024]{1,0:T(8,128)S(1)}, u32[]{:S(2)}, u32[]{:S(2)}) %collective-permute-start.7) | collective-permute-done | bytes 262176 | tf_op jit(solution)/shard_map/ppermute | solution.py:468
  37.6 0.7 %add.3 = f32[64,1024]{1,0:T(8,128)} add(f32[64,1024]{1,0:T(8,128)S(1)} %shard_map.80, f32[64,1024]{1,0:T(8,128)S(1)} %collective-permute-done.7) | non-fusion elementwise | flops 65536 | bytes 786432 | tf_op jit(solution)/shard_map/add | solution.py:579
  (2 shorter events, 0.0 us)
Async XLA Ops:
  0.6 8.2 %copy-start.1 = (s32[4,128]{1,0:T(4,128)S(1)}, s32[4,128]{1,0:T(4,128)}, u32[]{:S(2)}) copy-start(s32[4,128]{1,0:T(4,128)} %refs_4_.1) | copy-start | bytes 6148
  0.6 8.2 %copy-start.2 = (s32[4]{0:T(128)S(1)}, s32[4]{0:T(128)}, u32[]{:S(2)}) copy-start(s32[4]{0:T(128)} %tile_pos_ref.1) | copy-start | bytes 52
  0.7 8.2 %copy-start.3 = (s32[4]{0:T(128)S(1)}, s32[4]{0:T(128)}, u32[]{:S(2)}) copy-start(s32[4]{0:T(128)} %cam_index_ref.1) | copy-start | bytes 52
  0.7 11.3 %collective-permute-start.3 = (bf16[64,1024]{1,0:T(8,128)(2,1)}, bf16[64,1024]{1,0:T(8,128)(2,1)S(1)}, u32[]{:S(2)}, u32[]{:S(2)}) collective-permute-start(bf16[64,1024]{1,0:T(8,128)(2,1)} %params_ref.1), channel_id=1, source_target_pairs={{0,4},{4,0},{8,12},{12,8},{16,20},{20,16},{24,28},{28,24},{1,5},{5... | collective-permute-start | bytes 393224 | tf_op jit(solution)/shard_map/ppermute | solution.py:468
  3.7 7.4 %collective-permute-start = (s32[4,128]{1,0:T(4,128)}, s32[4,128]{1,0:T(4,128)S(1)}, u32[]{:S(2)}, u32[]{:S(2)}) collective-permute-start(s32[4,128]{1,0:T(4,128)} %refs_4_.1), channel_id=1, source_target_pairs={{0,24},{4,28},{8,16},{12,20},{16,8},{20,12},{24,0},{28,4},{1,25},{... | collective-permute-start | bytes 6152 | tf_op jit(solution)/shard_map/ppermute | solution.py:468
  7.3 4.7 %collective-permute-start.1 = (s32[4,128]{1,0:T(4,128)}, s32[4,128]{1,0:T(4,128)S(1)}, u32[]{:S(2)}, u32[]{:S(2)}) collective-permute-start(s32[4,128]{1,0:T(4,128)} %refs_4_.1), channel_id=1, source_target_pairs={{0,16},{4,20},{8,24},{12,28},{16,0},{20,4},{24,8},{28,12},{1,17},{... | collective-permute-start | bytes 6152 | tf_op jit(solution)/shard_map/ppermute | solution.py:468
  7.3 4.7 %collective-permute-start.2 = (s32[4,128]{1,0:T(4,128)}, s32[4,128]{1,0:T(4,128)S(1)}, u32[]{:S(2)}, u32[]{:S(2)}) collective-permute-start(s32[4,128]{1,0:T(4,128)} %refs_4_.1), channel_id=1, source_target_pairs={{0,8},{4,12},{8,0},{12,4},{16,24},{20,28},{24,16},{28,20},{1,9},{5... | collective-permute-start | bytes 6152 | tf_op jit(solution)/shard_map/ppermute | solution.py:468
  8.8 0.9 %copy-start = (bf16[64,1024]{1,0:T(8,128)(2,1)S(1)}, bf16[64,1024]{1,0:T(8,128)(2,1)}, u32[]{:S(2)}) copy-start(bf16[64,1024]{1,0:T(8,128)(2,1)} %params_ref.1) | copy-start | bytes 393220
  12.0 5.5 %copy-start.4 = (f32[3,4,256]{2,1,0:T(4,128)S(1)}, f32[3,4,256]{2,1,0:T(4,128)}, u32[]{:S(2)}) copy-start(f32[3,4,256]{2,1,0:T(4,128)} %param.11) | copy-start | bytes 36868
  13.0 5.6 %collective-permute-start.4 = (bf16[64,128]{1,0:T(8,128)(2,1)S(1)}, bf16[64,128]{1,0:T(8,128)(2,1)S(1)}, u32[]{:S(2)}, u32[]{:S(2)}) collective-permute-start(bf16[64,128]{1,0:T(8,128)(2,1)S(1)} %get-tuple-element.14), channel_id=1, source_target_pairs={{0,24},{4,28},{8,16},{12,20},{16,8},{20,12},{24,0},{28,4},{1,25},{... | collective-permute-start | bytes 49160 | tf_op jit(solution)/shard_map/ppermute | solution.py:468
  15.8 4.6 %collective-permute-start.5 = (bf16[64,128]{1,0:T(8,128)(2,1)S(1)}, bf16[64,128]{1,0:T(8,128)(2,1)S(1)}, u32[]{:S(2)}, u32[]{:S(2)}) collective-permute-start(bf16[64,128]{1,0:T(8,128)(2,1)S(1)} %get-tuple-element.15), channel_id=1, source_target_pairs={{0,16},{4,20},{8,24},{12,28},{16,0},{20,4},{24,8},{28,12},{1,17},{... | collective-permute-start | bytes 49160 | tf_op jit(solution)/shard_map/ppermute | solution.py:468
  15.8 4.6 %collective-permute-start.6 = (bf16[64,128]{1,0:T(8,128)(2,1)S(1)}, bf16[64,128]{1,0:T(8,128)(2,1)S(1)}, u32[]{:S(2)}, u32[]{:S(2)}) collective-permute-start(bf16[64,128]{1,0:T(8,128)(2,1)S(1)} %get-tuple-element.16), channel_id=1, source_target_pairs={{0,8},{4,12},{8,0},{12,4},{16,24},{20,28},{24,16},{28,20},{1,9},{5... | collective-permute-start | bytes 49160 | tf_op jit(solution)/shard_map/ppermute | solution.py:468
  36.0 1.6 %collective-permute-start.7 = (f32[64,1024]{1,0:T(8,128)S(1)}, f32[64,1024]{1,0:T(8,128)S(1)}, u32[]{:S(2)}, u32[]{:S(2)}) collective-permute-start(f32[64,1024]{1,0:T(8,128)S(1)} %shard_map.80), channel_id=1, source_target_pairs={{0,1},{1,0},{2,3},{3,2},{4,5},{5,4},{6,7},{7,6},{8,9},{9,8},{10,11... | collective-permute-start | bytes 786440 | tf_op jit(solution)/shard_map/ppermute | solution.py:468

commit v2 on v1

--- a/solution.py
+++ b/solution.py
@@ -156,7 +156,7 @@
     picked_refs, refs = refs[2 : 2 + peers], refs[2 + peers :]
     lists_scratch, picked_scratch = refs
     tiles, length = lists_refs[0].shape
-    width, g_dev = own_ref.shape
+    g_dev = own_ref.shape[1]
     me = lax.axis_index("gauss")
     first = me % 2 == 0
     for k in range(peers):
@@ -164,21 +164,16 @@
     ids = lists_scratch[...].reshape(peers * tiles, length)
     where_own = find(ids, me * g_dev, tiles, cap, g_dev)
     where_other = find(ids, (me ^ 1) * g_dev, tiles, cap, g_dev)
-    own, other = own_ref[...], other_ref[...]
-    blank = jnp.zeros((width, g_dev), BF16)
     lanes = iota((peers * cap, g_dev), 1)
-    picked = dot(
-        one_hot(where_own == lanes),
-        jnp.concatenate([jnp.where(first, own, blank), jnp.where(first, blank, own)], axis=0),
-        1,
-        1,
-    ) + dot(
-        one_hot(where_other == lanes),
-        jnp.concatenate([jnp.where(first, blank, other), jnp.where(first, other, blank)], axis=0),
-        1,
-        1,
-    )
-    picked_scratch[...] = picked.astype(BF16).reshape(peers, cap, 2 * width)
+    of_own = dot(own_ref[...], one_hot(where_own == lanes), 1, 1)
+    of_other = dot(other_ref[...], one_hot(where_other == lanes), 1, 1)
+    of_even = jnp.where(first, of_own, of_other)
+    of_odd = jnp.where(first, of_other, of_own)
+    for p in range(peers):
+        block = slice(p * cap, (p + 1) * cap)
+        picked_scratch[p] = jnp.concatenate(
+            [of_even[:, block], of_odd[:, block]], axis=1
+        ).astype(BF16)
     for k in range(peers):
         picked_refs[peers - 1 - k][...] = picked_scratch[(me // 2) ^ k]
 
@@ -251,18 +246,11 @@
         listed = dot(recv_refs[0][...].reshape(-1, LANES), hot, 0, 0)[:width]
     else:
         (recv_scratch,) = refs[13:]
-        cap = recv_refs[0].shape[0]
         place = lax.axis_index("gauss") // 2
         for k in range(pieces):
             recv_scratch[place ^ k] = recv_refs[pieces - 1 - k][...]
-        received = recv_scratch[...].reshape(pieces * cap, 2 * width)
-        halves = [
-            jnp.concatenate(
-                [hot[(2 * p + j) * cap : (2 * p + j + 1) * cap] for p in range(pieces)], axis=0
-            )
-            for j in range(2)
-        ]
-        listed = dot(received, halves[0], 0, 0)[:width] + dot(received, halves[1], 0, 0)[width:]
+        received = jnp.concatenate([recv_scratch[p] for p in range(pieces)], axis=1)
+        listed = dot(received, hot)
     for t in range(tiles):
         rows_ref[t * width : (t + 1) * width, :] = listed[:, t * length : (t + 1) * length]
     rows = [rows_ref[pl.ds(f, tiles, stride=width), :] for f in range(width)]
@@ -422,9 +410,8 @@
             send_ref[o, c] = block
 
 
-def scatter_kernel(cap, recv_ref, out_ref):
-    blocks, high, lanes = recv_ref.shape
-    g_dev = out_ref.shape[1]
+def scatter(cap, recv_ref, g_dev):
+    blocks, high, _ = recv_ref.shape
     values = jnp.concatenate(
         [
             jnp.concatenate(
@@ -443,10 +430,37 @@
     parts = split(jnp.concatenate(rows, axis=0), 2)
     total = dot(jnp.concatenate(parts, axis=0), hot, 1, 1)
     count = total.shape[0] // 2
-    total = total[:count] + total[count:]
+    return total[:count] + total[count:]
+
+
+def in_order(total, out_ref):
     out_ref[:11, :] = total[:11]
     out_ref[11:59, :] = total[SENT:]
     out_ref[59:, :] = total[16:21]
+
+
+def scatter_kernel(cap, recv_ref, out_ref):
+    in_order(scatter(cap, recv_ref, out_ref.shape[1]), out_ref)
+
+
+def first_kernel(cap, recv_ref, out_ref):
+    out_ref[...] = scatter(cap, recv_ref, out_ref.shape[1])
+
+
+def last_kernel(cap, recv_ref, sum_ref, spread_ref, out_ref, pictures_ref):
+    in_order(sum_ref[...] + scatter(cap, recv_ref, out_ref.shape[1]), out_ref)
+    _, tiles, _ = pictures_ref.shape
+    depth = spread_ref.shape[1]
+    share = LANES // tiles
+    for k in range(3):
+        for t in range(tiles):
+            pictures_ref[k, t : t + 1, :] = jnp.concatenate(
+                [
+                    spread_ref[k, s : s + 1, t * share : (t + 1) * share]
+                    for s in range(depth)
+                ],
+                axis=1,
+            )
 
 
 def call(kernel, out_shape, args, scalars=0, scratch=()):
@@ -530,11 +544,11 @@
     if paired:
         picked = call(
             functools.partial(pick_pair_kernel, cap, peers),
-            [shape((cap, 2 * width), BF16)] * peers,
+            [shape((width, 2 * cap), BF16)] * peers,
             (*all_lists, params_copy, other),
             scratch=(
                 pltpu.VMEM((peers, tiles, length), jnp.int32),
-                pltpu.VMEM((peers, cap, 2 * width), BF16),
+                pltpu.VMEM((peers, width, 2 * cap), BF16),
             ),
         )
         returned = far_first(picked)
@@ -564,22 +578,28 @@
             pltpu.VMEM((peers, *returned[0].shape[-2:]), BF16),
         ),
     )
+    if wide:
+        received = exchange_wide(sent)
+        other = swap(received, "view", 1)
+        total = call(
+            functools.partial(first_kernel, cap), shape((SENT + 48, g_dev), F32), (received,)
+        )
+        grads, pictures = call(
+            functools.partial(last_kernel, cap),
+            [shape((width, g_dev), F32), shape(targets.shape, F32)],
+            (other, total, pictures),
+        )
+        return (pictures, grads)
     pictures = (
         pictures.reshape(3, depth, tiles, share)
         .transpose(0, 2, 1, 3)
         .reshape(3, tiles, SIDE * SIDE)
     )
-    received = exchange_wide(sent) if wide else exchange(sent[:, 0])
+    received = exchange(sent[:, 0])
     grads = call(
-        functools.partial(scatter_kernel, cap),
-        shape((width, g_dev), F32),
-        (received,),
-    )
-    if wide:
-        grads = grads + swap(grads, "view", 1)
-    else:
-        grads = lax.psum(grads, "view")
-    return (pictures, grads)
+        functools.partial(scatter_kernel, cap), shape((width, g_dev), F32), (received,)
+    )
+    return (pictures, lax.psum(grads, "view"))
 
 
 def solution(mesh):

time: 38.6 us -> 38.3 us (level)
  Pallas kernels: 5.88 us -> 7.53 us
  local copies, waits for them, and re-layouts: 2.66 us -> 1.88 us
  other arithmetic: 0.73 us -> 0 us
    pallas_call x4 -> x5, Pallas kernels: 5.88 us -> 7.53 us  [call(): pl.pallas_call(kernel, out_shape=out_shape, in_specs=in_specs, out_specs=...]
    reshape x2 -> x0, local copies, waits for them, and re-layouts: 0.77 us -> none  [the longest x1 0.69 us: on_device(): pictures = pictures.reshape(3, depth, tiles, share).transpose(0, 2, 1, 3)...]
    add x1 -> x0, other arithmetic: 0.73 us -> none  [on_device(): grads = grads + swap(grads, 'view', 1)]
  transfers between devices with their start and end apart: 8 -> 8, of which waited for: 4 -> 4; matrix products, arithmetic and copies ran while one was open for 5% -> 3% of each run, Pallas kernels for 3% -> 6%
where the time goes in v2:
time: 38.3 us; the launch traced here: 38.1 us
  blocking collectives  12 us (31%)
  starting transfers between devices  11.8 us (31%)
  Pallas kernels  7.53 us (20%)
  waiting for transfers between devices  4.13 us (11%)
  local copies, waits for them, and re-layouts  1.88 us (5%)
  between operations  0.72 us (2%)
    all_to_all x1, blocking collectives, exchange_wide(): lax.all_to_all(blocks, ('gauss', 'view'), split_axis=0, concat_axis=0, ax...  12 us
    ppermute x8, starting transfers between devices, swap(): lax.ppermute(x, axis, [(i, i ^ k) for i in range(lax.axis_size(axis))])  11.8 us
    pallas_call x5, Pallas kernels, call(): pl.pallas_call(kernel, out_shape=out_shape, in_specs=in_specs, out_specs=...  7.53 us
    ppermute x8, waiting for transfers between devices, swap(): lax.ppermute(x, axis, [(i, i ^ k) for i in range(lax.axis_size(axis))])  4.13 us
    unnamed x11, local copies, waits for them, and re-layouts  1.7 us
  transfers between devices with their start and end apart: 8, of which 4 were waited for; matrix products, arithmetic and copies ran while one was open for 3% of the time, Pallas kernels for 6%

profile of v2, /device:TPU:0, one launch (start us, length us, event | category | flops | bytes accessed | tf_op | source)
XLA Modules:
  0.0 38.1 jit_solution(11978431736231304978)
XLA Ops:
  0.6 0.0 copy-start.1
  0.6 0.0 copy-start.2
  0.7 0.0 copy-start.3
  0.7 3.0 %collective-permute-start.3 = (bf16[64,1024]{1,0:T(8,128)(2,1)}, bf16[64,1024]{1,0:T(8,128)(2,1)S(1)}, u32[]{:S(2)}, u32[]{:S(2)}) collective-permute-start(bf16[64,1024]{1,0:T(8,128)(2,1)} %params_ref.1), channel_id=1, source_target_pairs={{0,4},{4,0},{8,12},{12,8},{16,20},{20,16},{24,28},{28,24},{1,5},{5... | collective-permute-start | bytes 393224 | tf_op jit(solution)/shard_map/ppermute | solution.py:482
  3.7 3.6 %collective-permute-start = (s32[4,128]{1,0:T(4,128)}, s32[4,128]{1,0:T(4,128)S(1)}, u32[]{:S(2)}, u32[]{:S(2)}) collective-permute-start(s32[4,128]{1,0:T(4,128)} %refs_4_.1), channel_id=1, source_target_pairs={{0,24},{4,28},{8,16},{12,20},{16,8},{20,12},{24,0},{28,4},{1,25},{... | collective-permute-start | bytes 6152 | tf_op jit(solution)/shard_map/ppermute | solution.py:482
  7.3 0.0 collective-permute-start.1
  7.3 0.8 %collective-permute-start.2 = (s32[4,128]{1,0:T(4,128)}, s32[4,128]{1,0:T(4,128)S(1)}, u32[]{:S(2)}, u32[]{:S(2)}) collective-permute-start(s32[4,128]{1,0:T(4,128)} %refs_4_.1), channel_id=1, source_target_pairs={{0,8},{4,12},{8,0},{12,4},{16,24},{20,28},{24,16},{28,20},{1,9},{5... | collective-permute-start | bytes 6152 | tf_op jit(solution)/shard_map/ppermute | solution.py:482
  8.1 0.8 %copy.8.cams_ref = f32[28,16]{1,0:T(8,128)S(1)} copy(f32[28,16]{0,1:T(8,128)} %param.10) | data formatting | bytes 3584 | tf_op args[4]
  8.8 0.0 copy-done.1
  8.8 0.0 copy-done.2
  8.8 0.0 copy-done.3
  8.8 0.0 copy-start
  8.9 0.9 %copy-done = bf16[64,1024]{1,0:T(8,128)(2,1)S(1)} copy-done((bf16[64,1024]{1,0:T(8,128)(2,1)S(1)}, bf16[64,1024]{1,0:T(8,128)(2,1)}, u32[]{:S(2)}) %copy-start) | copy-done | bytes 131096
  9.8 1.3 %shard_map.77 = (bf16[512,512]{1,0:T(8,128)(2,1)S(1)}, f32[4,128]{1,0:T(4,128)S(1)}, bf16[64,1024]{1,0:T(8,128)(2,1)S(1)}, f32[28,4,128]{2,1,0:T(4,128)S(1)}, f32[2,8,128]{2,1,0:T(8,128)S(1)}) custom-call(s32[4]{0:T(128)S(1)} %copy-done.2, s32[4]{0:T(128)S(1)} %copy-done.3, f32[28,16]{1,0:T(8,128)S(1)} %copy.8.cams_ref, s32[4,128]{1,0:T(4,128)S(1)} %copy-done.1, ...), custom_call_target="tpu_custom_call" | custom-call | tf_op jit(solution)/shard_map/pallas_call | solution.py:471
  11.0 0.0 collective-permute-done.refs_0_
  11.1 0.9 %collective-permute-done.1.refs_1_ = s32[4,128]{1,0:T(4,128)S(1)} collective-permute-done((s32[4,128]{1,0:T(4,128)}, s32[4,128]{1,0:T(4,128)S(1)}, u32[]{:S(2)}, u32[]{:S(2)}) %collective-permute-start.1) | collective-permute-done | bytes 2080 | tf_op jit(solution)/shard_map/ppermute | solution.py:482
  12.0 0.0 collective-permute-done.2.refs_2_
  12.0 0.0 collective-permute-done.3.refs_5_
  12.0 0.0 copy-start.4
  12.0 1.1 %shard_map.78 = (bf16[64,128]{1,0:T(8,128)(2,1)S(1)}, bf16[64,128]{1,0:T(8,128)(2,1)S(1)}, bf16[64,128]{1,0:T(8,128)(2,1)S(1)}, bf16[64,128]{1,0:T(8,128)(2,1)S(1)}) custom-call(s32[4,128]{1,0:T(4,128)S(1)} %collective-permute-done.refs_0_, s32[4,128]{1,0:T(4,128)S(1)} %collective-permute-done.1.refs_1_, s32[4,128]{1,0:T(4,128)S(1)} %collective-permute-done.2.refs_2_, ...), custom_call_target="tpu_custom_call" | custom-call | tf_op jit(solution)/shard_map/pallas_call | solution.py:471
  13.1 2.8 %collective-permute-start.4 = (bf16[64,128]{1,0:T(8,128)(2,1)S(1)}, bf16[64,128]{1,0:T(8,128)(2,1)S(1)}, u32[]{:S(2)}, u32[]{:S(2)}) collective-permute-start(bf16[64,128]{1,0:T(8,128)(2,1)S(1)} %get-tuple-element.16), channel_id=1, source_target_pairs={{0,24},{4,28},{8,16},{12,20},{16,8},{20,12},{24,0},{28,4},{1,25},{... | collective-permute-start | bytes 49160 | tf_op jit(solution)/shard_map/ppermute | solution.py:482
  15.9 0.0 collective-permute-start.5
  15.9 1.7 %collective-permute-start.6 = (bf16[64,128]{1,0:T(8,128)(2,1)S(1)}, bf16[64,128]{1,0:T(8,128)(2,1)S(1)}, u32[]{:S(2)}, u32[]{:S(2)}) collective-permute-start(bf16[64,128]{1,0:T(8,128)(2,1)S(1)} %get-tuple-element.18), channel_id=1, source_target_pairs={{0,8},{4,12},{8,0},{12,4},{16,24},{20,28},{24,16},{28,20},{1,9},{5... | collective-permute-start | bytes 49160 | tf_op jit(solution)/shard_map/ppermute | solution.py:482
  17.6 0.0 copy-done.4
  17.6 0.1 reshape.13
  17.7 0.1 reshape.14.refs_9_
  17.8 1.0 %collective-permute-done.4.refs_0_ = bf16[64,128]{1,0:T(8,128)(2,1)S(1)} collective-permute-done((bf16[64,128]{1,0:T(8,128)(2,1)S(1)}, bf16[64,128]{1,0:T(8,128)(2,1)S(1)}, u32[]{:S(2)}, u32[]{:S(2)}) %collective-permute-start.4) | collective-permute-done | bytes 16416 | tf_op jit(solution)/shard_map/ppermute | solution.py:482
  18.7 1.8 %collective-permute-done.5.refs_1_ = bf16[64,128]{1,0:T(8,128)(2,1)S(1)} collective-permute-done((bf16[64,128]{1,0:T(8,128)(2,1)S(1)}, bf16[64,128]{1,0:T(8,128)(2,1)S(1)}, u32[]{:S(2)}, u32[]{:S(2)}) %collective-permute-start.5) | collective-permute-done | bytes 16416 | tf_op jit(solution)/shard_map/ppermute | solution.py:482
  20.5 0.0 collective-permute-done.6.refs_2_
  20.5 2.6 %shard_map.79 = (f32[3,8,128]{2,1,0:T(8,128)S(1)}, f32[8,2,16,128]{3,2,1,0:T(8,128)S(1)}) custom-call(bf16[64,128]{1,0:T(8,128)(2,1)S(1)} %collective-permute-done.4.refs_0_, bf16[64,128]{1,0:T(8,128)(2,1)S(1)} %collective-permute-done.5.refs_1_, bf16[64,128]{1,0:T(8,128)(2,1)S(1)} %collective-permute-done.6.refs_2_, ...), custom_call_target="tpu_custom_call" | custom-call | tf_op jit(solution)/shard_map/pallas_call | solution.py:471
  23.1 12.0 %all_to_all.5.recv_ref = f32[16,16,128]{2,1,0:T(8,128)S(1)} all-to-all(f32[16,16,128]{2,1,0:T(8,128)S(1)} %bitcast.4), channel_id=1, replica_groups={{0,2,4,6,8,10,12,14,16,18,20,22,24,26,28,30},{1,3,5,7,9,11,13,15,17,19,..., dimensions={0} | all-to-all | bytes 262144 | tf_op jit(solution)/shard_map/all_to_all | solution.py:498
  35.1 0.0 collective-permute-start.7
  35.1 0.9 %shard_map.80.sum_ref = f32[80,1024]{1,0:T(8,128)S(1)} custom-call(f32[16,16,128]{2,1,0:T(8,128)S(1)} %all_to_all.5.recv_ref), custom_call_target="tpu_custom_call" | custom-call | tf_op jit(solution)/shard_map/pallas_call | solution.py:471
  36.0 0.4 %collective-permute-done.7.recv_ref = f32[16,16,128]{2,1,0:T(8,128)S(1)} collective-permute-done((f32[16,16,128]{2,1,0:T(8,128)S(1)}, f32[16,16,128]{2,1,0:T(8,128)S(1)}, u32[]{:S(2)}, u32[]{:S(2)}) %collective-permute-start.7) | collective-permute-done | bytes 131104 | tf_op jit(solution)/shard_map/ppermute | solution.py:482
  36.4 1.6 %shard_map.81 = (f32[64,1024]{1,0:T(8,128)}, f32[3,4,256]{2,1,0:T(4,128)}) custom-call(f32[16,16,128]{2,1,0:T(8,128)S(1)} %collective-permute-done.7.recv_ref, f32[80,1024]{1,0:T(8,128)S(1)} %shard_map.80.sum_ref, f32[3,8,128]{2,1,0:T(8,128)S(1)} %get-tuple-element.25.spread_ref), custom_call_target="tpu_custom_call" | custom-call | tf_op jit(solution)/shard_map/pallas_call | solution.py:471
  (1 shorter events, 0.0 us)
Async XLA Ops:
  0.6 8.2 %copy-start.1 = (s32[4,128]{1,0:T(4,128)S(1)}, s32[4,128]{1,0:T(4,128)}, u32[]{:S(2)}) copy-start(s32[4,128]{1,0:T(4,128)} %refs_4_.1) | copy-start | bytes 6148
  0.6 8.2 %copy-start.2 = (s32[4]{0:T(128)S(1)}, s32[4]{0:T(128)}, u32[]{:S(2)}) copy-start(s32[4]{0:T(128)} %tile_pos_ref.1) | copy-start | bytes 52
  0.7 8.2 %copy-start.3 = (s32[4]{0:T(128)S(1)}, s32[4]{0:T(128)}, u32[]{:S(2)}) copy-start(s32[4]{0:T(128)} %cam_index_ref.1) | copy-start | bytes 52
  0.7 11.3 %collective-permute-start.3 = (bf16[64,1024]{1,0:T(8,128)(2,1)}, bf16[64,1024]{1,0:T(8,128)(2,1)S(1)}, u32[]{:S(2)}, u32[]{:S(2)}) collective-permute-start(bf16[64,1024]{1,0:T(8,128)(2,1)} %params_ref.1), channel_id=1, source_target_pairs={{0,4},{4,0},{8,12},{12,8},{16,20},{20,16},{24,28},{28,24},{1,5},{5... | collective-permute-start | bytes 393224 | tf_op jit(solution)/shard_map/ppermute | solution.py:482
  3.7 7.4 %collective-permute-start = (s32[4,128]{1,0:T(4,128)}, s32[4,128]{1,0:T(4,128)S(1)}, u32[]{:S(2)}, u32[]{:S(2)}) collective-permute-start(s32[4,128]{1,0:T(4,128)} %refs_4_.1), channel_id=1, source_target_pairs={{0,24},{4,28},{8,16},{12,20},{16,8},{20,12},{24,0},{28,4},{1,25},{... | collective-permute-start | bytes 6152 | tf_op jit(solution)/shard_map/ppermute | solution.py:482
  7.3 4.7 %collective-permute-start.1 = (s32[4,128]{1,0:T(4,128)}, s32[4,128]{1,0:T(4,128)S(1)}, u32[]{:S(2)}, u32[]{:S(2)}) collective-permute-start(s32[4,128]{1,0:T(4,128)} %refs_4_.1), channel_id=1, source_target_pairs={{0,16},{4,20},{8,24},{12,28},{16,0},{20,4},{24,8},{28,12},{1,17},{... | collective-permute-start | bytes 6152 | tf_op jit(solution)/shard_map/ppermute | solution.py:482
  7.3 4.7 %collective-permute-start.2 = (s32[4,128]{1,0:T(4,128)}, s32[4,128]{1,0:T(4,128)S(1)}, u32[]{:S(2)}, u32[]{:S(2)}) collective-permute-start(s32[4,128]{1,0:T(4,128)} %refs_4_.1), channel_id=1, source_target_pairs={{0,8},{4,12},{8,0},{12,4},{16,24},{20,28},{24,16},{28,20},{1,9},{5... | collective-permute-start | bytes 6152 | tf_op jit(solution)/shard_map/ppermute | solution.py:482
  8.8 0.9 %copy-start = (bf16[64,1024]{1,0:T(8,128)(2,1)S(1)}, bf16[64,1024]{1,0:T(8,128)(2,1)}, u32[]{:S(2)}) copy-start(bf16[64,1024]{1,0:T(8,128)(2,1)} %params_ref.1) | copy-start | bytes 393220
  12.0 5.6 %copy-start.4 = (f32[3,4,256]{2,1,0:T(4,128)S(1)}, f32[3,4,256]{2,1,0:T(4,128)}, u32[]{:S(2)}) copy-start(f32[3,4,256]{2,1,0:T(4,128)} %param.11) | copy-start | bytes 36868
  13.1 5.6 %collective-permute-start.4 = (bf16[64,128]{1,0:T(8,128)(2,1)S(1)}, bf16[64,128]{1,0:T(8,128)(2,1)S(1)}, u32[]{:S(2)}, u32[]{:S(2)}) collective-permute-start(bf16[64,128]{1,0:T(8,128)(2,1)S(1)} %get-tuple-element.16), channel_id=1, source_target_pairs={{0,24},{4,28},{8,16},{12,20},{16,8},{20,12},{24,0},{28,4},{1,25},{... | collective-permute-start | bytes 49160 | tf_op jit(solution)/shard_map/ppermute | solution.py:482
  15.9 4.6 %collective-permute-start.5 = (bf16[64,128]{1,0:T(8,128)(2,1)S(1)}, bf16[64,128]{1,0:T(8,128)(2,1)S(1)}, u32[]{:S(2)}, u32[]{:S(2)}) collective-permute-start(bf16[64,128]{1,0:T(8,128)(2,1)S(1)} %get-tuple-element.17), channel_id=1, source_target_pairs={{0,16},{4,20},{8,24},{12,28},{16,0},{20,4},{24,8},{28,12},{1,17},{... | collective-permute-start | bytes 49160 | tf_op jit(solution)/shard_map/ppermute | solution.py:482
  15.9 4.6 %collective-permute-start.6 = (bf16[64,128]{1,0:T(8,128)(2,1)S(1)}, bf16[64,128]{1,0:T(8,128)(2,1)S(1)}, u32[]{:S(2)}, u32[]{:S(2)}) collective-permute-start(bf16[64,128]{1,0:T(8,128)(2,1)S(1)} %get-tuple-element.18), channel_id=1, source_target_pairs={{0,8},{4,12},{8,0},{12,4},{16,24},{20,28},{24,16},{28,20},{1,9},{5... | collective-permute-start | bytes 49160 | tf_op jit(solution)/shard_map/ppermute | solution.py:482
  35.1 1.3 %collective-permute-start.7 = (f32[16,16,128]{2,1,0:T(8,128)S(1)}, f32[16,16,128]{2,1,0:T(8,128)S(1)}, u32[]{:S(2)}, u32[]{:S(2)}) collective-permute-start(f32[16,16,128]{2,1,0:T(8,128)S(1)} %all_to_all.5.recv_ref), channel_id=1, source_target_pairs={{0,1},{1,0},{2,3},{3,2},{4,5},{5,4},{6,7},{7,6},{8,9},{9,8},{10,11... | collective-permute-start | bytes 393224 | tf_op jit(solution)/shard_map/ppermute | solution.py:482

commit v3 on v2

--- a/solution.py
+++ b/solution.py
@@ -160,7 +160,7 @@
     me = lax.axis_index("gauss")
     first = me % 2 == 0
     for k in range(peers):
-        lists_scratch[(me // 2) ^ k] = lists_refs[peers - 1 - k][...]
+        lists_scratch[(me // 2) ^ k] = lists_refs[k][...]
     ids = lists_scratch[...].reshape(peers * tiles, length)
     where_own = find(ids, me * g_dev, tiles, cap, g_dev)
     where_other = find(ids, (me ^ 1) * g_dev, tiles, cap, g_dev)
@@ -186,27 +186,16 @@
 
 
 def prepare_kernel(
-    owners,
-    cap,
-    g_dev,
-    tile_pos_ref,
-    cam_index_ref,
-    cams_ref,
-    lists_ref,
-    params_ref,
-    hot_ref,
-    local_ref,
-    copy_ref,
-    cam_ref,
-    pixel_ref,
+    tile_pos_ref, cam_index_ref, cams_ref, params_ref, copy_ref, cam_ref, pixel_ref
 ):
-    tiles, length = lists_ref.shape
+    copy_ref[...] = params_ref[...]
+    values, tiles, length = cam_ref.shape
     share = LANES // tiles
     depth = SIDE * SIDE // share
     cam_ids = [cam_index_ref[t] for t in range(tiles)]
     tile_row = iota((tiles, length), 0)
-    for j in range(cams_ref.shape[0]):
-        cam_ref[j] = by_tile([cams_ref[j, cam_ids[t]] for t in range(tiles)], tile_row)
+    for j in range(values):
+        cam_ref[j] = by_tile([cams_ref[cam_ids[t], j] for t in range(tiles)], tile_row)
     pos = [tile_pos_ref[t] for t in range(tiles)]
     lane = iota((depth, LANES), 1)
     origin_x = [(SIDE * (lax.rem(p, WIN) - WIN // 2)).astype(F32) + 0.5 for p in pos]
@@ -215,6 +204,9 @@
     pixel_row = iota((depth, LANES), 0) * (share // SIDE) + (lane % share) // SIDE
     pixel_ref[1] = by_tile(origin_y, lane // share) + pixel_row.astype(F32)
 
+
+def place_kernel(owners, cap, g_dev, lists_ref, after_ref, hot_ref, local_ref):
+    tiles, length = lists_ref.shape
     slots = owners * cap
     ids = lists_ref[...]
     masks = [(ids >= o * g_dev) & (ids < (o + 1) * g_dev) for o in range(owners)]
@@ -229,7 +221,6 @@
         [one_hot(slot_iota == place[t : t + 1, :]) for t in range(tiles)], axis=1
     )
     local_ref[...] = local.astype(F32)
-    copy_ref[...] = params_ref[...]
 
 
 def render_kernel(pieces, width, *refs):
@@ -463,9 +454,10 @@
             )
 
 
-def call(kernel, out_shape, args, scalars=0, scratch=()):
+def call(kernel, out_shape, args, scalars=0, left=0, scratch=()):
     in_specs = [pl.BlockSpec(memory_space=pltpu.SMEM)] * scalars
-    in_specs += [pl.BlockSpec(memory_space=pltpu.VMEM)] * (len(args) - scalars)
+    in_specs += [pl.BlockSpec(memory_space=pltpu.VMEM)] * (len(args) - scalars - left)
+    in_specs += [pl.BlockSpec(memory_space=pl.ANY)] * left
     many = isinstance(out_shape, (list, tuple))
     spec = pl.BlockSpec(memory_space=pltpu.VMEM)
     return pl.pallas_call(
@@ -482,9 +474,22 @@
     return lax.ppermute(x, axis, [(i, i ^ k) for i in range(lax.axis_size(axis))])
 
 
+def crossed(owner, owners):
+    return int(owner >= owners // 2)
+
+
 def far_first(blocks):
+    owners, views = lax.axis_size("gauss"), lax.axis_size("view")
     last = len(blocks) - 1
-    return [swap(b, "gauss", 2 * (last - i)) if i < last else b for i, b in enumerate(blocks)]
+    out = []
+    for i, block in enumerate(blocks):
+        k = 2 * (last - i)
+        pairs = []
+        for g in range(owners):
+            flip = crossed(g, owners) ^ crossed(g ^ k, owners) if views % 2 == 0 else 0
+            pairs += [(g * views + v, (g ^ k) * views + (v ^ flip)) for v in range(views)]
+        out.append(lax.ppermute(block, ("gauss", "view"), pairs) if k else block)
+    return out
 
 
 def exchange(x):
@@ -494,7 +499,15 @@
 def exchange_wide(x):
     owners, views = lax.axis_size("gauss"), lax.axis_size("view")
     blocks = x.reshape(owners * views // 2, *x.shape[2:])
-    groups = [[i for i in range(owners * views) if i % 2 == c] for c in range(2)]
+    groups = [
+        [
+            g * views + v
+            for g in range(owners)
+            for v in range(views)
+            if v % 2 == c ^ crossed(g, owners)
+        ]
+        for c in range(2)
+    ]
     return lax.all_to_all(
         blocks,
         ("gauss", "view"),
@@ -529,29 +542,28 @@
     if paired:
         other = swap(params, "gauss", 1)
         all_lists = far_first([lists] * peers)
-    hot, local, params_copy, cam, pixel = call(
-        functools.partial(prepare_kernel, owners, cap, g_dev),
-        [
-            shape((slots, tiles * length), BF16),
-            shape((tiles, length), F32),
+    params_copy, cam, pixel = call(
+        prepare_kernel,
+        [
             shape((width, g_dev), BF16),
             shape((cams.shape[0], tiles, length), F32),
             shape((2, depth, LANES), F32),
         ],
-        (tile_pos, cam_index, cams, lists, params),
+        (tile_pos, cam_index, cams.T, params),
         scalars=3,
     )
     if paired:
         picked = call(
             functools.partial(pick_pair_kernel, cap, peers),
             [shape((width, 2 * cap), BF16)] * peers,
-            (*all_lists, params_copy, other),
+            (*all_lists[::-1], params_copy, other),
             scratch=(
                 pltpu.VMEM((peers, tiles, length), jnp.int32),
                 pltpu.VMEM((peers, width, 2 * cap), BF16),
             ),
         )
         returned = far_first(picked)
+        after = picked[-1]
     else:
         all_lists = exchange(jnp.broadcast_to(lists[None], (owners, tiles, length)))
         picked = call(
@@ -560,6 +572,13 @@
             (all_lists.reshape(owners * tiles, length), params_copy),
         )
         returned = [exchange(picked.reshape(owners, cap, LANES))]
+        after = picked
+    hot, local = call(
+        functools.partial(place_kernel, owners, cap, g_dev),
+        [shape((slots, tiles * length), BF16), shape((tiles, length), F32)],
+        (lists, after),
+        left=1,
+    )
     spread_targets = (
         targets.reshape(3, tiles, depth, share).transpose(0, 2, 1, 3).reshape(3, depth, LANES)
     )

time: 38.3 us -> 36.3 us (0.948)
  waiting for transfers between devices: 4.13 us -> 1.98 us
  starting transfers between devices: 11.8 us -> 12.7 us
  blocking collectives: 12 us -> 11.3 us
    ppermute x0 -> x6, starting transfers between devices: none -> 8.28 us  [far_first(): out.append(lax.ppermute(block, ('gauss', 'view'), pairs) if k else block)]
    ppermute x8 -> x2, starting transfers between devices: 11.8 us -> 4.44 us  [swap(): lax.ppermute(x, axis, [(i, i ^ k) for i in range(lax.axis_size(axis))])]
    ppermute x8 -> x2, waiting for transfers between devices: 4.13 us -> 0.07 us  [swap(): lax.ppermute(x, axis, [(i, i ^ k) for i in range(lax.axis_size(axis))])]
    ppermute x0 -> x6, waiting for transfers between devices: none -> 1.91 us  [far_first(): out.append(lax.ppermute(block, ('gauss', 'view'), pairs) if k else block)]
    all_to_all x1, blocking collectives: 12 us -> 11.3 us  [exchange_wide(): lax.all_to_all(blocks, ('gauss', 'view'), split_axis=0, concat_axis=0, ax...]
    unnamed x11 -> x12, local copies, waits for them, and re-layouts: 1.7 us -> 1.62 us
    pallas_call x5 -> x6, Pallas kernels: 7.53 us -> 7.49 us  [call(): pl.pallas_call(kernel, out_shape=out_shape, in_specs=in_specs, out_specs=...]
  transfers between devices with their start and end apart: 8 -> 8, of which waited for: 4 -> 4; matrix products, arithmetic and copies ran while one was open for 3% -> 1% of each run, Pallas kernels for 6% -> 6%
where the time goes in v3:
time: 36.3 us; the launch traced here: 36.1 us
  starting transfers between devices  12.7 us (35%)
  blocking collectives  11.3 us (31%)
  Pallas kernels  7.49 us (21%)
  waiting for transfers between devices  1.98 us (5%)
  local copies, waits for them, and re-layouts  1.8 us (5%)
  between operations  0.72 us (2%)
    all_to_all x1, blocking collectives, exchange_wide(): lax.all_to_all(blocks, ('gauss', 'view'), split_axis=0, concat_axis=0, ax...  11.3 us
    ppermute x6, starting transfers between devices, far_first(): out.append(lax.ppermute(block, ('gauss', 'view'), pairs) if k else block)  8.28 us
    pallas_call x6, Pallas kernels, call(): pl.pallas_call(kernel, out_shape=out_shape, in_specs=in_specs, out_specs=...  7.49 us
    ppermute x2, starting transfers between devices, swap(): lax.ppermute(x, axis, [(i, i ^ k) for i in range(lax.axis_size(axis))])  4.44 us
    ppermute x6, waiting for transfers between devices, far_first(): out.append(lax.ppermute(block, ('gauss', 'view'), pairs) if k else block)  1.91 us
    unnamed x12, local copies, waits for them, and re-layouts  1.62 us
  transfers between devices with their start and end apart: 8, of which 4 were waited for; matrix products, arithmetic and copies ran while one was open for 1% of the time, Pallas kernels for 6%

profile of v3, /device:TPU:0, one launch (start us, length us, event | category | flops | bytes accessed | tf_op | source)
XLA Modules:
  0.0 36.1 jit_solution(2573006708130622697)
XLA Ops:
  0.6 0.0 copy-start.4
  0.6 0.0 copy-start.3
  0.7 3.0 %collective-permute-start.3 = (bf16[64,1024]{1,0:T(8,128)(2,1)}, bf16[64,1024]{1,0:T(8,128)(2,1)S(1)}, u32[]{:S(2)}, u32[]{:S(2)}) collective-permute-start(bf16[64,1024]{1,0:T(8,128)(2,1)} %params_ref.1), channel_id=1, source_target_pairs={{0,4},{4,0},{8,12},{12,8},{16,20},{20,16},{24,28},{28,24},{1,5},{5... | collective-permute-start | bytes 393224 | tf_op jit(solution)/shard_map/ppermute | solution.py:474
  3.7 2.8 %collective-permute-start.2 = (s32[4,128]{1,0:T(4,128)}, s32[4,128]{1,0:T(4,128)S(1)}, u32[]{:S(2)}, u32[]{:S(2)}) collective-permute-start(s32[4,128]{1,0:T(4,128)} %refs_4_.1), channel_id=1, source_target_pairs={{0,25},{1,24},{2,27},{3,26},{4,29},{5,28},{6,31},{7,30},{8,17},{9,... | collective-permute-start | bytes 6152 | tf_op jit(solution)/shard_map/ppermute | solution.py:491
  6.4 0.0 collective-permute-start.1
  6.4 1.3 %collective-permute-start = (s32[4,128]{1,0:T(4,128)}, s32[4,128]{1,0:T(4,128)S(1)}, u32[]{:S(2)}, u32[]{:S(2)}) collective-permute-start(s32[4,128]{1,0:T(4,128)} %refs_4_.1), channel_id=1, source_target_pairs={{0,8},{1,9},{2,10},{3,11},{4,12},{5,13},{6,14},{7,15},{8,0},{9,1},... | collective-permute-start | bytes 6152 | tf_op jit(solution)/shard_map/ppermute | solution.py:491
  7.8 0.0 copy-done.4
  7.8 0.0 copy-done.3
  7.8 0.0 copy-start
  7.8 0.9 %copy-done = bf16[64,1024]{1,0:T(8,128)(2,1)S(1)} copy-done((bf16[64,1024]{1,0:T(8,128)(2,1)S(1)}, bf16[64,1024]{1,0:T(8,128)(2,1)}, u32[]{:S(2)}) %copy-start) | copy-done | bytes 131096
  8.7 0.0 copy-start.2
  8.7 0.7 %copy-done.2 = f32[28,16]{0,1:T(8,128)S(1)} copy-done((f32[28,16]{0,1:T(8,128)S(1)}, f32[28,16]{0,1:T(8,128)}, u32[]{:S(2)}) %copy-start.2) | copy-done | bytes 1816
  9.4 0.0 copy-start.1
  9.4 0.8 %shard_map.77 = (bf16[64,1024]{1,0:T(8,128)(2,1)S(1)}, f32[28,4,128]{2,1,0:T(4,128)S(1)}, f32[2,8,128]{2,1,0:T(8,128)S(1)}) custom-call(s32[4]{0:T(128)S(1)} %copy-done.3, s32[4]{0:T(128)S(1)} %copy-done.4, f32[16,28]{1,0:T(8,128)S(1)} %bitcast.6, bf16[64,1024]{1,0:T(8,128)(2,1)S(1)} %copy-done), custom_call_target="tpu_custom_call" | custom-call | tf_op jit(solution)/shard_map/pallas_call | solution.py:463
  10.1 0.0 collective-permute-done.2.refs_3_
  10.2 0.4 %collective-permute-done.1.refs_2_ = s32[4,128]{1,0:T(4,128)S(1)} collective-permute-done((s32[4,128]{1,0:T(4,128)}, s32[4,128]{1,0:T(4,128)S(1)}, u32[]{:S(2)}, u32[]{:S(2)}) %collective-permute-start.1) | collective-permute-done | bytes 2080 | tf_op jit(solution)/shard_map/ppermute | solution.py:491
  10.5 0.0 collective-permute-done.refs_1_
  10.5 0.0 collective-permute-done.3.refs_5_
  10.5 0.0 copy-done.1
  10.5 0.0 copy-start.5
  10.6 1.1 %shard_map.78 = (bf16[64,128]{1,0:T(8,128)(2,1)S(1)}, bf16[64,128]{1,0:T(8,128)(2,1)S(1)}, bf16[64,128]{1,0:T(8,128)(2,1)S(1)}, bf16[64,128]{1,0:T(8,128)(2,1)S(1)}) custom-call(s32[4,128]{1,0:T(4,128)S(1)} %copy-done.1, s32[4,128]{1,0:T(4,128)S(1)} %collective-permute-done.refs_1_, s32[4,128]{1,0:T(4,128)S(1)} %collective-permute-done.1.refs_2_, ...), custom_call_target="tpu_custom_call" | custom-call | tf_op jit(solution)/shard_map/pallas_call | solution.py:463
  11.7 2.2 %collective-permute-start.4 = (bf16[64,128]{1,0:T(8,128)(2,1)S(1)}, bf16[64,128]{1,0:T(8,128)(2,1)S(1)}, u32[]{:S(2)}, u32[]{:S(2)}) collective-permute-start(bf16[64,128]{1,0:T(8,128)(2,1)S(1)} %get-tuple-element.16), channel_id=1, source_target_pairs={{0,25},{1,24},{2,27},{3,26},{4,29},{5,28},{6,31},{7,30},{8,17},{9,... | collective-permute-start | bytes 49160 | tf_op jit(solution)/shard_map/ppermute | solution.py:491
  13.9 0.1 collective-permute-start.5
  14.0 1.9 %collective-permute-start.6 = (bf16[64,128]{1,0:T(8,128)(2,1)S(1)}, bf16[64,128]{1,0:T(8,128)(2,1)S(1)}, u32[]{:S(2)}, u32[]{:S(2)}) collective-permute-start(bf16[64,128]{1,0:T(8,128)(2,1)S(1)} %get-tuple-element.18), channel_id=1, source_target_pairs={{0,8},{1,9},{2,10},{3,11},{4,12},{5,13},{6,14},{7,15},{8,0},{9,1},... | collective-permute-start | bytes 49160 | tf_op jit(solution)/shard_map/ppermute | solution.py:491
  15.9 0.0 copy-done.5
  15.9 0.1 reshape.13
  16.0 0.1 reshape.14.refs_9_
  16.1 0.5 %shard_map.79 = (bf16[512,512]{1,0:T(8,128)(2,1)S(1)}, f32[4,128]{1,0:T(4,128)S(1)}) custom-call(s32[4,128]{1,0:T(4,128)S(1)} %copy-done.1, bf16[64,128]{1,0:T(8,128)(2,1)S(1)} %get-tuple-element.19.after_ref.refs_3_), custom_call_target="tpu_custom_call" | custom-call | tf_op jit(solution)/shard_map/pallas_call | solution.py:463
  16.6 0.3 collective-permute-done.4.refs_0_
  16.8 1.3 %collective-permute-done.5.refs_1_ = bf16[64,128]{1,0:T(8,128)(2,1)S(1)} collective-permute-done((bf16[64,128]{1,0:T(8,128)(2,1)S(1)}, bf16[64,128]{1,0:T(8,128)(2,1)S(1)}, u32[]{:S(2)}, u32[]{:S(2)}) %collective-permute-start.5) | collective-permute-done | bytes 16416 | tf_op jit(solution)/shard_map/ppermute | solution.py:491
  18.1 0.0 collective-permute-done.6.refs_2_
  18.1 2.6 %shard_map.80 = (f32[3,8,128]{2,1,0:T(8,128)S(1)}, f32[8,2,16,128]{3,2,1,0:T(8,128)S(1)}) custom-call(bf16[64,128]{1,0:T(8,128)(2,1)S(1)} %collective-permute-done.4.refs_0_, bf16[64,128]{1,0:T(8,128)(2,1)S(1)} %collective-permute-done.5.refs_1_, bf16[64,128]{1,0:T(8,128)(2,1)S(1)} %collective-permute-done.6.refs_2_, ...), custom_call_target="tpu_custom_call" | custom-call | tf_op jit(solution)/shard_map/pallas_call | solution.py:463
  20.7 11.3 %all_to_all.5.recv_ref = f32[16,16,128]{2,1,0:T(8,128)S(1)} all-to-all(f32[16,16,128]{2,1,0:T(8,128)S(1)} %bitcast.5), channel_id=1, replica_groups={{0,2,4,6,8,10,12,14,17,19,21,23,25,27,29,31},{1,3,5,7,9,11,13,15,16,18,..., dimensions={0} | all-to-all | bytes 262144 | tf_op jit(solution)/shard_map/all_to_all | solution.py:511
  32.0 1.4 %collective-permute-start.7 = (f32[16,16,128]{2,1,0:T(8,128)S(1)}, f32[16,16,128]{2,1,0:T(8,128)S(1)}, u32[]{:S(2)}, u32[]{:S(2)}) collective-permute-start(f32[16,16,128]{2,1,0:T(8,128)S(1)} %all_to_all.5.recv_ref), channel_id=1, source_target_pairs={{0,1},{1,0},{2,3},{3,2},{4,5},{5,4},{6,7},{7,6},{8,9},{9,8},{10,11... | collective-permute-start | bytes 393224 | tf_op jit(solution)/shard_map/ppermute | solution.py:474
  33.4 0.9 %shard_map.81.sum_ref = f32[80,1024]{1,0:T(8,128)S(1)} custom-call(f32[16,16,128]{2,1,0:T(8,128)S(1)} %all_to_all.5.recv_ref), custom_call_target="tpu_custom_call" | custom-call | tf_op jit(solution)/shard_map/pallas_call | solution.py:463
  34.4 0.1 collective-permute-done.7.recv_ref
  34.4 1.6 %shard_map.82 = (f32[64,1024]{1,0:T(8,128)}, f32[3,4,256]{2,1,0:T(4,128)}) custom-call(f32[16,16,128]{2,1,0:T(8,128)S(1)} %collective-permute-done.7.recv_ref, f32[80,1024]{1,0:T(8,128)S(1)} %shard_map.81.sum_ref, f32[3,8,128]{2,1,0:T(8,128)S(1)} %get-tuple-element.25.spread_ref), custom_call_target="tpu_custom_call" | custom-call | tf_op jit(solution)/shard_map/pallas_call | solution.py:463
  (1 shorter events, 0.0 us)
Async XLA Ops:
  0.6 7.1 %copy-start.4 = (s32[4]{0:T(128)S(1)}, s32[4]{0:T(128)}, u32[]{:S(2)}) copy-start(s32[4]{0:T(128)} %cam_index_ref.1) | copy-start | bytes 52
  0.6 7.1 %copy-start.3 = (s32[4]{0:T(128)S(1)}, s32[4]{0:T(128)}, u32[]{:S(2)}) copy-start(s32[4]{0:T(128)} %tile_pos_ref.1) | copy-start | bytes 52
  0.7 9.9 %collective-permute-start.3 = (bf16[64,1024]{1,0:T(8,128)(2,1)}, bf16[64,1024]{1,0:T(8,128)(2,1)S(1)}, u32[]{:S(2)}, u32[]{:S(2)}) collective-permute-start(bf16[64,1024]{1,0:T(8,128)(2,1)} %params_ref.1), channel_id=1, source_target_pairs={{0,4},{4,0},{8,12},{12,8},{16,20},{20,16},{24,28},{28,24},{1,5},{5... | collective-permute-start | bytes 393224 | tf_op jit(solution)/shard_map/ppermute | solution.py:474
  3.7 6.5 %collective-permute-start.2 = (s32[4,128]{1,0:T(4,128)}, s32[4,128]{1,0:T(4,128)S(1)}, u32[]{:S(2)}, u32[]{:S(2)}) collective-permute-start(s32[4,128]{1,0:T(4,128)} %refs_4_.1), channel_id=1, source_target_pairs={{0,25},{1,24},{2,27},{3,26},{4,29},{5,28},{6,31},{7,30},{8,17},{9,... | collective-permute-start | bytes 6152 | tf_op jit(solution)/shard_map/ppermute | solution.py:491
  6.4 4.1 %collective-permute-start.1 = (s32[4,128]{1,0:T(4,128)}, s32[4,128]{1,0:T(4,128)S(1)}, u32[]{:S(2)}, u32[]{:S(2)}) collective-permute-start(s32[4,128]{1,0:T(4,128)} %refs_4_.1), channel_id=1, source_target_pairs={{0,17},{1,16},{2,19},{3,18},{4,21},{5,20},{6,23},{7,22},{8,25},{9,... | collective-permute-start | bytes 6152 | tf_op jit(solution)/shard_map/ppermute | solution.py:491
  6.4 4.1 %collective-permute-start = (s32[4,128]{1,0:T(4,128)}, s32[4,128]{1,0:T(4,128)S(1)}, u32[]{:S(2)}, u32[]{:S(2)}) collective-permute-start(s32[4,128]{1,0:T(4,128)} %refs_4_.1), channel_id=1, source_target_pairs={{0,8},{1,9},{2,10},{3,11},{4,12},{5,13},{6,14},{7,15},{8,0},{9,1},... | collective-permute-start | bytes 6152 | tf_op jit(solution)/shard_map/ppermute | solution.py:491
  7.8 0.9 %copy-start = (bf16[64,1024]{1,0:T(8,128)(2,1)S(1)}, bf16[64,1024]{1,0:T(8,128)(2,1)}, u32[]{:S(2)}) copy-start(bf16[64,1024]{1,0:T(8,128)(2,1)} %params_ref.1) | copy-start | bytes 393220
  8.7 0.7 %copy-start.2 = (f32[28,16]{0,1:T(8,128)S(1)}, f32[28,16]{0,1:T(8,128)}, u32[]{:S(2)}) copy-start(f32[28,16]{0,1:T(8,128)} %param.10) | copy-start | bytes 5380
  9.4 1.2 %copy-start.1 = (s32[4,128]{1,0:T(4,128)S(1)}, s32[4,128]{1,0:T(4,128)}, u32[]{:S(2)}) copy-start(s32[4,128]{1,0:T(4,128)} %refs_4_.1) | copy-start | bytes 6148
  10.5 5.3 %copy-start.5 = (f32[3,4,256]{2,1,0:T(4,128)S(1)}, f32[3,4,256]{2,1,0:T(4,128)}, u32[]{:S(2)}) copy-start(f32[3,4,256]{2,1,0:T(4,128)} %param.11) | copy-start | bytes 36868
  11.7 5.1 %collective-permute-start.4 = (bf16[64,128]{1,0:T(8,128)(2,1)S(1)}, bf16[64,128]{1,0:T(8,128)(2,1)S(1)}, u32[]{:S(2)}, u32[]{:S(2)}) collective-permute-start(bf16[64,128]{1,0:T(8,128)(2,1)S(1)} %get-tuple-element.16), channel_id=1, source_target_pairs={{0,25},{1,24},{2,27},{3,26},{4,29},{5,28},{6,31},{7,30},{8,17},{9,... | collective-permute-start | bytes 49160 | tf_op jit(solution)/shard_map/ppermute | solution.py:491
  13.9 4.2 %collective-permute-start.5 = (bf16[64,128]{1,0:T(8,128)(2,1)S(1)}, bf16[64,128]{1,0:T(8,128)(2,1)S(1)}, u32[]{:S(2)}, u32[]{:S(2)}) collective-permute-start(bf16[64,128]{1,0:T(8,128)(2,1)S(1)} %get-tuple-element.17), channel_id=1, source_target_pairs={{0,17},{1,16},{2,19},{3,18},{4,21},{5,20},{6,23},{7,22},{8,25},{9,... | collective-permute-start | bytes 49160 | tf_op jit(solution)/shard_map/ppermute | solution.py:491
  14.0 4.1 %collective-permute-start.6 = (bf16[64,128]{1,0:T(8,128)(2,1)S(1)}, bf16[64,128]{1,0:T(8,128)(2,1)S(1)}, u32[]{:S(2)}, u32[]{:S(2)}) collective-permute-start(bf16[64,128]{1,0:T(8,128)(2,1)S(1)} %get-tuple-element.18), channel_id=1, source_target_pairs={{0,8},{1,9},{2,10},{3,11},{4,12},{5,13},{6,14},{7,15},{8,0},{9,1},... | collective-permute-start | bytes 49160 | tf_op jit(solution)/shard_map/ppermute | solution.py:491
  32.0 2.4 %collective-permute-start.7 = (f32[16,16,128]{2,1,0:T(8,128)S(1)}, f32[16,16,128]{2,1,0:T(8,128)S(1)}, u32[]{:S(2)}, u32[]{:S(2)}) collective-permute-start(f32[16,16,128]{2,1,0:T(8,128)S(1)} %all_to_all.5.recv_ref), channel_id=1, source_target_pairs={{0,1},{1,0},{2,3},{3,2},{4,5},{5,4},{6,7},{7,6},{8,9},{9,8},{10,11... | collective-permute-start | bytes 393224 | tf_op jit(solution)/shard_map/ppermute | solution.py:474

commit v4 on v3

--- a/solution.py
+++ b/solution.py
@@ -185,10 +185,24 @@
     return out
 
 
-def prepare_kernel(
-    tile_pos_ref, cam_index_ref, cams_ref, params_ref, copy_ref, cam_ref, pixel_ref
+def prepare_kernel(params_ref, copy_ref):
+    copy_ref[...] = params_ref[...]
+
+
+def place_kernel(
+    owners,
+    cap,
+    g_dev,
+    tile_pos_ref,
+    cam_index_ref,
+    cams_ref,
+    lists_ref,
+    after_ref,
+    hot_ref,
+    local_ref,
+    cam_ref,
+    pixel_ref,
 ):
-    copy_ref[...] = params_ref[...]
     values, tiles, length = cam_ref.shape
     share = LANES // tiles
     depth = SIDE * SIDE // share
@@ -203,10 +217,6 @@
     origin_y = [(SIDE * (lax.div(p, WIN) - WIN // 2)).astype(F32) + 0.5 for p in pos]
     pixel_row = iota((depth, LANES), 0) * (share // SIDE) + (lane % share) // SIDE
     pixel_ref[1] = by_tile(origin_y, lane // share) + pixel_row.astype(F32)
-
-
-def place_kernel(owners, cap, g_dev, lists_ref, after_ref, hot_ref, local_ref):
-    tiles, length = lists_ref.shape
     slots = owners * cap
     ids = lists_ref[...]
     masks = [(ids >= o * g_dev) & (ids < (o + 1) * g_dev) for o in range(owners)]
@@ -401,7 +411,7 @@
             send_ref[o, c] = block
 
 
-def scatter(cap, recv_ref, g_dev):
+def entry_rows(cap, recv_ref):
     blocks, high, _ = recv_ref.shape
     values = jnp.concatenate(
         [
@@ -417,49 +427,69 @@
     terms = sh_terms(ray_x * dir_z, ray_y * dir_z, dir_z)
     terms = jnp.concatenate([jnp.ones_like(dir_z)] + terms, axis=0)
     rows = [values] + [terms * values[11 + k : 12 + k] for k in range(3)]
-    hot = one_hot(iota((g_dev, blocks * cap), 0) == values[21:22].astype(jnp.int32))
     parts = split(jnp.concatenate(rows, axis=0), 2)
-    total = dot(jnp.concatenate(parts, axis=0), hot, 1, 1)
-    count = total.shape[0] // 2
-    return total[:count] + total[count:]
-
-
-def in_order(total, out_ref):
-    out_ref[:11, :] = total[:11]
-    out_ref[11:59, :] = total[SENT:]
-    out_ref[59:, :] = total[16:21]
+    return jnp.concatenate(parts, axis=0), values[21:22].astype(jnp.int32)
+
+
+def scatter(rows, where, first, count):
+    hot = one_hot(iota((count, where.shape[1]), 0) + first == where)
+    total = dot(rows, hot, 1, 1)
+    half = total.shape[0] // 2
+    return total[:half] + total[half:]
+
+
+def in_order(total):
+    return jnp.concatenate([total[:11], total[SENT:], total[16:21]], axis=0)
 
 
 def scatter_kernel(cap, recv_ref, out_ref):
-    in_order(scatter(cap, recv_ref, out_ref.shape[1]), out_ref)
+    rows, where = entry_rows(cap, recv_ref)
+    out_ref[...] = in_order(scatter(rows, where, 0, out_ref.shape[1]))
 
 
 def first_kernel(cap, recv_ref, out_ref):
-    out_ref[...] = scatter(cap, recv_ref, out_ref.shape[1])
-
-
-def last_kernel(cap, recv_ref, sum_ref, spread_ref, out_ref, pictures_ref):
-    in_order(sum_ref[...] + scatter(cap, recv_ref, out_ref.shape[1]), out_ref)
-    _, tiles, _ = pictures_ref.shape
+    rows, where = entry_rows(cap, recv_ref)
+    out_ref[...] = scatter(rows, where, 0, out_ref.shape[1])
+
+
+def last_kernel(
+    cap, recv_ref, sum_ref, spread_ref, out_ref, pictures_ref, sums, pictures, out_sem, picture_sem
+):
+    _, tiles, _ = pictures.shape
     depth = spread_ref.shape[1]
     share = LANES // tiles
     for k in range(3):
         for t in range(tiles):
-            pictures_ref[k, t : t + 1, :] = jnp.concatenate(
+            pictures[k, t : t + 1, :] = jnp.concatenate(
                 [
                     spread_ref[k, s : s + 1, t * share : (t + 1) * share]
                     for s in range(depth)
                 ],
                 axis=1,
             )
-
-
-def call(kernel, out_shape, args, scalars=0, left=0, scratch=()):
+    copies = [pltpu.make_async_copy(pictures, pictures_ref, picture_sem)]
+    copies[0].start()
+    rows, where = entry_rows(cap, recv_ref)
+    blocks, _, count = sums.shape
+    for b in range(blocks):
+        columns = slice(b * count, (b + 1) * count)
+        sums[b] = in_order(sum_ref[:, columns] + scatter(rows, where, b * count, count))
+        copies.append(
+            pltpu.make_async_copy(
+                sums.at[b], out_ref.at[:, pl.ds(b * count, count)], out_sem.at[b]
+            )
+        )
+        copies[-1].start()
+    for copy in copies:
+        copy.wait()
+
+
+def call(kernel, out_shape, args, scalars=0, left=0, out_left=False, scratch=()):
     in_specs = [pl.BlockSpec(memory_space=pltpu.SMEM)] * scalars
     in_specs += [pl.BlockSpec(memory_space=pltpu.VMEM)] * (len(args) - scalars - left)
     in_specs += [pl.BlockSpec(memory_space=pl.ANY)] * left
     many = isinstance(out_shape, (list, tuple))
-    spec = pl.BlockSpec(memory_space=pltpu.VMEM)
+    spec = pl.BlockSpec(memory_space=pl.ANY if out_left else pltpu.VMEM)
     return pl.pallas_call(
         kernel,
         out_shape=out_shape,
@@ -542,16 +572,7 @@
     if paired:
         other = swap(params, "gauss", 1)
         all_lists = far_first([lists] * peers)
-    params_copy, cam, pixel = call(
-        prepare_kernel,
-        [
-            shape((width, g_dev), BF16),
-            shape((cams.shape[0], tiles, length), F32),
-            shape((2, depth, LANES), F32),
-        ],
-        (tile_pos, cam_index, cams.T, params),
-        scalars=3,
-    )
+    params_copy = call(prepare_kernel, shape((width, g_dev), BF16), (params,))
     if paired:
         picked = call(
             functools.partial(pick_pair_kernel, cap, peers),
@@ -573,10 +594,16 @@
         )
         returned = [exchange(picked.reshape(owners, cap, LANES))]
         after = picked
-    hot, local = call(
+    hot, local, cam, pixel = call(
         functools.partial(place_kernel, owners, cap, g_dev),
-        [shape((slots, tiles * length), BF16), shape((tiles, length), F32)],
-        (lists, after),
+        [
+            shape((slots, tiles * length), BF16),
+            shape((tiles, length), F32),
+            shape((cams.shape[0], tiles, length), F32),
+            shape((2, depth, LANES), F32),
+        ],
+        (tile_pos, cam_index, cams.T, lists, after),
+        scalars=3,
         left=1,
     )
     spread_targets = (
@@ -603,10 +630,18 @@
         total = call(
             functools.partial(first_kernel, cap), shape((SENT + 48, g_dev), F32), (received,)
         )
+        parts = 4
         grads, pictures = call(
             functools.partial(last_kernel, cap),
             [shape((width, g_dev), F32), shape(targets.shape, F32)],
             (other, total, pictures),
+            out_left=True,
+            scratch=(
+                pltpu.VMEM((parts, width, g_dev // parts), F32),
+                pltpu.VMEM(targets.shape, F32),
+                pltpu.SemaphoreType.DMA((parts,)),
+                pltpu.SemaphoreType.DMA,
+            ),
         )
         return (pictures, grads)
     pictures = (

time: 36.3 us -> 36.2 us (level)
  transfers between devices with their start and end apart: 8 -> 8, of which waited for: 4 -> 2; matrix products, arithmetic and copies ran while one was open for 1% -> 1% of each run, Pallas kernels for 6% -> 6%
where the time goes in v4:
time: 36.2 us; the launch traced here: 35.9 us
  starting transfers between devices  12.8 us (35%)
  blocking collectives  11.3 us (31%)
  Pallas kernels  7.4 us (20%)
  waiting for transfers between devices  1.92 us (5%)
  local copies, waits for them, and re-layouts  1.76 us (5%)
  between operations  0.74 us (2%)
    all_to_all x1, blocking collectives, exchange_wide(): lax.all_to_all(blocks, ('gauss', 'view'), split_axis=0, concat_axis=0, ax...  11.3 us
    ppermute x6, starting transfers between devices, far_first(): out.append(lax.ppermute(block, ('gauss', 'view'), pairs) if k else block)  8.28 us
    pallas_call x6, Pallas kernels, call(): pl.pallas_call(kernel, out_shape=out_shape, in_specs=in_specs, out_specs=...  7.4 us
    ppermute x2, starting transfers between devices, swap(): lax.ppermute(x, axis, [(i, i ^ k) for i in range(lax.axis_size(axis))])  4.5 us
    ppermute x6, waiting for transfers between devices, far_first(): out.append(lax.ppermute(block, ('gauss', 'view'), pairs) if k else block)  1.86 us
    unnamed x12, local copies, waits for them, and re-layouts  1.58 us
  transfers between devices with their start and end apart: 8, of which 2 were waited for; matrix products, arithmetic and copies ran while one was open for 1% of the time, Pallas kernels for 6%

profile of v4, /device:TPU:0, one launch (start us, length us, event | category | flops | bytes accessed | tf_op | source)
XLA Modules:
  0.0 35.9 jit_solution(16042734895030311847)
XLA Ops:
  0.6 3.0 %collective-permute-start.3 = (bf16[64,1024]{1,0:T(8,128)(2,1)}, bf16[64,1024]{1,0:T(8,128)(2,1)S(1)}, u32[]{:S(2)}, u32[]{:S(2)}) collective-permute-start(bf16[64,1024]{1,0:T(8,128)(2,1)} %params_ref.1), channel_id=1, source_target_pairs={{0,4},{4,0},{8,12},{12,8},{16,20},{20,16},{24,28},{28,24},{1,5},{5... | collective-permute-start | bytes 393224 | tf_op jit(solution)/shard_map/ppermute | solution.py:504
  3.6 2.8 %collective-permute-start.2 = (s32[4,128]{1,0:T(4,128)}, s32[4,128]{1,0:T(4,128)S(1)}, u32[]{:S(2)}, u32[]{:S(2)}) collective-permute-start(s32[4,128]{1,0:T(4,128)} %refs_4_.1), channel_id=1, source_target_pairs={{0,25},{1,24},{2,27},{3,26},{4,29},{5,28},{6,31},{7,30},{8,17},{9,... | collective-permute-start | bytes 6152 | tf_op jit(solution)/shard_map/ppermute | solution.py:521
  6.4 0.0 collective-permute-start.1
  6.4 1.3 %collective-permute-start = (s32[4,128]{1,0:T(4,128)}, s32[4,128]{1,0:T(4,128)S(1)}, u32[]{:S(2)}, u32[]{:S(2)}) collective-permute-start(s32[4,128]{1,0:T(4,128)} %refs_4_.1), channel_id=1, source_target_pairs={{0,8},{1,9},{2,10},{3,11},{4,12},{5,13},{6,14},{7,15},{8,0},{9,1},... | collective-permute-start | bytes 6152 | tf_op jit(solution)/shard_map/ppermute | solution.py:521
  7.7 0.0 copy-start
  7.7 0.9 %copy-done = bf16[64,1024]{1,0:T(8,128)(2,1)S(1)} copy-done((bf16[64,1024]{1,0:T(8,128)(2,1)S(1)}, bf16[64,1024]{1,0:T(8,128)(2,1)}, u32[]{:S(2)}) %copy-start) | copy-done | bytes 131096
  8.6 0.0 copy-start.1
  8.7 0.0 collective-permute-done.2.refs_3_
  8.7 1.8 %collective-permute-done.1.refs_2_ = s32[4,128]{1,0:T(4,128)S(1)} collective-permute-done((s32[4,128]{1,0:T(4,128)}, s32[4,128]{1,0:T(4,128)S(1)}, u32[]{:S(2)}, u32[]{:S(2)}) %collective-permute-start.1) | collective-permute-done | bytes 2080 | tf_op jit(solution)/shard_map/ppermute | solution.py:521
  10.5 0.0 collective-permute-done.refs_1_
  10.5 0.0 collective-permute-done.3.refs_5_
  10.5 0.0 copy-done.1
  10.5 0.0 copy-start.5
  10.5 1.1 %shard_map.78 = (bf16[64,128]{1,0:T(8,128)(2,1)S(1)}, bf16[64,128]{1,0:T(8,128)(2,1)S(1)}, bf16[64,128]{1,0:T(8,128)(2,1)S(1)}, bf16[64,128]{1,0:T(8,128)(2,1)S(1)}) custom-call(s32[4,128]{1,0:T(4,128)S(1)} %copy-done.1, s32[4,128]{1,0:T(4,128)S(1)} %collective-permute-done.refs_1_, s32[4,128]{1,0:T(4,128)S(1)} %collective-permute-done.1.refs_2_, ...), custom_call_target="tpu_custom_call" | custom-call | tf_op jit(solution)/shard_map/pallas_call | solution.py:493
  11.7 1.3 %collective-permute-start.4 = (bf16[64,128]{1,0:T(8,128)(2,1)S(1)}, bf16[64,128]{1,0:T(8,128)(2,1)S(1)}, u32[]{:S(2)}, u32[]{:S(2)}) collective-permute-start(bf16[64,128]{1,0:T(8,128)(2,1)S(1)} %get-tuple-element.14), channel_id=1, source_target_pairs={{0,25},{1,24},{2,27},{3,26},{4,29},{5,28},{6,31},{7,30},{8,17},{9,... | collective-permute-start | bytes 49160 | tf_op jit(solution)/shard_map/ppermute | solution.py:521
  13.0 0.9 %collective-permute-start.5 = (bf16[64,128]{1,0:T(8,128)(2,1)S(1)}, bf16[64,128]{1,0:T(8,128)(2,1)S(1)}, u32[]{:S(2)}, u32[]{:S(2)}) collective-permute-start(bf16[64,128]{1,0:T(8,128)(2,1)S(1)} %get-tuple-element.15), channel_id=1, source_target_pairs={{0,17},{1,16},{2,19},{3,18},{4,21},{5,20},{6,23},{7,22},{8,25},{9,... | collective-permute-start | bytes 49160 | tf_op jit(solution)/shard_map/ppermute | solution.py:521
  13.9 1.9 %collective-permute-start.6 = (bf16[64,128]{1,0:T(8,128)(2,1)S(1)}, bf16[64,128]{1,0:T(8,128)(2,1)S(1)}, u32[]{:S(2)}, u32[]{:S(2)}) collective-permute-start(bf16[64,128]{1,0:T(8,128)(2,1)S(1)} %get-tuple-element.16), channel_id=1, source_target_pairs={{0,8},{1,9},{2,10},{3,11},{4,12},{5,13},{6,14},{7,15},{8,0},{9,1},... | collective-permute-start | bytes 49160 | tf_op jit(solution)/shard_map/ppermute | solution.py:521
  15.9 0.0 copy-done.5
  15.9 0.1 reshape.13
  16.0 0.0 copy-start.2
  16.0 0.1 reshape.14.refs_9_
  16.1 0.0 copy-start.3
  16.1 0.0 copy-start.4
  16.1 0.6 %copy-done.2 = f32[28,16]{0,1:T(8,128)S(1)} copy-done((f32[28,16]{0,1:T(8,128)S(1)}, f32[28,16]{0,1:T(8,128)}, u32[]{:S(2)}) %copy-start.2) | copy-done | bytes 1816
  16.7 0.1 copy-done.3
  16.7 0.0 copy-done.4
  16.7 1.2 %shard_map.79 = (bf16[512,512]{1,0:T(8,128)(2,1)S(1)}, f32[4,128]{1,0:T(4,128)S(1)}, f32[28,4,128]{2,1,0:T(4,128)S(1)}, f32[2,8,128]{2,1,0:T(8,128)S(1)}) custom-call(s32[4]{0:T(128)S(1)} %copy-done.3, s32[4]{0:T(128)S(1)} %copy-done.4, f32[16,28]{1,0:T(8,128)S(1)} %bitcast.6, s32[4,128]{1,0:T(4,128)S(1)} %copy-done.1, ...), custom_call_target="tpu_custom_call" | custom-call | tf_op jit(solution)/shard_map/pallas_call | solution.py:493
  17.9 0.0 collective-permute-done.4.refs_0_
  17.9 0.0 collective-permute-done.5.refs_1_
  17.9 0.0 collective-permute-done.6.refs_2_
  17.9 2.6 %shard_map.80 = (f32[3,8,128]{2,1,0:T(8,128)S(1)}, f32[8,2,16,128]{3,2,1,0:T(8,128)S(1)}) custom-call(bf16[64,128]{1,0:T(8,128)(2,1)S(1)} %collective-permute-done.4.refs_0_, bf16[64,128]{1,0:T(8,128)(2,1)S(1)} %collective-permute-done.5.refs_1_, bf16[64,128]{1,0:T(8,128)(2,1)S(1)} %collective-permute-done.6.refs_2_, ...), custom_call_target="tpu_custom_call" | custom-call | tf_op jit(solution)/shard_map/pallas_call | solution.py:493
  20.5 11.3 %all_to_all.5.recv_ref = f32[16,16,128]{2,1,0:T(8,128)S(1)} all-to-all(f32[16,16,128]{2,1,0:T(8,128)S(1)} %bitcast.5), channel_id=1, replica_groups={{0,2,4,6,8,10,12,14,17,19,21,23,25,27,29,31},{1,3,5,7,9,11,13,15,16,18,..., dimensions={0} | all-to-all | bytes 262144 | tf_op jit(solution)/shard_map/all_to_all | solution.py:541
  31.8 1.5 %collective-permute-start.7 = (f32[16,16,128]{2,1,0:T(8,128)S(1)}, f32[16,16,128]{2,1,0:T(8,128)S(1)}, u32[]{:S(2)}, u32[]{:S(2)}) collective-permute-start(f32[16,16,128]{2,1,0:T(8,128)S(1)} %all_to_all.5.recv_ref), channel_id=1, source_target_pairs={{0,1},{1,0},{2,3},{3,2},{4,5},{5,4},{6,7},{7,6},{8,9},{9,8},{10,11... | collective-permute-start | bytes 393224 | tf_op jit(solution)/shard_map/ppermute | solution.py:504
  33.3 0.9 %shard_map.81.sum_ref = f32[80,1024]{1,0:T(8,128)S(1)} custom-call(f32[16,16,128]{2,1,0:T(8,128)S(1)} %all_to_all.5.recv_ref), custom_call_target="tpu_custom_call" | custom-call | tf_op jit(solution)/shard_map/pallas_call | solution.py:493
  34.2 0.1 collective-permute-done.7.recv_ref
  34.3 1.6 %shard_map.82 = (f32[64,1024]{1,0:T(8,128)}, f32[3,4,256]{2,1,0:T(4,128)}) custom-call(f32[16,16,128]{2,1,0:T(8,128)S(1)} %collective-permute-done.7.recv_ref, f32[80,1024]{1,0:T(8,128)S(1)} %shard_map.81.sum_ref, f32[3,8,128]{2,1,0:T(8,128)S(1)} %get-tuple-element.23.spread_ref), custom_call_target="tpu_custom_call" | custom-call | tf_op jit(solution)/shard_map/pallas_call | solution.py:493
  (2 shorter events, 0.0 us)
Async XLA Ops:
  0.6 9.9 %collective-permute-start.3 = (bf16[64,1024]{1,0:T(8,128)(2,1)}, bf16[64,1024]{1,0:T(8,128)(2,1)S(1)}, u32[]{:S(2)}, u32[]{:S(2)}) collective-permute-start(bf16[64,1024]{1,0:T(8,128)(2,1)} %params_ref.1), channel_id=1, source_target_pairs={{0,4},{4,0},{8,12},{12,8},{16,20},{20,16},{24,28},{28,24},{1,5},{5... | collective-permute-start | bytes 393224 | tf_op jit(solution)/shard_map/ppermute | solution.py:504
  3.6 5.0 %collective-permute-start.2 = (s32[4,128]{1,0:T(4,128)}, s32[4,128]{1,0:T(4,128)S(1)}, u32[]{:S(2)}, u32[]{:S(2)}) collective-permute-start(s32[4,128]{1,0:T(4,128)} %refs_4_.1), channel_id=1, source_target_pairs={{0,25},{1,24},{2,27},{3,26},{4,29},{5,28},{6,31},{7,30},{8,17},{9,... | collective-permute-start | bytes 6152 | tf_op jit(solution)/shard_map/ppermute | solution.py:521
  6.4 4.1 %collective-permute-start.1 = (s32[4,128]{1,0:T(4,128)}, s32[4,128]{1,0:T(4,128)S(1)}, u32[]{:S(2)}, u32[]{:S(2)}) collective-permute-start(s32[4,128]{1,0:T(4,128)} %refs_4_.1), channel_id=1, source_target_pairs={{0,17},{1,16},{2,19},{3,18},{4,21},{5,20},{6,23},{7,22},{8,25},{9,... | collective-permute-start | bytes 6152 | tf_op jit(solution)/shard_map/ppermute | solution.py:521
  6.4 4.1 %collective-permute-start = (s32[4,128]{1,0:T(4,128)}, s32[4,128]{1,0:T(4,128)S(1)}, u32[]{:S(2)}, u32[]{:S(2)}) collective-permute-start(s32[4,128]{1,0:T(4,128)} %refs_4_.1), channel_id=1, source_target_pairs={{0,8},{1,9},{2,10},{3,11},{4,12},{5,13},{6,14},{7,15},{8,0},{9,1},... | collective-permute-start | bytes 6152 | tf_op jit(solution)/shard_map/ppermute | solution.py:521
  7.7 0.9 %copy-start = (bf16[64,1024]{1,0:T(8,128)(2,1)S(1)}, bf16[64,1024]{1,0:T(8,128)(2,1)}, u32[]{:S(2)}) copy-start(bf16[64,1024]{1,0:T(8,128)(2,1)} %params_ref.1) | copy-start | bytes 393220
  8.6 1.9 %copy-start.1 = (s32[4,128]{1,0:T(4,128)S(1)}, s32[4,128]{1,0:T(4,128)}, u32[]{:S(2)}) copy-start(s32[4,128]{1,0:T(4,128)} %refs_4_.1) | copy-start | bytes 6148
  10.5 5.3 %copy-start.5 = (f32[3,4,256]{2,1,0:T(4,128)S(1)}, f32[3,4,256]{2,1,0:T(4,128)}, u32[]{:S(2)}) copy-start(f32[3,4,256]{2,1,0:T(4,128)} %param.11) | copy-start | bytes 36868
  11.7 6.2 %collective-permute-start.4 = (bf16[64,128]{1,0:T(8,128)(2,1)S(1)}, bf16[64,128]{1,0:T(8,128)(2,1)S(1)}, u32[]{:S(2)}, u32[]{:S(2)}) collective-permute-start(bf16[64,128]{1,0:T(8,128)(2,1)S(1)} %get-tuple-element.14), channel_id=1, source_target_pairs={{0,25},{1,24},{2,27},{3,26},{4,29},{5,28},{6,31},{7,30},{8,17},{9,... | collective-permute-start | bytes 49160 | tf_op jit(solution)/shard_map/ppermute | solution.py:521
  13.0 4.9 %collective-permute-start.5 = (bf16[64,128]{1,0:T(8,128)(2,1)S(1)}, bf16[64,128]{1,0:T(8,128)(2,1)S(1)}, u32[]{:S(2)}, u32[]{:S(2)}) collective-permute-start(bf16[64,128]{1,0:T(8,128)(2,1)S(1)} %get-tuple-element.15), channel_id=1, source_target_pairs={{0,17},{1,16},{2,19},{3,18},{4,21},{5,20},{6,23},{7,22},{8,25},{9,... | collective-permute-start | bytes 49160 | tf_op jit(solution)/shard_map/ppermute | solution.py:521
  13.9 4.0 %collective-permute-start.6 = (bf16[64,128]{1,0:T(8,128)(2,1)S(1)}, bf16[64,128]{1,0:T(8,128)(2,1)S(1)}, u32[]{:S(2)}, u32[]{:S(2)}) collective-permute-start(bf16[64,128]{1,0:T(8,128)(2,1)S(1)} %get-tuple-element.16), channel_id=1, source_target_pairs={{0,8},{1,9},{2,10},{3,11},{4,12},{5,13},{6,14},{7,15},{8,0},{9,1},... | collective-permute-start | bytes 49160 | tf_op jit(solution)/shard_map/ppermute | solution.py:521
  16.0 0.7 %copy-start.2 = (f32[28,16]{0,1:T(8,128)S(1)}, f32[28,16]{0,1:T(8,128)}, u32[]{:S(2)}) copy-start(f32[28,16]{0,1:T(8,128)} %param.10) | copy-start | bytes 5380
  16.1 0.7 %copy-start.3 = (s32[4]{0:T(128)S(1)}, s32[4]{0:T(128)}, u32[]{:S(2)}) copy-start(s32[4]{0:T(128)} %tile_pos_ref.1) | copy-start | bytes 52
  16.1 0.7 %copy-start.4 = (s32[4]{0:T(128)S(1)}, s32[4]{0:T(128)}, u32[]{:S(2)}) copy-start(s32[4]{0:T(128)} %cam_index_ref.1) | copy-start | bytes 52
  31.8 2.5 %collective-permute-start.7 = (f32[16,16,128]{2,1,0:T(8,128)S(1)}, f32[16,16,128]{2,1,0:T(8,128)S(1)}, u32[]{:S(2)}, u32[]{:S(2)}) collective-permute-start(f32[16,16,128]{2,1,0:T(8,128)S(1)} %all_to_all.5.recv_ref), channel_id=1, source_target_pairs={{0,1},{1,0},{2,3},{3,2},{4,5},{5,4},{6,7},{7,6},{8,9},{9,8},{10,11... | collective-permute-start | bytes 393224 | tf_op jit(solution)/shard_map/ppermute | solution.py:504

commit v5 on v4

--- a/solution.py
+++ b/solution.py
@@ -118,13 +118,14 @@
 
 def ranks(mask, tiles):
     rows, length = mask.shape
-    bits = one_hot(mask)
+    bits = jnp.where(mask, 1.0, 0.0)
+    place = iota((rows, length), 0) % tiles
+    shifted = [bits] + [
+        jnp.where(place >= d, pltpu.roll(bits, d, 0), 0.0) for d in range(1, tiles)
+    ]
     earlier = one_hot(iota((length, length), 0) < iota((length, length), 1))
-    within = dot(bits, earlier)
-    count = dot(bits, jnp.ones((length, length), BF16)).astype(BF16)
-    here, there = iota((rows, rows), 0), iota((rows, rows), 1)
-    above = one_hot((there < here) & (there >= here - lax.rem(here, tiles)))
-    return (within + dot(above, count)).astype(jnp.int32)
+    counted = jnp.concatenate([earlier] + [jnp.ones_like(earlier)] * (tiles - 1), axis=0)
+    return dot(jnp.concatenate(shifted, axis=1).astype(BF16), counted).astype(jnp.int32)
 
 
 def find(ids, base, tiles, cap, g_dev):
@@ -185,24 +186,10 @@
     return out
 
 
-def prepare_kernel(params_ref, copy_ref):
+def prepare_kernel(
+    tile_pos_ref, cam_index_ref, cams_ref, params_ref, copy_ref, cam_ref, pixel_ref
+):
     copy_ref[...] = params_ref[...]
-
-
-def place_kernel(
-    owners,
-    cap,
-    g_dev,
-    tile_pos_ref,
-    cam_index_ref,
-    cams_ref,
-    lists_ref,
-    after_ref,
-    hot_ref,
-    local_ref,
-    cam_ref,
-    pixel_ref,
-):
     values, tiles, length = cam_ref.shape
     share = LANES // tiles
     depth = SIDE * SIDE // share
@@ -217,6 +204,10 @@
     origin_y = [(SIDE * (lax.div(p, WIN) - WIN // 2)).astype(F32) + 0.5 for p in pos]
     pixel_row = iota((depth, LANES), 0) * (share // SIDE) + (lane % share) // SIDE
     pixel_ref[1] = by_tile(origin_y, lane // share) + pixel_row.astype(F32)
+
+
+def place_kernel(owners, cap, g_dev, lists_ref, after_ref, hot_ref, local_ref):
+    tiles, length = lists_ref.shape
     slots = owners * cap
     ids = lists_ref[...]
     masks = [(ids >= o * g_dev) & (ids < (o + 1) * g_dev) for o in range(owners)]
@@ -298,56 +289,44 @@
     table_ref[3 * length :, :] = table[4 * length :]
 
     def row(index, l):
-        return table_ref[pl.ds(index * length + l, 1), :]
-
-    group = 16
+        return table_ref[index * length + l : index * length + l + 1, :]
+
     zero = jnp.zeros((depth, LANES), F32)
-
-    def forward(chunk, carry):
-        through, red, green, blue = carry
-        for i in range(group):
-            l = chunk * group + i
-            dy = pixel_y - row(2, l)
-            power = row(0, l) + dy * (row(1, l) + row(3, l) * dy)
-            alpha = row(4, l) * jnp.exp2(power)
-            weight = through * alpha
-            red = red + weight * row(5, l)
-            green = green + weight * row(6, l)
-            blue = blue + weight * row(7, l)
-            through = through - weight
-            at = pl.ds(pl.multiple_of(l * depth, depth), depth)
-            alpha_ref[at, :] = alpha
-            weight_ref[at, :] = weight
-        return through, red, green, blue
-
-    start = (jnp.ones((depth, LANES), F32), zero, zero, zero)
-    _, red, green, blue = lax.fori_loop(0, length // group, forward, start)
+    through = jnp.ones((depth, LANES), F32)
+    red, green, blue = zero, zero, zero
+    for l in range(length):
+        dy = pixel_y - row(2, l)
+        power = row(0, l) + dy * (row(1, l) + row(3, l) * dy)
+        alpha = row(4, l) * jnp.exp2(power)
+        weight = through * alpha
+        red = red + weight * row(5, l)
+        green = green + weight * row(6, l)
+        blue = blue + weight * row(7, l)
+        through = through - weight
+        at = slice(l * depth, (l + 1) * depth)
+        alpha_ref[at, :] = alpha
+        weight_ref[at, :] = weight
     pictures_ref[0] = red
     pictures_ref[1] = green
     pictures_ref[2] = blue
     res = [red - targets_ref[0], green - targets_ref[1], blue - targets_ref[2]]
 
-    def backward(step, behind):
-        chunk = length // group - 1 - step
-        for i in reversed(range(group)):
-            l = chunk * group + i
-            at = pl.ds(pl.multiple_of(l * depth, depth), depth)
-            alpha = alpha_ref[at, :]
-            weight = weight_ref[at, :]
-            dy = pixel_y - row(2, l)
-            seen = row(5, l) * res[0] + row(6, l) * res[1] + row(7, l) * res[2]
-            gap = seen - behind
-            behind = behind + alpha * gap
-            g = weight * gap
-            gy = g * dy
-            part_ref[0, at, :] = g
-            part_ref[1, at, :] = gy
-            part_ref[2, at, :] = gy * dy
-            for k in range(3):
-                part_ref[3 + k, at, :] = weight * res[k]
-        return behind
-
-    lax.fori_loop(0, length // group, backward, zero)
+    behind = zero
+    for l in reversed(range(length)):
+        at = slice(l * depth, (l + 1) * depth)
+        alpha = alpha_ref[at, :]
+        weight = weight_ref[at, :]
+        dy = pixel_y - row(2, l)
+        seen = row(5, l) * res[0] + row(6, l) * res[1] + row(7, l) * res[2]
+        gap = seen - behind
+        behind = behind + alpha * gap
+        g = weight * gap
+        gy = g * dy
+        part_ref[0, at, :] = g
+        part_ref[1, at, :] = gy
+        part_ref[2, at, :] = gy * dy
+        for k in range(3):
+            part_ref[3 + k, at, :] = weight * res[k]
 
     def down(index):
         blocks = []
@@ -458,15 +437,18 @@
     _, tiles, _ = pictures.shape
     depth = spread_ref.shape[1]
     share = LANES // tiles
+    lane_block = iota((depth, LANES), 1) // share
+    row = iota((depth, LANES), 0) % tiles
     for k in range(3):
-        for t in range(tiles):
-            pictures[k, t : t + 1, :] = jnp.concatenate(
-                [
-                    spread_ref[k, s : s + 1, t * share : (t + 1) * share]
-                    for s in range(depth)
-                ],
-                axis=1,
-            )
+        spread = spread_ref[k]
+        whole = spread
+        for d in range(1, tiles):
+            down = pltpu.roll(spread, d, 0)
+            up = pltpu.roll(spread, depth + d - tiles, 0)
+            moved = pltpu.roll(jnp.where(row >= d, down, up), LANES - d * share, 1)
+            whole = jnp.where((row - lane_block) % tiles == d, moved, whole)
+        for h in range(depth // tiles):
+            pictures[k, :, h * LANES : (h + 1) * LANES] = whole[h * tiles : (h + 1) * tiles]
     copies = [pltpu.make_async_copy(pictures, pictures_ref, picture_sem)]
     copies[0].start()
     rows, where = entry_rows(cap, recv_ref)
@@ -572,7 +554,16 @@
     if paired:
         other = swap(params, "gauss", 1)
         all_lists = far_first([lists] * peers)
-    params_copy = call(prepare_kernel, shape((width, g_dev), BF16), (params,))
+    params_copy, cam, pixel = call(
+        prepare_kernel,
+        [
+            shape((width, g_dev), BF16),
+            shape((cams.shape[0], tiles, length), F32),
+            shape((2, depth, LANES), F32),
+        ],
+        (tile_pos, cam_index, cams.T, params),
+        scalars=3,
+    )
     if paired:
         picked = call(
             functools.partial(pick_pair_kernel, cap, peers),
@@ -594,16 +585,10 @@
         )
         returned = [exchange(picked.reshape(owners, cap, LANES))]
         after = picked
-    hot, local, cam, pixel = call(
+    hot, local = call(
         functools.partial(place_kernel, owners, cap, g_dev),
-        [
-            shape((slots, tiles * length), BF16),
-            shape((tiles, length), F32),
-            shape((cams.shape[0], tiles, length), F32),
-            shape((2, depth, LANES), F32),
-        ],
-        (tile_pos, cam_index, cams.T, lists, after),
-        scalars=3,
+        [shape((slots, tiles * length), BF16), shape((tiles, length), F32)],
+        (lists, after),
         left=1,
     )
     spread_targets = (

time: 36.2 us -> 36 us (level)
  Pallas kernels: 7.4 us -> 7.02 us
    pallas_call x6, Pallas kernels: 7.4 us -> 7.02 us  [call(): pl.pallas_call(kernel, out_shape=out_shape, in_specs=in_specs, out_specs=...]
  transfers between devices with their start and end apart: 8 -> 8, of which waited for: 2 -> 4; matrix products, arithmetic and copies ran while one was open for 1% -> 1% of each run, Pallas kernels for 6% -> 6%
where the time goes in v5:
time: 36 us; the launch traced here: 35.7 us
  starting transfers between devices  12.7 us (35%)
  blocking collectives  11.3 us (31%)
  Pallas kernels  7.02 us (20%)
  waiting for transfers between devices  2.1 us (6%)
  local copies, waits for them, and re-layouts  1.8 us (5%)
  between operations  0.72 us (2%)
    all_to_all x1, blocking collectives, exchange_wide(): lax.all_to_all(blocks, ('gauss', 'view'), split_axis=0, concat_axis=0, ax...  11.3 us
    ppermute x6, starting transfers between devices, far_first(): out.append(lax.ppermute(block, ('gauss', 'view'), pairs) if k else block)  8.28 us
    pallas_call x6, Pallas kernels, call(): pl.pallas_call(kernel, out_shape=out_shape, in_specs=in_specs, out_specs=...  7.02 us
    ppermute x2, starting transfers between devices, swap(): lax.ppermute(x, axis, [(i, i ^ k) for i in range(lax.axis_size(axis))])  4.45 us
    ppermute x6, waiting for transfers between devices, far_first(): out.append(lax.ppermute(block, ('gauss', 'view'), pairs) if k else block)  2.04 us
    unnamed x12, local copies, waits for them, and re-layouts  1.62 us
  transfers between devices with their start and end apart: 8, of which 4 were waited for; matrix products, arithmetic and copies ran while one was open for 1% of the time, Pallas kernels for 6%

profile of v5, /device:TPU:0, one launch (start us, length us, event | category | flops | bytes accessed | tf_op | source)
XLA Modules:
  0.0 35.7 jit_solution(14880856363924712445)
XLA Ops:
  0.6 0.0 copy-start.4
  0.6 0.0 copy-start.3
  0.7 3.0 %collective-permute-start.3 = (bf16[64,1024]{1,0:T(8,128)(2,1)}, bf16[64,1024]{1,0:T(8,128)(2,1)S(1)}, u32[]{:S(2)}, u32[]{:S(2)}) collective-permute-start(bf16[64,1024]{1,0:T(8,128)(2,1)} %params_ref.1), channel_id=1, source_target_pairs={{0,4},{4,0},{8,12},{12,8},{16,20},{20,16},{24,28},{28,24},{1,5},{5... | collective-permute-start | bytes 393224 | tf_op jit(solution)/shard_map/ppermute | solution.py:486
  3.7 2.8 %collective-permute-start.2 = (s32[4,128]{1,0:T(4,128)}, s32[4,128]{1,0:T(4,128)S(1)}, u32[]{:S(2)}, u32[]{:S(2)}) collective-permute-start(s32[4,128]{1,0:T(4,128)} %refs_4_.1), channel_id=1, source_target_pairs={{0,25},{1,24},{2,27},{3,26},{4,29},{5,28},{6,31},{7,30},{8,17},{9,... | collective-permute-start | bytes 6152 | tf_op jit(solution)/shard_map/ppermute | solution.py:503
  6.4 0.0 collective-permute-start.1
  6.4 1.3 %collective-permute-start = (s32[4,128]{1,0:T(4,128)}, s32[4,128]{1,0:T(4,128)S(1)}, u32[]{:S(2)}, u32[]{:S(2)}) collective-permute-start(s32[4,128]{1,0:T(4,128)} %refs_4_.1), channel_id=1, source_target_pairs={{0,8},{1,9},{2,10},{3,11},{4,12},{5,13},{6,14},{7,15},{8,0},{9,1},... | collective-permute-start | bytes 6152 | tf_op jit(solution)/shard_map/ppermute | solution.py:503
  7.8 0.0 copy-done.4
  7.8 0.0 copy-done.3
  7.8 0.0 copy-start
  7.8 0.9 %copy-done = bf16[64,1024]{1,0:T(8,128)(2,1)S(1)} copy-done((bf16[64,1024]{1,0:T(8,128)(2,1)S(1)}, bf16[64,1024]{1,0:T(8,128)(2,1)}, u32[]{:S(2)}) %copy-start) | copy-done | bytes 131096
  8.7 0.0 copy-start.2
  8.7 0.7 %copy-done.2 = f32[28,16]{0,1:T(8,128)S(1)} copy-done((f32[28,16]{0,1:T(8,128)S(1)}, f32[28,16]{0,1:T(8,128)}, u32[]{:S(2)}) %copy-start.2) | copy-done | bytes 1816
  9.4 0.0 copy-start.1
  9.4 0.8 %shard_map.77 = (bf16[64,1024]{1,0:T(8,128)(2,1)S(1)}, f32[28,4,128]{2,1,0:T(4,128)S(1)}, f32[2,8,128]{2,1,0:T(8,128)S(1)}) custom-call(s32[4]{0:T(128)S(1)} %copy-done.3, s32[4]{0:T(128)S(1)} %copy-done.4, f32[16,28]{1,0:T(8,128)S(1)} %bitcast.6, bf16[64,1024]{1,0:T(8,128)(2,1)S(1)} %copy-done), custom_call_target="tpu_custom_call" | custom-call | tf_op jit(solution)/shard_map/pallas_call | solution.py:475
  10.1 0.0 collective-permute-done.2.refs_3_
  10.2 0.4 %collective-permute-done.1.refs_2_ = s32[4,128]{1,0:T(4,128)S(1)} collective-permute-done((s32[4,128]{1,0:T(4,128)}, s32[4,128]{1,0:T(4,128)S(1)}, u32[]{:S(2)}, u32[]{:S(2)}) %collective-permute-start.1) | collective-permute-done | bytes 2080 | tf_op jit(solution)/shard_map/ppermute | solution.py:503
  10.5 0.0 collective-permute-done.refs_1_
  10.5 0.0 collective-permute-done.3.refs_5_
  10.5 0.0 copy-done.1
  10.5 0.0 copy-start.5
  10.6 1.0 %shard_map.78 = (bf16[64,128]{1,0:T(8,128)(2,1)S(1)}, bf16[64,128]{1,0:T(8,128)(2,1)S(1)}, bf16[64,128]{1,0:T(8,128)(2,1)S(1)}, bf16[64,128]{1,0:T(8,128)(2,1)S(1)}) custom-call(s32[4,128]{1,0:T(4,128)S(1)} %copy-done.1, s32[4,128]{1,0:T(4,128)S(1)} %collective-permute-done.refs_1_, s32[4,128]{1,0:T(4,128)S(1)} %collective-permute-done.1.refs_2_, ...), custom_call_target="tpu_custom_call" | custom-call | tf_op jit(solution)/shard_map/pallas_call | solution.py:475
  11.5 2.2 %collective-permute-start.4 = (bf16[64,128]{1,0:T(8,128)(2,1)S(1)}, bf16[64,128]{1,0:T(8,128)(2,1)S(1)}, u32[]{:S(2)}, u32[]{:S(2)}) collective-permute-start(bf16[64,128]{1,0:T(8,128)(2,1)S(1)} %get-tuple-element.16), channel_id=1, source_target_pairs={{0,25},{1,24},{2,27},{3,26},{4,29},{5,28},{6,31},{7,30},{8,17},{9,... | collective-permute-start | bytes 49160 | tf_op jit(solution)/shard_map/ppermute | solution.py:503
  13.7 0.1 collective-permute-start.5
  13.8 1.9 %collective-permute-start.6 = (bf16[64,128]{1,0:T(8,128)(2,1)S(1)}, bf16[64,128]{1,0:T(8,128)(2,1)S(1)}, u32[]{:S(2)}, u32[]{:S(2)}) collective-permute-start(bf16[64,128]{1,0:T(8,128)(2,1)S(1)} %get-tuple-element.18), channel_id=1, source_target_pairs={{0,8},{1,9},{2,10},{3,11},{4,12},{5,13},{6,14},{7,15},{8,0},{9,1},... | collective-permute-start | bytes 49160 | tf_op jit(solution)/shard_map/ppermute | solution.py:503
  15.7 0.0 copy-done.5
  15.7 0.1 reshape.13
  15.8 0.1 reshape.14.refs_9_
  15.9 0.4 shard_map.79
  16.2 0.4 %collective-permute-done.4.refs_0_ = bf16[64,128]{1,0:T(8,128)(2,1)S(1)} collective-permute-done((bf16[64,128]{1,0:T(8,128)(2,1)S(1)}, bf16[64,128]{1,0:T(8,128)(2,1)S(1)}, u32[]{:S(2)}, u32[]{:S(2)}) %collective-permute-start.4) | collective-permute-done | bytes 16416 | tf_op jit(solution)/shard_map/ppermute | solution.py:503
  16.6 1.3 %collective-permute-done.5.refs_1_ = bf16[64,128]{1,0:T(8,128)(2,1)S(1)} collective-permute-done((bf16[64,128]{1,0:T(8,128)(2,1)S(1)}, bf16[64,128]{1,0:T(8,128)(2,1)S(1)}, u32[]{:S(2)}, u32[]{:S(2)}) %collective-permute-start.5) | collective-permute-done | bytes 16416 | tf_op jit(solution)/shard_map/ppermute | solution.py:503
  17.9 0.0 collective-permute-done.6.refs_2_
  17.9 2.4 %shard_map.80 = (f32[3,8,128]{2,1,0:T(8,128)S(1)}, f32[8,2,16,128]{3,2,1,0:T(8,128)S(1)}) custom-call(bf16[64,128]{1,0:T(8,128)(2,1)S(1)} %collective-permute-done.4.refs_0_, bf16[64,128]{1,0:T(8,128)(2,1)S(1)} %collective-permute-done.5.refs_1_, bf16[64,128]{1,0:T(8,128)(2,1)S(1)} %collective-permute-done.6.refs_2_, ...), custom_call_target="tpu_custom_call" | custom-call | tf_op jit(solution)/shard_map/pallas_call | solution.py:475
  20.3 11.3 %all_to_all.5.recv_ref = f32[16,16,128]{2,1,0:T(8,128)S(1)} all-to-all(f32[16,16,128]{2,1,0:T(8,128)S(1)} %bitcast.5), channel_id=1, replica_groups={{0,2,4,6,8,10,12,14,17,19,21,23,25,27,29,31},{1,3,5,7,9,11,13,15,16,18,..., dimensions={0} | all-to-all | bytes 262144 | tf_op jit(solution)/shard_map/all_to_all | solution.py:523
  31.7 1.5 %collective-permute-start.7 = (f32[16,16,128]{2,1,0:T(8,128)S(1)}, f32[16,16,128]{2,1,0:T(8,128)S(1)}, u32[]{:S(2)}, u32[]{:S(2)}) collective-permute-start(f32[16,16,128]{2,1,0:T(8,128)S(1)} %all_to_all.5.recv_ref), channel_id=1, source_target_pairs={{0,1},{1,0},{2,3},{3,2},{4,5},{5,4},{6,7},{7,6},{8,9},{9,8},{10,11... | collective-permute-start | bytes 393224 | tf_op jit(solution)/shard_map/ppermute | solution.py:486
  33.1 0.9 %shard_map.81.sum_ref = f32[80,1024]{1,0:T(8,128)S(1)} custom-call(f32[16,16,128]{2,1,0:T(8,128)S(1)} %all_to_all.5.recv_ref), custom_call_target="tpu_custom_call" | custom-call | tf_op jit(solution)/shard_map/pallas_call | solution.py:475
  34.0 0.1 collective-permute-done.7.recv_ref
  34.1 1.6 %shard_map.82 = (f32[64,1024]{1,0:T(8,128)}, f32[3,4,256]{2,1,0:T(4,128)}) custom-call(f32[16,16,128]{2,1,0:T(8,128)S(1)} %collective-permute-done.7.recv_ref, f32[80,1024]{1,0:T(8,128)S(1)} %shard_map.81.sum_ref, f32[3,8,128]{2,1,0:T(8,128)S(1)} %get-tuple-element.25.spread_ref), custom_call_target="tpu_custom_call" | custom-call | tf_op jit(solution)/shard_map/pallas_call | solution.py:475
  (1 shorter events, 0.0 us)
Async XLA Ops:
  0.6 7.1 %copy-start.4 = (s32[4]{0:T(128)S(1)}, s32[4]{0:T(128)}, u32[]{:S(2)}) copy-start(s32[4]{0:T(128)} %cam_index_ref.1) | copy-start | bytes 52
  0.6 7.1 %copy-start.3 = (s32[4]{0:T(128)S(1)}, s32[4]{0:T(128)}, u32[]{:S(2)}) copy-start(s32[4]{0:T(128)} %tile_pos_ref.1) | copy-start | bytes 52
  0.7 9.9 %collective-permute-start.3 = (bf16[64,1024]{1,0:T(8,128)(2,1)}, bf16[64,1024]{1,0:T(8,128)(2,1)S(1)}, u32[]{:S(2)}, u32[]{:S(2)}) collective-permute-start(bf16[64,1024]{1,0:T(8,128)(2,1)} %params_ref.1), channel_id=1, source_target_pairs={{0,4},{4,0},{8,12},{12,8},{16,20},{20,16},{24,28},{28,24},{1,5},{5... | collective-permute-start | bytes 393224 | tf_op jit(solution)/shard_map/ppermute | solution.py:486
  3.7 6.5 %collective-permute-start.2 = (s32[4,128]{1,0:T(4,128)}, s32[4,128]{1,0:T(4,128)S(1)}, u32[]{:S(2)}, u32[]{:S(2)}) collective-permute-start(s32[4,128]{1,0:T(4,128)} %refs_4_.1), channel_id=1, source_target_pairs={{0,25},{1,24},{2,27},{3,26},{4,29},{5,28},{6,31},{7,30},{8,17},{9,... | collective-permute-start | bytes 6152 | tf_op jit(solution)/shard_map/ppermute | solution.py:503
  6.4 4.1 %collective-permute-start.1 = (s32[4,128]{1,0:T(4,128)}, s32[4,128]{1,0:T(4,128)S(1)}, u32[]{:S(2)}, u32[]{:S(2)}) collective-permute-start(s32[4,128]{1,0:T(4,128)} %refs_4_.1), channel_id=1, source_target_pairs={{0,17},{1,16},{2,19},{3,18},{4,21},{5,20},{6,23},{7,22},{8,25},{9,... | collective-permute-start | bytes 6152 | tf_op jit(solution)/shard_map/ppermute | solution.py:503
  6.4 4.1 %collective-permute-start = (s32[4,128]{1,0:T(4,128)}, s32[4,128]{1,0:T(4,128)S(1)}, u32[]{:S(2)}, u32[]{:S(2)}) collective-permute-start(s32[4,128]{1,0:T(4,128)} %refs_4_.1), channel_id=1, source_target_pairs={{0,8},{1,9},{2,10},{3,11},{4,12},{5,13},{6,14},{7,15},{8,0},{9,1},... | collective-permute-start | bytes 6152 | tf_op jit(solution)/shard_map/ppermute | solution.py:503
  7.8 0.9 %copy-start = (bf16[64,1024]{1,0:T(8,128)(2,1)S(1)}, bf16[64,1024]{1,0:T(8,128)(2,1)}, u32[]{:S(2)}) copy-start(bf16[64,1024]{1,0:T(8,128)(2,1)} %params_ref.1) | copy-start | bytes 393220
  8.7 0.7 %copy-start.2 = (f32[28,16]{0,1:T(8,128)S(1)}, f32[28,16]{0,1:T(8,128)}, u32[]{:S(2)}) copy-start(f32[28,16]{0,1:T(8,128)} %param.10) | copy-start | bytes 5380
  9.4 1.2 %copy-start.1 = (s32[4,128]{1,0:T(4,128)S(1)}, s32[4,128]{1,0:T(4,128)}, u32[]{:S(2)}) copy-start(s32[4,128]{1,0:T(4,128)} %refs_4_.1) | copy-start | bytes 6148
  10.5 5.1 %copy-start.5 = (f32[3,4,256]{2,1,0:T(4,128)S(1)}, f32[3,4,256]{2,1,0:T(4,128)}, u32[]{:S(2)}) copy-start(f32[3,4,256]{2,1,0:T(4,128)} %param.11) | copy-start | bytes 36868
  11.5 5.1 %collective-permute-start.4 = (bf16[64,128]{1,0:T(8,128)(2,1)S(1)}, bf16[64,128]{1,0:T(8,128)(2,1)S(1)}, u32[]{:S(2)}, u32[]{:S(2)}) collective-permute-start(bf16[64,128]{1,0:T(8,128)(2,1)S(1)} %get-tuple-element.16), channel_id=1, source_target_pairs={{0,25},{1,24},{2,27},{3,26},{4,29},{5,28},{6,31},{7,30},{8,17},{9,... | collective-permute-start | bytes 49160 | tf_op jit(solution)/shard_map/ppermute | solution.py:503
  13.7 4.2 %collective-permute-start.5 = (bf16[64,128]{1,0:T(8,128)(2,1)S(1)}, bf16[64,128]{1,0:T(8,128)(2,1)S(1)}, u32[]{:S(2)}, u32[]{:S(2)}) collective-permute-start(bf16[64,128]{1,0:T(8,128)(2,1)S(1)} %get-tuple-element.17), channel_id=1, source_target_pairs={{0,17},{1,16},{2,19},{3,18},{4,21},{5,20},{6,23},{7,22},{8,25},{9,... | collective-permute-start | bytes 49160 | tf_op jit(solution)/shard_map/ppermute | solution.py:503
  13.8 4.1 %collective-permute-start.6 = (bf16[64,128]{1,0:T(8,128)(2,1)S(1)}, bf16[64,128]{1,0:T(8,128)(2,1)S(1)}, u32[]{:S(2)}, u32[]{:S(2)}) collective-permute-start(bf16[64,128]{1,0:T(8,128)(2,1)S(1)} %get-tuple-element.18), channel_id=1, source_target_pairs={{0,8},{1,9},{2,10},{3,11},{4,12},{5,13},{6,14},{7,15},{8,0},{9,1},... | collective-permute-start | bytes 49160 | tf_op jit(solution)/shard_map/ppermute | solution.py:503
  31.7 2.4 %collective-permute-start.7 = (f32[16,16,128]{2,1,0:T(8,128)S(1)}, f32[16,16,128]{2,1,0:T(8,128)S(1)}, u32[]{:S(2)}, u32[]{:S(2)}) collective-permute-start(f32[16,16,128]{2,1,0:T(8,128)S(1)} %all_to_all.5.recv_ref), channel_id=1, source_target_pairs={{0,1},{1,0},{2,3},{3,2},{4,5},{5,4},{6,7},{7,6},{8,9},{9,8},{10,11... | collective-permute-start | bytes 393224 | tf_op jit(solution)/shard_map/ppermute | solution.py:486

commit v6 on v5

--- a/solution.py
+++ b/solution.py
@@ -151,32 +151,29 @@
     picked_ref[...] = dot(hot, wide, 1, 1).astype(BF16)
 
 
-def pick_pair_kernel(cap, peers, *refs):
-    lists_refs, refs = refs[:peers], refs[peers:]
-    own_ref, other_ref = refs[:2]
-    picked_refs, refs = refs[2 : 2 + peers], refs[2 + peers :]
-    lists_scratch, picked_scratch = refs
-    tiles, length = lists_refs[0].shape
+def pick_near_kernel(
+    cap,
+    far_lists_ref,
+    third_ref,
+    second_ref,
+    first_ref,
+    own_ref,
+    lists_ref,
+    answer_ref,
+    far_answer_ref,
+    scratch,
+):
+    tiles, _ = lists_ref.shape
     g_dev = own_ref.shape[1]
     me = lax.axis_index("gauss")
-    first = me % 2 == 0
-    for k in range(peers):
-        lists_scratch[(me // 2) ^ k] = lists_refs[k][...]
-    ids = lists_scratch[...].reshape(peers * tiles, length)
-    where_own = find(ids, me * g_dev, tiles, cap, g_dev)
-    where_other = find(ids, (me ^ 1) * g_dev, tiles, cap, g_dev)
-    lanes = iota((peers * cap, g_dev), 1)
-    of_own = dot(own_ref[...], one_hot(where_own == lanes), 1, 1)
-    of_other = dot(other_ref[...], one_hot(where_other == lanes), 1, 1)
-    of_even = jnp.where(first, of_own, of_other)
-    of_odd = jnp.where(first, of_other, of_own)
-    for p in range(peers):
-        block = slice(p * cap, (p + 1) * cap)
-        picked_scratch[p] = jnp.concatenate(
-            [of_even[:, block], of_odd[:, block]], axis=1
-        ).astype(BF16)
-    for k in range(peers):
-        picked_refs[peers - 1 - k][...] = picked_scratch[(me // 2) ^ k]
+    ids = jnp.concatenate([lists_ref[...], far_lists_ref[...]], axis=0)
+    near = [own_ref, first_ref, second_ref, third_ref]
+    lanes = iota((2 * cap, g_dev), 1)
+    for r in range(4):
+        where = find(ids, (me ^ r) * g_dev, tiles, cap, g_dev)
+        scratch[(me % 4) ^ r] = dot(near[r][...], one_hot(where == lanes), 1, 1)
+    for ref, block in ((answer_ref, slice(0, cap)), (far_answer_ref, slice(cap, 2 * cap))):
+        ref[...] = jnp.concatenate([scratch[n][:, block] for n in range(4)], axis=1).astype(BF16)
 
 
 def by_tile(values, row):
@@ -237,11 +234,9 @@
     if pieces == 1:
         listed = dot(recv_refs[0][...].reshape(-1, LANES), hot, 0, 0)[:width]
     else:
-        (recv_scratch,) = refs[13:]
-        place = lax.axis_index("gauss") // 2
-        for k in range(pieces):
-            recv_scratch[place ^ k] = recv_refs[pieces - 1 - k][...]
-        received = jnp.concatenate([recv_scratch[p] for p in range(pieces)], axis=1)
+        own, far = recv_refs[0][...], recv_refs[1][...]
+        low = lax.axis_index("gauss") < 4
+        received = jnp.concatenate([jnp.where(low, own, far), jnp.where(low, far, own)], axis=1)
         listed = dot(received, hot)
     for t in range(tiles):
         rows_ref[t * width : (t + 1) * width, :] = listed[:, t * length : (t + 1) * length]
@@ -490,18 +485,15 @@
     return int(owner >= owners // 2)
 
 
-def far_first(blocks):
+def reach(x, step):
     owners, views = lax.axis_size("gauss"), lax.axis_size("view")
-    last = len(blocks) - 1
-    out = []
-    for i, block in enumerate(blocks):
-        k = 2 * (last - i)
-        pairs = []
-        for g in range(owners):
-            flip = crossed(g, owners) ^ crossed(g ^ k, owners) if views % 2 == 0 else 0
-            pairs += [(g * views + v, (g ^ k) * views + (v ^ flip)) for v in range(views)]
-        out.append(lax.ppermute(block, ("gauss", "view"), pairs) if k else block)
-    return out
+    flip = int(step > 1)
+    pairs = [
+        (g * views + v, (g ^ step) * views + (v ^ flip))
+        for g in range(owners)
+        for v in range(views)
+    ]
+    return lax.ppermute(x, ("gauss", "view"), pairs)
 
 
 def exchange(x):
@@ -528,10 +520,6 @@
         axis_index_groups=groups,
         tiled=True,
     )
-
-
-def power_of_two(n):
-    return n & (n - 1) == 0
 
 
 def shape(dims, dtype):
@@ -547,13 +535,12 @@
     slots = owners * cap
     share = LANES // tiles
     depth = SIDE * SIDE // share
-    paired = 2 <= owners <= 16 and power_of_two(owners) and LANES == 2 * width
-    peers = owners // 2 if paired else 1
+    near = owners == 8 and views % 2 == 0
     wide = views % 2 == 0 and owners * views <= 32
 
-    if paired:
-        other = swap(params, "gauss", 1)
-        all_lists = far_first([lists] * peers)
+    if near:
+        third, second, first = [reach(params, step) for step in (3, 2, 1)]
+        far_lists = reach(lists, 4)
     params_copy, cam, pixel = call(
         prepare_kernel,
         [
@@ -564,18 +551,15 @@
         (tile_pos, cam_index, cams.T, params),
         scalars=3,
     )
-    if paired:
-        picked = call(
-            functools.partial(pick_pair_kernel, cap, peers),
-            [shape((width, 2 * cap), BF16)] * peers,
-            (*all_lists[::-1], params_copy, other),
-            scratch=(
-                pltpu.VMEM((peers, tiles, length), jnp.int32),
-                pltpu.VMEM((peers, width, 2 * cap), BF16),
-            ),
+    if near:
+        answer, far_answer = call(
+            functools.partial(pick_near_kernel, cap),
+            [shape((width, 4 * cap), BF16)] * 2,
+            (far_lists, third, second, first, params_copy, lists),
+            scratch=(pltpu.VMEM((4, width, 2 * cap), F32),),
         )
-        returned = far_first(picked)
-        after = picked[-1]
+        returned = [answer, reach(far_answer, 4)]
+        after = answer
     else:
         all_lists = exchange(jnp.broadcast_to(lists[None], (owners, tiles, length)))
         picked = call(
@@ -597,7 +581,7 @@
     copies = views // 2 if wide else 1
     high = SENT * cap // LANES
     pictures, sent = call(
-        functools.partial(render_kernel, peers, width),
+        functools.partial(render_kernel, len(returned), width),
         [shape((3, depth, LANES), F32), shape((owners, copies, high, LANES), F32)],
         (*returned, lists, hot, local, cam, pixel, spread_targets),
         scratch=(
@@ -606,7 +590,6 @@
             pltpu.VMEM((length * depth, LANES), F32),
             pltpu.VMEM((length * depth, LANES), F32),
             pltpu.VMEM((6, length * depth, LANES), F32),
-            pltpu.VMEM((peers, *returned[0].shape[-2:]), BF16),
         ),
     )
     if wide:

time: 36 us -> 37.4 us (1.039)
  waiting for transfers between devices: 2.1 us -> 6.07 us
  starting transfers between devices: 12.7 us -> 9.6 us
  Pallas kernels: 7.02 us -> 7.4 us
    ppermute x6 -> x5, waiting for transfers between devices: 2.04 us -> 6.01 us  [reach(): return lax.ppermute(x, ('gauss', 'view'), pairs)]
    ppermute x2 -> x1, starting transfers between devices: 4.45 us -> 1.51 us  [swap(): lax.ppermute(x, axis, [(i, i ^ k) for i in range(lax.axis_size(axis))])]
    pallas_call x6, Pallas kernels: 7.02 us -> 7.4 us  [call(): pl.pallas_call(kernel, out_shape=out_shape, in_specs=in_specs, out_specs=...]
    ppermute x6 -> x5, starting transfers between devices: 8.28 us -> 8.1 us  [reach(): return lax.ppermute(x, ('gauss', 'view'), pairs)]
  transfers between devices with their start and end apart: 8 -> 6, of which waited for: 4 -> 5; matrix products, arithmetic and copies ran while one was open for 1% -> 0% of each run, Pallas kernels for 6% -> 5%
where the time goes in v6:
time: 37.4 us; the launch traced here: 37.2 us
  blocking collectives  11.6 us (31%)
  starting transfers between devices  9.6 us (26%)
  Pallas kernels  7.4 us (20%)
  waiting for transfers between devices  6.07 us (16%)
  local copies, waits for them, and re-layouts  1.8 us (5%)
  between operations  0.7 us (2%)
    all_to_all x1, blocking collectives, exchange_wide(): lax.all_to_all(blocks, ('gauss', 'view'), split_axis=0, concat_axis=0, ax...  11.6 us
    ppermute x5, starting transfers between devices, reach(): return lax.ppermute(x, ('gauss', 'view'), pairs)  8.1 us
    pallas_call x6, Pallas kernels, call(): pl.pallas_call(kernel, out_shape=out_shape, in_specs=in_specs, out_specs=...  7.4 us
    ppermute x5, waiting for transfers between devices, reach(): return lax.ppermute(x, ('gauss', 'view'), pairs)  6.01 us
    unnamed x12, local copies, waits for them, and re-layouts  1.62 us
    ppermute x1, starting transfers between devices, swap(): lax.ppermute(x, axis, [(i, i ^ k) for i in range(lax.axis_size(axis))])  1.51 us
  transfers between devices with their start and end apart: 6, of which 5 were waited for; matrix products, arithmetic and copies ran while one was open for 0% of the time, Pallas kernels for 5%

profile of v6, /device:TPU:0, one launch (start us, length us, event | category | flops | bytes accessed | tf_op | source)
XLA Modules:
  0.0 37.2 jit_solution(15310260490045031491)
XLA Ops:
  0.6 0.0 copy-start.4
  0.6 0.0 copy-start.3
  0.7 2.5 %collective-permute-start.2 = (bf16[64,1024]{1,0:T(8,128)(2,1)}, bf16[64,1024]{1,0:T(8,128)(2,1)S(1)}, u32[]{:S(2)}, u32[]{:S(2)}) collective-permute-start(bf16[64,1024]{1,0:T(8,128)(2,1)} %params_ref.1), channel_id=1, source_target_pairs={{0,9},{1,8},{2,11},{3,10},{4,13},{5,12},{6,15},{7,14},{8,1},{9,0},... | collective-permute-start | bytes 393224 | tf_op jit(solution)/shard_map/ppermute | solution.py:496
  3.2 1.7 %collective-permute-start.1 = (bf16[64,1024]{1,0:T(8,128)(2,1)}, bf16[64,1024]{1,0:T(8,128)(2,1)S(1)}, u32[]{:S(2)}, u32[]{:S(2)}) collective-permute-start(bf16[64,1024]{1,0:T(8,128)(2,1)} %params_ref.1), channel_id=1, source_target_pairs={{0,13},{1,12},{2,15},{3,14},{4,9},{5,8},{6,11},{7,10},{8,5},{9,4},... | collective-permute-start | bytes 393224 | tf_op jit(solution)/shard_map/ppermute | solution.py:496
  4.8 0.0 collective-permute-start.3
  4.8 2.5 %collective-permute-start = (s32[4,128]{1,0:T(4,128)}, s32[4,128]{1,0:T(4,128)S(1)}, u32[]{:S(2)}, u32[]{:S(2)}) collective-permute-start(s32[4,128]{1,0:T(4,128)} %refs_2_.1), channel_id=1, source_target_pairs={{0,17},{1,16},{2,19},{3,18},{4,21},{5,20},{6,23},{7,22},{8,25},{9,... | collective-permute-start | bytes 6152 | tf_op jit(solution)/shard_map/ppermute | solution.py:496
  7.3 0.0 copy-done.4
  7.3 0.0 copy-done.3
  7.3 0.0 copy-start
  7.3 0.9 %copy-done = bf16[64,1024]{1,0:T(8,128)(2,1)S(1)} copy-done((bf16[64,1024]{1,0:T(8,128)(2,1)S(1)}, bf16[64,1024]{1,0:T(8,128)(2,1)}, u32[]{:S(2)}) %copy-start) | copy-done | bytes 131096
  8.2 0.0 copy-start.2
  8.2 0.7 %copy-done.2 = f32[28,16]{0,1:T(8,128)S(1)} copy-done((f32[28,16]{0,1:T(8,128)S(1)}, f32[28,16]{0,1:T(8,128)}, u32[]{:S(2)}) %copy-start.2) | copy-done | bytes 1816
  8.9 0.0 copy-start.1
  8.9 0.8 %shard_map.77 = (bf16[64,1024]{1,0:T(8,128)(2,1)S(1)}, f32[28,4,128]{2,1,0:T(4,128)S(1)}, f32[2,8,128]{2,1,0:T(8,128)S(1)}) custom-call(s32[4]{0:T(128)S(1)} %copy-done.3, s32[4]{0:T(128)S(1)} %copy-done.4, f32[16,28]{1,0:T(8,128)S(1)} %bitcast.6, bf16[64,1024]{1,0:T(8,128)(2,1)S(1)} %copy-done), custom_call_target="tpu_custom_call" | custom-call | tf_op jit(solution)/shard_map/pallas_call | solution.py:470
  9.7 0.5 %collective-permute-done.far_lists_ref = s32[4,128]{1,0:T(4,128)S(1)} collective-permute-done((s32[4,128]{1,0:T(4,128)}, s32[4,128]{1,0:T(4,128)S(1)}, u32[]{:S(2)}, u32[]{:S(2)}) %collective-permute-start) | collective-permute-done | bytes 2080 | tf_op jit(solution)/shard_map/ppermute | solution.py:496
  10.2 0.0 collective-permute-done.2.second_ref
  10.2 1.7 %collective-permute-done.1.third_ref = bf16[64,1024]{1,0:T(8,128)(2,1)S(1)} collective-permute-done((bf16[64,1024]{1,0:T(8,128)(2,1)}, bf16[64,1024]{1,0:T(8,128)(2,1)S(1)}, u32[]{:S(2)}, u32[]{:S(2)}) %collective-permute-start.1) | collective-permute-done | bytes 131104 | tf_op jit(solution)/shard_map/ppermute | solution.py:496
  11.9 1.4 %collective-permute-done.3.first_ref = bf16[64,1024]{1,0:T(8,128)(2,1)S(1)} collective-permute-done((bf16[64,1024]{1,0:T(8,128)(2,1)}, bf16[64,1024]{1,0:T(8,128)(2,1)S(1)}, u32[]{:S(2)}, u32[]{:S(2)}) %collective-permute-start.3) | collective-permute-done | bytes 131104 | tf_op jit(solution)/shard_map/ppermute | solution.py:496
  13.3 0.0 copy-done.1
  13.3 0.0 copy-start.5
  13.3 1.3 %shard_map.78 = (bf16[64,256]{1,0:T(8,128)(2,1)S(1)}, bf16[64,256]{1,0:T(8,128)(2,1)S(1)}) custom-call(s32[4,128]{1,0:T(4,128)S(1)} %collective-permute-done.far_lists_ref, bf16[64,1024]{1,0:T(8,128)(2,1)S(1)} %collective-permute-done.1.third_ref, bf16[64,1024]{1,0:T(8,128)(2,1)S(1)} %collective-permute-done.2.second_ref, ...), custom_call_target="tpu_custom_call" | custom-call | tf_op jit(solution)/shard_map/pallas_call | solution.py:470
  14.6 1.4 %collective-permute-start.4 = (bf16[64,256]{1,0:T(8,128)(2,1)S(1)}, bf16[64,256]{1,0:T(8,128)(2,1)S(1)}, u32[]{:S(2)}, u32[]{:S(2)}) collective-permute-start(bf16[64,256]{1,0:T(8,128)(2,1)S(1)} %get-tuple-element.15), channel_id=1, source_target_pairs={{0,17},{1,16},{2,19},{3,18},{4,21},{5,20},{6,23},{7,22},{8,25},{9,... | collective-permute-start | bytes 98312 | tf_op jit(solution)/shard_map/ppermute | solution.py:496
  16.1 0.0 copy-done.5
  16.1 0.1 reshape.13
  16.2 0.1 reshape.14.refs_7_
  16.3 0.4 shard_map.79
  16.6 2.4 %collective-permute-done.4.refs_1_ = bf16[64,256]{1,0:T(8,128)(2,1)S(1)} collective-permute-done((bf16[64,256]{1,0:T(8,128)(2,1)S(1)}, bf16[64,256]{1,0:T(8,128)(2,1)S(1)}, u32[]{:S(2)}, u32[]{:S(2)}) %collective-permute-start.4) | collective-permute-done | bytes 32800 | tf_op jit(solution)/shard_map/ppermute | solution.py:496
  19.0 2.4 %shard_map.80 = (f32[3,8,128]{2,1,0:T(8,128)S(1)}, f32[8,2,16,128]{3,2,1,0:T(8,128)S(1)}) custom-call(bf16[64,256]{1,0:T(8,128)(2,1)S(1)} %get-tuple-element.14.after_ref.refs_0_, bf16[64,256]{1,0:T(8,128)(2,1)S(1)} %collective-permute-done.4.refs_1_, s32[4,128]{1,0:T(4,128)S(1)} %copy-done.1, bf16[512,512]{1,0:T(8,128)(2,1)S(1)} %get-tuple-element.16.refs_3_, ...), custom_call_target="tpu_custom_call" | custom-call | tf_op jit(solution)/shard_map/pallas_call | solution.py:470
  21.5 11.6 %all_to_all.5.recv_ref = f32[16,16,128]{2,1,0:T(8,128)S(1)} all-to-all(f32[16,16,128]{2,1,0:T(8,128)S(1)} %bitcast.5), channel_id=1, replica_groups={{0,2,4,6,8,10,12,14,17,19,21,23,25,27,29,31},{1,3,5,7,9,11,13,15,16,18,..., dimensions={0} | all-to-all | bytes 262144 | tf_op jit(solution)/shard_map/all_to_all | solution.py:515
  33.1 1.5 %collective-permute-start.5 = (f32[16,16,128]{2,1,0:T(8,128)S(1)}, f32[16,16,128]{2,1,0:T(8,128)S(1)}, u32[]{:S(2)}, u32[]{:S(2)}) collective-permute-start(f32[16,16,128]{2,1,0:T(8,128)S(1)} %all_to_all.5.recv_ref), channel_id=1, source_target_pairs={{0,1},{1,0},{2,3},{3,2},{4,5},{5,4},{6,7},{7,6},{8,9},{9,8},{10,11... | collective-permute-start | bytes 393224 | tf_op jit(solution)/shard_map/ppermute | solution.py:481
  34.6 0.9 %shard_map.81.sum_ref = f32[80,1024]{1,0:T(8,128)S(1)} custom-call(f32[16,16,128]{2,1,0:T(8,128)S(1)} %all_to_all.5.recv_ref), custom_call_target="tpu_custom_call" | custom-call | tf_op jit(solution)/shard_map/pallas_call | solution.py:470
  35.5 0.1 collective-permute-done.5.recv_ref
  35.6 1.6 %shard_map.82 = (f32[64,1024]{1,0:T(8,128)}, f32[3,4,256]{2,1,0:T(4,128)}) custom-call(f32[16,16,128]{2,1,0:T(8,128)S(1)} %collective-permute-done.5.recv_ref, f32[80,1024]{1,0:T(8,128)S(1)} %shard_map.81.sum_ref, f32[3,8,128]{2,1,0:T(8,128)S(1)} %get-tuple-element.21.spread_ref), custom_call_target="tpu_custom_call" | custom-call | tf_op jit(solution)/shard_map/pallas_call | solution.py:470
  (1 shorter events, 0.0 us)
Async XLA Ops:
  0.6 6.7 %copy-start.4 = (s32[4]{0:T(128)S(1)}, s32[4]{0:T(128)}, u32[]{:S(2)}) copy-start(s32[4]{0:T(128)} %cam_index_ref.1) | copy-start | bytes 52
  0.6 6.7 %copy-start.3 = (s32[4]{0:T(128)S(1)}, s32[4]{0:T(128)}, u32[]{:S(2)}) copy-start(s32[4]{0:T(128)} %tile_pos_ref.1) | copy-start | bytes 52
  0.7 9.6 %collective-permute-start.2 = (bf16[64,1024]{1,0:T(8,128)(2,1)}, bf16[64,1024]{1,0:T(8,128)(2,1)S(1)}, u32[]{:S(2)}, u32[]{:S(2)}) collective-permute-start(bf16[64,1024]{1,0:T(8,128)(2,1)} %params_ref.1), channel_id=1, source_target_pairs={{0,9},{1,8},{2,11},{3,10},{4,13},{5,12},{6,15},{7,14},{8,1},{9,0},... | collective-permute-start | bytes 393224 | tf_op jit(solution)/shard_map/ppermute | solution.py:496
  3.2 8.7 %collective-permute-start.1 = (bf16[64,1024]{1,0:T(8,128)(2,1)}, bf16[64,1024]{1,0:T(8,128)(2,1)S(1)}, u32[]{:S(2)}, u32[]{:S(2)}) collective-permute-start(bf16[64,1024]{1,0:T(8,128)(2,1)} %params_ref.1), channel_id=1, source_target_pairs={{0,13},{1,12},{2,15},{3,14},{4,9},{5,8},{6,11},{7,10},{8,5},{9,4},... | collective-permute-start | bytes 393224 | tf_op jit(solution)/shard_map/ppermute | solution.py:496
  4.8 8.4 %collective-permute-start.3 = (bf16[64,1024]{1,0:T(8,128)(2,1)}, bf16[64,1024]{1,0:T(8,128)(2,1)S(1)}, u32[]{:S(2)}, u32[]{:S(2)}) collective-permute-start(bf16[64,1024]{1,0:T(8,128)(2,1)} %params_ref.1), channel_id=1, source_target_pairs={{0,4},{1,5},{2,6},{3,7},{4,0},{5,1},{6,2},{7,3},{8,12},{9,13},{10,... | collective-permute-start | bytes 393224 | tf_op jit(solution)/shard_map/ppermute | solution.py:496
  4.8 5.4 %collective-permute-start = (s32[4,128]{1,0:T(4,128)}, s32[4,128]{1,0:T(4,128)S(1)}, u32[]{:S(2)}, u32[]{:S(2)}) collective-permute-start(s32[4,128]{1,0:T(4,128)} %refs_2_.1), channel_id=1, source_target_pairs={{0,17},{1,16},{2,19},{3,18},{4,21},{5,20},{6,23},{7,22},{8,25},{9,... | collective-permute-start | bytes 6152 | tf_op jit(solution)/shard_map/ppermute | solution.py:496
  7.3 0.9 %copy-start = (bf16[64,1024]{1,0:T(8,128)(2,1)S(1)}, bf16[64,1024]{1,0:T(8,128)(2,1)}, u32[]{:S(2)}) copy-start(bf16[64,1024]{1,0:T(8,128)(2,1)} %params_ref.1) | copy-start | bytes 393220
  8.2 0.7 %copy-start.2 = (f32[28,16]{0,1:T(8,128)S(1)}, f32[28,16]{0,1:T(8,128)}, u32[]{:S(2)}) copy-start(f32[28,16]{0,1:T(8,128)} %param.10) | copy-start | bytes 5380
  8.9 4.4 %copy-start.1 = (s32[4,128]{1,0:T(4,128)S(1)}, s32[4,128]{1,0:T(4,128)}, u32[]{:S(2)}) copy-start(s32[4,128]{1,0:T(4,128)} %refs_2_.1) | copy-start | bytes 6148
  13.3 2.8 %copy-start.5 = (f32[3,4,256]{2,1,0:T(4,128)S(1)}, f32[3,4,256]{2,1,0:T(4,128)}, u32[]{:S(2)}) copy-start(f32[3,4,256]{2,1,0:T(4,128)} %param.11) | copy-start | bytes 36868
  14.6 4.4 %collective-permute-start.4 = (bf16[64,256]{1,0:T(8,128)(2,1)S(1)}, bf16[64,256]{1,0:T(8,128)(2,1)S(1)}, u32[]{:S(2)}, u32[]{:S(2)}) collective-permute-start(bf16[64,256]{1,0:T(8,128)(2,1)S(1)} %get-tuple-element.15), channel_id=1, source_target_pairs={{0,17},{1,16},{2,19},{3,18},{4,21},{5,20},{6,23},{7,22},{8,25},{9,... | collective-permute-start | bytes 98312 | tf_op jit(solution)/shard_map/ppermute | solution.py:496
  33.1 2.5 %collective-permute-start.5 = (f32[16,16,128]{2,1,0:T(8,128)S(1)}, f32[16,16,128]{2,1,0:T(8,128)S(1)}, u32[]{:S(2)}, u32[]{:S(2)}) collective-permute-start(f32[16,16,128]{2,1,0:T(8,128)S(1)} %all_to_all.5.recv_ref), channel_id=1, source_target_pairs={{0,1},{1,0},{2,3},{3,2},{4,5},{5,4},{6,7},{7,6},{8,9},{9,8},{10,11... | collective-permute-start | bytes 393224 | tf_op jit(solution)/shard_map/ppermute | solution.py:481

commit v7 on v6

--- a/solution.py
+++ b/solution.py
@@ -128,11 +128,10 @@
     return dot(jnp.concatenate(shifted, axis=1).astype(BF16), counted).astype(jnp.int32)
 
 
-def find(ids, base, tiles, cap, g_dev):
-    local = ids - base
+def find(local, tiles, cap, g_dev):
     mine = (local >= 0) & (local < g_dev)
     key = jnp.where(mine, ranks(mine, tiles), -1)
-    rows, length = ids.shape
+    rows, length = local.shape
     slot = iota((cap, length), 0)
     found = []
     for r in range(0, rows, tiles):
@@ -145,7 +144,7 @@
 
 def pick_kernel(tiles, cap, lists_ref, params_ref, picked_ref):
     width, g_dev = params_ref.shape
-    where = find(lists_ref[...], lax.axis_index("gauss") * g_dev, tiles, cap, g_dev)
+    where = find(lists_ref[...] - lax.axis_index("gauss") * g_dev, tiles, cap, g_dev)
     hot = one_hot(where == iota((where.shape[0], g_dev), 1))
     wide = jnp.concatenate([params_ref[...], jnp.zeros((LANES - width, g_dev), BF16)], axis=0)
     picked_ref[...] = dot(hot, wide, 1, 1).astype(BF16)
@@ -154,9 +153,10 @@
 def pick_near_kernel(
     cap,
     far_lists_ref,
+    got_ref,
+    got_by_ref,
     third_ref,
-    second_ref,
-    first_ref,
+    third_by_ref,
     own_ref,
     lists_ref,
     answer_ref,
@@ -166,12 +166,21 @@
     tiles, _ = lists_ref.shape
     g_dev = own_ref.shape[1]
     me = lax.axis_index("gauss")
+    core_0 = lax.axis_index("view") % 2 == 0
     ids = jnp.concatenate([lists_ref[...], far_lists_ref[...]], axis=0)
-    near = [own_ref, first_ref, second_ref, third_ref]
+    local = jnp.concatenate([ids - (me ^ r) * g_dev for r in range(4)], axis=0)
+    where = find(local, tiles, cap, g_dev)
+    got, got_by = got_ref[...], got_by_ref[...]
+    near = [
+        own_ref[...],
+        jnp.where(core_0, got, got_by),
+        jnp.where(core_0, got_by, got),
+        jnp.where(core_0, third_by_ref[...], third_ref[...]),
+    ]
     lanes = iota((2 * cap, g_dev), 1)
     for r in range(4):
-        where = find(ids, (me ^ r) * g_dev, tiles, cap, g_dev)
-        scratch[(me % 4) ^ r] = dot(near[r][...], one_hot(where == lanes), 1, 1)
+        hot = one_hot(where[2 * r * cap : 2 * (r + 1) * cap] == lanes)
+        scratch[(me % 4) ^ r] = dot(near[r], hot, 1, 1)
     for ref, block in ((answer_ref, slice(0, cap)), (far_answer_ref, slice(cap, 2 * cap))):
         ref[...] = jnp.concatenate([scratch[n][:, block] for n in range(4)], axis=1).astype(BF16)
 
@@ -485,14 +494,15 @@
     return int(owner >= owners // 2)
 
 
-def reach(x, step):
+def reach(x, steps):
     owners, views = lax.axis_size("gauss"), lax.axis_size("view")
-    flip = int(step > 1)
-    pairs = [
-        (g * views + v, (g ^ step) * views + (v ^ flip))
-        for g in range(owners)
-        for v in range(views)
-    ]
+    pairs = []
+    for g in range(owners):
+        for v in range(views):
+            step = steps[v % 2]
+            if step is not None:
+                flip = crossed(g, owners) ^ crossed(g ^ step, owners)
+                pairs.append((g * views + v, (g ^ step) * views + (v ^ flip)))
     return lax.ppermute(x, ("gauss", "view"), pairs)
 
 
@@ -539,8 +549,9 @@
     wide = views % 2 == 0 and owners * views <= 32
 
     if near:
-        third, second, first = [reach(params, step) for step in (3, 2, 1)]
-        far_lists = reach(lists, 4)
+        third = reach(params, (None, 3))
+        got = reach(params, (1, 2))
+        far_lists = reach(lists, (4, 4))
     params_copy, cam, pixel = call(
         prepare_kernel,
         [
@@ -552,13 +563,17 @@
         scalars=3,
     )
     if near:
+        third, got, far_lists, params_copy = lax.optimization_barrier(
+            (third, got, far_lists, params_copy)
+        )
+        got_by, third_by = swap(got, "view", 1), swap(third, "view", 1)
         answer, far_answer = call(
             functools.partial(pick_near_kernel, cap),
             [shape((width, 4 * cap), BF16)] * 2,
-            (far_lists, third, second, first, params_copy, lists),
+            (far_lists, got, got_by, third, third_by, params_copy, lists),
             scratch=(pltpu.VMEM((4, width, 2 * cap), F32),),
         )
-        returned = [answer, reach(far_answer, 4)]
+        returned = [answer, reach(far_answer, (4, 4))]
         after = answer
     else:
         all_lists = exchange(jnp.broadcast_to(lists[None], (owners, tiles, length)))

time: 37.4 us -> 37.1 us (level)
  waiting for transfers between devices: 6.07 us -> 2.86 us
  blocking collectives: 11.6 us -> 13.2 us
  starting transfers between devices: 9.6 us -> 11.1 us
    ppermute x5 -> x4, waiting for transfers between devices: 6.01 us -> 1.77 us  [reach(): return lax.ppermute(x, ('gauss', 'view'), pairs)]
    ppermute x5 -> x4, starting transfers between devices: 8.1 us -> 9.96 us  [reach(): return lax.ppermute(x, ('gauss', 'view'), pairs)]
    all_to_all x1, blocking collectives: 11.6 us -> 13.2 us  [exchange_wide(): lax.all_to_all(blocks, ('gauss', 'view'), split_axis=0, concat_axis=0, ax...]
    ppermute x1 -> x3, waiting for transfers between devices: 0.06 us -> 1.09 us  [swap(): lax.ppermute(x, axis, [(i, i ^ k) for i in range(lax.axis_size(axis))])]
    ppermute x1 -> x3, starting transfers between devices: 1.51 us -> 1.18 us  [swap(): lax.ppermute(x, axis, [(i, i ^ k) for i in range(lax.axis_size(axis))])]
  transfers between devices with their start and end apart: 6 -> 7, of which waited for: 5 -> 4; matrix products, arithmetic and copies ran while one was open for 0% -> 0% of each run, Pallas kernels for 5% -> 6%
where the time goes in v7:
time: 37.1 us; the launch traced here: 36.8 us
  blocking collectives  13.2 us (36%)
  starting transfers between devices  11.1 us (30%)
  Pallas kernels  7.07 us (19%)
  waiting for transfers between devices  2.86 us (8%)
  local copies, waits for them, and re-layouts  1.8 us (5%)
  between operations  0.75 us (2%)
    all_to_all x1, blocking collectives, exchange_wide(): lax.all_to_all(blocks, ('gauss', 'view'), split_axis=0, concat_axis=0, ax...  13.2 us
    ppermute x4, starting transfers between devices, reach(): return lax.ppermute(x, ('gauss', 'view'), pairs)  9.96 us
    pallas_call x6, Pallas kernels, call(): pl.pallas_call(kernel, out_shape=out_shape, in_specs=in_specs, out_specs=...  7.07 us
    ppermute x4, waiting for transfers between devices, reach(): return lax.ppermute(x, ('gauss', 'view'), pairs)  1.77 us
    unnamed x12, local copies, waits for them, and re-layouts  1.62 us
    ppermute x3, starting transfers between devices, swap(): lax.ppermute(x, axis, [(i, i ^ k) for i in range(lax.axis_size(axis))])  1.18 us
    ppermute x3, waiting for transfers between devices, swap(): lax.ppermute(x, axis, [(i, i ^ k) for i in range(lax.axis_size(axis))])  1.09 us
  transfers between devices with their start and end apart: 7, of which 4 were waited for; matrix products, arithmetic and copies ran while one was open for 0% of the time, Pallas kernels for 6%

profile of v7, /device:TPU:0, one launch (start us, length us, event | category | flops | bytes accessed | tf_op | source)
XLA Modules:
  0.0 36.8 jit_solution(15249588049910320808)
XLA Ops:
  0.6 0.0 copy-start.4
  0.6 0.0 copy-start.3
  0.7 0.8 %collective-permute-start = (bf16[64,1024]{1,0:T(8,128)(2,1)}, bf16[64,1024]{1,0:T(8,128)(2,1)S(1)}, u32[]{:S(2)}, u32[]{:S(2)}) collective-permute-start(bf16[64,1024]{1,0:T(8,128)(2,1)} %params_ref.1), channel_id=1, source_target_pairs={{1,13},{3,15},{5,9},{7,11},{9,5},{11,7},{13,1},{15,3},{17,29},{19,... | collective-permute-start | bytes 393224 | tf_op jit(solution)/shard_map/ppermute | solution.py:506
  1.5 3.0 %collective-permute-start.1 = (bf16[64,1024]{1,0:T(8,128)(2,1)}, bf16[64,1024]{1,0:T(8,128)(2,1)S(1)}, u32[]{:S(2)}, u32[]{:S(2)}) collective-permute-start(bf16[64,1024]{1,0:T(8,128)(2,1)} %params_ref.1), channel_id=1, source_target_pairs={{0,4},{1,9},{2,6},{3,11},{4,0},{5,13},{6,2},{7,15},{8,12},{9,1},{1... | collective-permute-start | bytes 393224 | tf_op jit(solution)/shard_map/ppermute | solution.py:506
  4.5 4.2 %collective-permute-start.2 = (s32[4,128]{1,0:T(4,128)}, s32[4,128]{1,0:T(4,128)S(1)}, u32[]{:S(2)}, u32[]{:S(2)}) collective-permute-start(s32[4,128]{1,0:T(4,128)} %refs_2_.1), channel_id=1, source_target_pairs={{0,17},{1,16},{2,19},{3,18},{4,21},{5,20},{6,23},{7,22},{8,25},{9,... | collective-permute-start | bytes 6152 | tf_op jit(solution)/shard_map/ppermute | solution.py:506
  8.6 0.0 copy-done.4
  8.6 0.0 copy-done.3
  8.6 0.0 copy-start
  8.6 0.9 %copy-done = bf16[64,1024]{1,0:T(8,128)(2,1)S(1)} copy-done((bf16[64,1024]{1,0:T(8,128)(2,1)S(1)}, bf16[64,1024]{1,0:T(8,128)(2,1)}, u32[]{:S(2)}) %copy-start) | copy-done | bytes 131096
  9.5 0.0 copy-start.2
  9.5 0.7 %copy-done.2 = f32[28,16]{0,1:T(8,128)S(1)} copy-done((f32[28,16]{0,1:T(8,128)S(1)}, f32[28,16]{0,1:T(8,128)}, u32[]{:S(2)}) %copy-start.2) | copy-done | bytes 1816
  10.2 0.0 copy-start.1
  10.2 0.8 %shard_map.77 = (bf16[64,1024]{1,0:T(8,128)(2,1)S(1)}, f32[28,4,128]{2,1,0:T(4,128)S(1)}, f32[2,8,128]{2,1,0:T(8,128)S(1)}) custom-call(s32[4]{0:T(128)S(1)} %copy-done.3, s32[4]{0:T(128)S(1)} %copy-done.4, f32[16,28]{1,0:T(8,128)S(1)} %bitcast.6, bf16[64,1024]{1,0:T(8,128)(2,1)S(1)} %copy-done), custom_call_target="tpu_custom_call" | custom-call | tf_op jit(solution)/shard_map/pallas_call | solution.py:479
  11.0 0.0 collective-permute-done.2.far_lists_ref
  11.0 0.0 collective-permute-done.third_ref
  11.0 0.0 collective-permute-done.1.got_ref
  11.0 0.0 copy-start.5
  11.1 0.1 collective-permute-start.3
  11.1 0.5 %collective-permute-start.4 = (bf16[64,1024]{1,0:T(8,128)(2,1)S(1)}, bf16[64,1024]{1,0:T(8,128)(2,1)S(1)}, u32[]{:S(2)}, u32[]{:S(2)}) collective-permute-start(bf16[64,1024]{1,0:T(8,128)(2,1)S(1)} %collective-permute-done.third_ref), channel_id=1, source_target_pairs={{0,1},{1,0},{2,3},{3,2},{4,5},{5,4},{6,7},{7,6},{8,9},{9,8},{10,11... | collective-permute-start | bytes 393224 | tf_op jit(solution)/shard_map/ppermute | solution.py:490
  11.6 0.8 %collective-permute-done.3.got_by_ref = bf16[64,1024]{1,0:T(8,128)(2,1)S(1)} collective-permute-done((bf16[64,1024]{1,0:T(8,128)(2,1)S(1)}, bf16[64,1024]{1,0:T(8,128)(2,1)S(1)}, u32[]{:S(2)}, u32[]{:S(2)}) %collective-permute-start.3) | collective-permute-done | bytes 131104 | tf_op jit(solution)/shard_map/ppermute | solution.py:490
  12.5 0.2 collective-permute-done.4.third_by_ref
  12.7 0.0 copy-done.1
  12.7 1.0 %shard_map.78 = (bf16[64,256]{1,0:T(8,128)(2,1)S(1)}, bf16[64,256]{1,0:T(8,128)(2,1)S(1)}) custom-call(s32[4,128]{1,0:T(4,128)S(1)} %collective-permute-done.2.far_lists_ref, bf16[64,1024]{1,0:T(8,128)(2,1)S(1)} %collective-permute-done.1.got_ref, bf16[64,1024]{1,0:T(8,128)(2,1)S(1)} %collective-permute-done.3.got_by_ref, ...), custom_call_target="tpu_custom_call" | custom-call | tf_op jit(solution)/shard_map/pallas_call | solution.py:479
  13.7 2.0 %collective-permute-start.5 = (bf16[64,256]{1,0:T(8,128)(2,1)S(1)}, bf16[64,256]{1,0:T(8,128)(2,1)S(1)}, u32[]{:S(2)}, u32[]{:S(2)}) collective-permute-start(bf16[64,256]{1,0:T(8,128)(2,1)S(1)} %get-tuple-element.23), channel_id=1, source_target_pairs={{0,17},{1,16},{2,19},{3,18},{4,21},{5,20},{6,23},{7,22},{8,25},{9,... | collective-permute-start | bytes 98312 | tf_op jit(solution)/shard_map/ppermute | solution.py:506
  15.7 0.0 copy-done.5
  15.7 0.1 reshape.13
  15.8 0.1 reshape.14.refs_7_
  15.8 0.4 shard_map.79
  16.2 1.8 %collective-permute-done.5.refs_1_ = bf16[64,256]{1,0:T(8,128)(2,1)S(1)} collective-permute-done((bf16[64,256]{1,0:T(8,128)(2,1)S(1)}, bf16[64,256]{1,0:T(8,128)(2,1)S(1)}, u32[]{:S(2)}, u32[]{:S(2)}) %collective-permute-start.5) | collective-permute-done | bytes 32800 | tf_op jit(solution)/shard_map/ppermute | solution.py:506
  18.0 2.4 %shard_map.80 = (f32[3,8,128]{2,1,0:T(8,128)S(1)}, f32[8,2,16,128]{3,2,1,0:T(8,128)S(1)}) custom-call(bf16[64,256]{1,0:T(8,128)(2,1)S(1)} %get-tuple-element.22.after_ref.refs_0_, bf16[64,256]{1,0:T(8,128)(2,1)S(1)} %collective-permute-done.5.refs_1_, s32[4,128]{1,0:T(4,128)S(1)} %copy-done.1, bf16[512,512]{1,0:T(8,128)(2,1)S(1)} %get-tuple-element.24.refs_3_, ...), custom_call_target="tpu_custom_call" | custom-call | tf_op jit(solution)/shard_map/pallas_call | solution.py:479
  20.4 13.2 %all_to_all.5.recv_ref = f32[16,16,128]{2,1,0:T(8,128)S(1)} all-to-all(f32[16,16,128]{2,1,0:T(8,128)S(1)} %bitcast.5), channel_id=1, replica_groups={{0,2,4,6,8,10,12,14,17,19,21,23,25,27,29,31},{1,3,5,7,9,11,13,15,16,18,..., dimensions={0} | all-to-all | bytes 262144 | tf_op jit(solution)/shard_map/all_to_all | solution.py:525
  33.6 0.6 %collective-permute-start.6 = (f32[16,16,128]{2,1,0:T(8,128)S(1)}, f32[16,16,128]{2,1,0:T(8,128)S(1)}, u32[]{:S(2)}, u32[]{:S(2)}) collective-permute-start(f32[16,16,128]{2,1,0:T(8,128)S(1)} %all_to_all.5.recv_ref), channel_id=1, source_target_pairs={{0,1},{1,0},{2,3},{3,2},{4,5},{5,4},{6,7},{7,6},{8,9},{9,8},{10,11... | collective-permute-start | bytes 393224 | tf_op jit(solution)/shard_map/ppermute | solution.py:490
  34.2 0.9 %shard_map.81.sum_ref = f32[80,1024]{1,0:T(8,128)S(1)} custom-call(f32[16,16,128]{2,1,0:T(8,128)S(1)} %all_to_all.5.recv_ref), custom_call_target="tpu_custom_call" | custom-call | tf_op jit(solution)/shard_map/pallas_call | solution.py:479
  35.1 0.1 collective-permute-done.6.recv_ref
  35.2 1.6 %shard_map.82 = (f32[64,1024]{1,0:T(8,128)}, f32[3,4,256]{2,1,0:T(4,128)}) custom-call(f32[16,16,128]{2,1,0:T(8,128)S(1)} %collective-permute-done.6.recv_ref, f32[80,1024]{1,0:T(8,128)S(1)} %shard_map.81.sum_ref, f32[3,8,128]{2,1,0:T(8,128)S(1)} %get-tuple-element.29.spread_ref), custom_call_target="tpu_custom_call" | custom-call | tf_op jit(solution)/shard_map/pallas_call | solution.py:479
  (1 shorter events, 0.0 us)
Async XLA Ops:
  0.6 8.0 %copy-start.4 = (s32[4]{0:T(128)S(1)}, s32[4]{0:T(128)}, u32[]{:S(2)}) copy-start(s32[4]{0:T(128)} %cam_index_ref.1) | copy-start | bytes 52
  0.6 8.0 %copy-start.3 = (s32[4]{0:T(128)S(1)}, s32[4]{0:T(128)}, u32[]{:S(2)}) copy-start(s32[4]{0:T(128)} %tile_pos_ref.1) | copy-start | bytes 52
  0.7 10.4 %collective-permute-start = (bf16[64,1024]{1,0:T(8,128)(2,1)}, bf16[64,1024]{1,0:T(8,128)(2,1)S(1)}, u32[]{:S(2)}, u32[]{:S(2)}) collective-permute-start(bf16[64,1024]{1,0:T(8,128)(2,1)} %params_ref.1), channel_id=1, source_target_pairs={{1,13},{3,15},{5,9},{7,11},{9,5},{11,7},{13,1},{15,3},{17,29},{19,... | collective-permute-start | bytes 393224 | tf_op jit(solution)/shard_map/ppermute | solution.py:506
  1.5 9.6 %collective-permute-start.1 = (bf16[64,1024]{1,0:T(8,128)(2,1)}, bf16[64,1024]{1,0:T(8,128)(2,1)S(1)}, u32[]{:S(2)}, u32[]{:S(2)}) collective-permute-start(bf16[64,1024]{1,0:T(8,128)(2,1)} %params_ref.1), channel_id=1, source_target_pairs={{0,4},{1,9},{2,6},{3,11},{4,0},{5,13},{6,2},{7,15},{8,12},{9,1},{1... | collective-permute-start | bytes 393224 | tf_op jit(solution)/shard_map/ppermute | solution.py:506
  4.5 6.6 %collective-permute-start.2 = (s32[4,128]{1,0:T(4,128)}, s32[4,128]{1,0:T(4,128)S(1)}, u32[]{:S(2)}, u32[]{:S(2)}) collective-permute-start(s32[4,128]{1,0:T(4,128)} %refs_2_.1), channel_id=1, source_target_pairs={{0,17},{1,16},{2,19},{3,18},{4,21},{5,20},{6,23},{7,22},{8,25},{9,... | collective-permute-start | bytes 6152 | tf_op jit(solution)/shard_map/ppermute | solution.py:506
  8.6 0.9 %copy-start = (bf16[64,1024]{1,0:T(8,128)(2,1)S(1)}, bf16[64,1024]{1,0:T(8,128)(2,1)}, u32[]{:S(2)}) copy-start(bf16[64,1024]{1,0:T(8,128)(2,1)} %params_ref.1) | copy-start | bytes 393220
  9.5 0.7 %copy-start.2 = (f32[28,16]{0,1:T(8,128)S(1)}, f32[28,16]{0,1:T(8,128)}, u32[]{:S(2)}) copy-start(f32[28,16]{0,1:T(8,128)} %param.10) | copy-start | bytes 5380
  10.2 2.4 %copy-start.1 = (s32[4,128]{1,0:T(4,128)S(1)}, s32[4,128]{1,0:T(4,128)}, u32[]{:S(2)}) copy-start(s32[4,128]{1,0:T(4,128)} %refs_2_.1) | copy-start | bytes 6148
  11.0 4.6 %copy-start.5 = (f32[3,4,256]{2,1,0:T(4,128)S(1)}, f32[3,4,256]{2,1,0:T(4,128)}, u32[]{:S(2)}) copy-start(f32[3,4,256]{2,1,0:T(4,128)} %param.11) | copy-start | bytes 36868
  11.1 1.4 %collective-permute-start.3 = (bf16[64,1024]{1,0:T(8,128)(2,1)S(1)}, bf16[64,1024]{1,0:T(8,128)(2,1)S(1)}, u32[]{:S(2)}, u32[]{:S(2)}) collective-permute-start(bf16[64,1024]{1,0:T(8,128)(2,1)S(1)} %collective-permute-done.1.got_ref), channel_id=1, source_target_pairs={{0,1},{1,0},{2,3},{3,2},{4,5},{5,4},{6,7},{7,6},{8,9},{9,8},{10,11... | collective-permute-start | bytes 393224 | tf_op jit(solution)/shard_map/ppermute | solution.py:490
  11.1 1.5 %collective-permute-start.4 = (bf16[64,1024]{1,0:T(8,128)(2,1)S(1)}, bf16[64,1024]{1,0:T(8,128)(2,1)S(1)}, u32[]{:S(2)}, u32[]{:S(2)}) collective-permute-start(bf16[64,1024]{1,0:T(8,128)(2,1)S(1)} %collective-permute-done.third_ref), channel_id=1, source_target_pairs={{0,1},{1,0},{2,3},{3,2},{4,5},{5,4},{6,7},{7,6},{8,9},{9,8},{10,11... | collective-permute-start | bytes 393224 | tf_op jit(solution)/shard_map/ppermute | solution.py:490
  13.7 4.3 %collective-permute-start.5 = (bf16[64,256]{1,0:T(8,128)(2,1)S(1)}, bf16[64,256]{1,0:T(8,128)(2,1)S(1)}, u32[]{:S(2)}, u32[]{:S(2)}) collective-permute-start(bf16[64,256]{1,0:T(8,128)(2,1)S(1)} %get-tuple-element.23), channel_id=1, source_target_pairs={{0,17},{1,16},{2,19},{3,18},{4,21},{5,20},{6,23},{7,22},{8,25},{9,... | collective-permute-start | bytes 98312 | tf_op jit(solution)/shard_map/ppermute | solution.py:506
  33.6 1.6 %collective-permute-start.6 = (f32[16,16,128]{2,1,0:T(8,128)S(1)}, f32[16,16,128]{2,1,0:T(8,128)S(1)}, u32[]{:S(2)}, u32[]{:S(2)}) collective-permute-start(f32[16,16,128]{2,1,0:T(8,128)S(1)} %all_to_all.5.recv_ref), channel_id=1, source_target_pairs={{0,1},{1,0},{2,3},{3,2},{4,5},{5,4},{6,7},{7,6},{8,9},{9,8},{10,11... | collective-permute-start | bytes 393224 | tf_op jit(solution)/shard_map/ppermute | solution.py:490

commit v8 on v5

--- a/solution.py
+++ b/solution.py
@@ -128,11 +128,10 @@
     return dot(jnp.concatenate(shifted, axis=1).astype(BF16), counted).astype(jnp.int32)
 
 
-def find(ids, base, tiles, cap, g_dev):
-    local = ids - base
+def find(local, tiles, cap, g_dev):
     mine = (local >= 0) & (local < g_dev)
     key = jnp.where(mine, ranks(mine, tiles), -1)
-    rows, length = ids.shape
+    rows, length = local.shape
     slot = iota((cap, length), 0)
     found = []
     for r in range(0, rows, tiles):
@@ -145,7 +144,7 @@
 
 def pick_kernel(tiles, cap, lists_ref, params_ref, picked_ref):
     width, g_dev = params_ref.shape
-    where = find(lists_ref[...], lax.axis_index("gauss") * g_dev, tiles, cap, g_dev)
+    where = find(lists_ref[...] - lax.axis_index("gauss") * g_dev, tiles, cap, g_dev)
     hot = one_hot(where == iota((where.shape[0], g_dev), 1))
     wide = jnp.concatenate([params_ref[...], jnp.zeros((LANES - width, g_dev), BF16)], axis=0)
     picked_ref[...] = dot(hot, wide, 1, 1).astype(BF16)
@@ -163,8 +162,9 @@
     for k in range(peers):
         lists_scratch[(me // 2) ^ k] = lists_refs[k][...]
     ids = lists_scratch[...].reshape(peers * tiles, length)
-    where_own = find(ids, me * g_dev, tiles, cap, g_dev)
-    where_other = find(ids, (me ^ 1) * g_dev, tiles, cap, g_dev)
+    local = jnp.concatenate([ids - me * g_dev, ids - (me ^ 1) * g_dev], axis=0)
+    where = find(local, tiles, cap, g_dev)
+    where_own, where_other = where[: peers * cap], where[peers * cap :]
     lanes = iota((peers * cap, g_dev), 1)
     of_own = dot(own_ref[...], one_hot(where_own == lanes), 1, 1)
     of_other = dot(other_ref[...], one_hot(where_other == lanes), 1, 1)
@@ -342,8 +342,8 @@
     sums = [down(index) for index in range(6)]
     g_x = sums[0] * dx
     sums = sums + [g_x, g_x * dx, sums[1] * dx]
-    wide = jnp.concatenate([jnp.concatenate(split(s, 3), axis=1) for s in sums], axis=0)
-    gather = one_hot(iota((8, 3 * LANES), 0) == (iota((8, 3 * LANES), 1) % LANES) // share)
+    wide = jnp.concatenate([jnp.concatenate(split(s, 2), axis=1) for s in sums], axis=0)
+    gather = one_hot(iota((8, 2 * LANES), 0) == (iota((8, 2 * LANES), 1) % LANES) // share)
     reduced = dot(gather, wide, 1, 1)
     g_0, g_y, g_yy, s_0, s_1, s_2, g_x, g_xx, g_xy = [
         reduced[:tiles, q * length : (q + 1) * length] for q in range(len(sums))
@@ -498,7 +498,7 @@
         k = 2 * (last - i)
         pairs = []
         for g in range(owners):
-            flip = crossed(g, owners) ^ crossed(g ^ k, owners) if views % 2 == 0 else 0
+            flip = k // 2 % 2 if views % 2 == 0 else 0
             pairs += [(g * views + v, (g ^ k) * views + (v ^ flip)) for v in range(views)]
         out.append(lax.ppermute(block, ("gauss", "view"), pairs) if k else block)
     return out

time: 36 us -> 35.5 us (0.986)
  waiting for transfers between devices: 2.1 us -> 3.45 us
  starting transfers between devices: 12.7 us -> 11.6 us
  blocking collectives: 11.3 us -> 10.8 us
    ppermute x6, waiting for transfers between devices: 2.04 us -> 3.38 us  [far_first(): out.append(lax.ppermute(block, ('gauss', 'view'), pairs) if k else block)]
    ppermute x2, starting transfers between devices: 4.45 us -> 3.85 us  [swap(): lax.ppermute(x, axis, [(i, i ^ k) for i in range(lax.axis_size(axis))])]
    all_to_all x1, blocking collectives: 11.3 us -> 10.8 us  [exchange_wide(): lax.all_to_all(blocks, ('gauss', 'view'), split_axis=0, concat_axis=0, ax...]
    ppermute x6, starting transfers between devices: 8.28 us -> 7.74 us  [far_first(): out.append(lax.ppermute(block, ('gauss', 'view'), pairs) if k else block)]
where the time goes in v8:
time: 35.5 us; the launch traced here: 35.2 us
  starting transfers between devices  11.6 us (33%)
  blocking collectives  10.8 us (30%)
  Pallas kernels  6.88 us (19%)
  waiting for transfers between devices  3.45 us (10%)
  local copies, waits for them, and re-layouts  1.8 us (5%)
  between operations  0.72 us (2%)
    all_to_all x1, blocking collectives, exchange_wide(): lax.all_to_all(blocks, ('gauss', 'view'), split_axis=0, concat_axis=0, ax...  10.8 us
    ppermute x6, starting transfers between devices, far_first(): out.append(lax.ppermute(block, ('gauss', 'view'), pairs) if k else block)  7.74 us
    pallas_call x6, Pallas kernels, call(): pl.pallas_call(kernel, out_shape=out_shape, in_specs=in_specs, out_specs=...  6.88 us
    ppermute x2, starting transfers between devices, swap(): lax.ppermute(x, axis, [(i, i ^ k) for i in range(lax.axis_size(axis))])  3.85 us
    ppermute x6, waiting for transfers between devices, far_first(): out.append(lax.ppermute(block, ('gauss', 'view'), pairs) if k else block)  3.38 us
    unnamed x12, local copies, waits for them, and re-layouts  1.62 us
  transfers between devices with their start and end apart: 8, of which 4 were waited for; matrix products, arithmetic and copies ran while one was open for 1% of the time, Pallas kernels for 6%

profile of v8, /device:TPU:0, one launch (start us, length us, event | category | flops | bytes accessed | tf_op | source)
XLA Modules:
  0.0 35.2 jit_solution(9861201241277536489)
XLA Ops:
  0.6 0.0 copy-start.4
  0.6 0.0 copy-start.3
  0.7 3.0 %collective-permute-start.3 = (bf16[64,1024]{1,0:T(8,128)(2,1)}, bf16[64,1024]{1,0:T(8,128)(2,1)S(1)}, u32[]{:S(2)}, u32[]{:S(2)}) collective-permute-start(bf16[64,1024]{1,0:T(8,128)(2,1)} %params_ref.1), channel_id=1, source_target_pairs={{0,4},{4,0},{8,12},{12,8},{16,20},{20,16},{24,28},{28,24},{1,5},{5... | collective-permute-start | bytes 393224 | tf_op jit(solution)/shard_map/ppermute | solution.py:486
  3.7 2.8 %collective-permute-start.2 = (s32[4,128]{1,0:T(4,128)}, s32[4,128]{1,0:T(4,128)S(1)}, u32[]{:S(2)}, u32[]{:S(2)}) collective-permute-start(s32[4,128]{1,0:T(4,128)} %refs_4_.1), channel_id=1, source_target_pairs={{0,25},{1,24},{2,27},{3,26},{4,29},{5,28},{6,31},{7,30},{8,17},{9,... | collective-permute-start | bytes 6152 | tf_op jit(solution)/shard_map/ppermute | solution.py:503
  6.4 0.0 collective-permute-start.1
  6.4 1.1 %collective-permute-start = (s32[4,128]{1,0:T(4,128)}, s32[4,128]{1,0:T(4,128)S(1)}, u32[]{:S(2)}, u32[]{:S(2)}) collective-permute-start(s32[4,128]{1,0:T(4,128)} %refs_4_.1), channel_id=1, source_target_pairs={{0,9},{1,8},{2,11},{3,10},{4,13},{5,12},{6,15},{7,14},{8,1},{9,0},... | collective-permute-start | bytes 6152 | tf_op jit(solution)/shard_map/ppermute | solution.py:503
  7.5 0.0 copy-done.4
  7.5 0.0 copy-done.3
  7.5 0.0 copy-start
  7.5 0.9 %copy-done = bf16[64,1024]{1,0:T(8,128)(2,1)S(1)} copy-done((bf16[64,1024]{1,0:T(8,128)(2,1)S(1)}, bf16[64,1024]{1,0:T(8,128)(2,1)}, u32[]{:S(2)}) %copy-start) | copy-done | bytes 131096
  8.4 0.0 copy-start.2
  8.4 0.7 %copy-done.2 = f32[28,16]{0,1:T(8,128)S(1)} copy-done((f32[28,16]{0,1:T(8,128)S(1)}, f32[28,16]{0,1:T(8,128)}, u32[]{:S(2)}) %copy-start.2) | copy-done | bytes 1816
  9.1 0.0 copy-start.1
  9.1 0.8 %shard_map.77 = (bf16[64,1024]{1,0:T(8,128)(2,1)S(1)}, f32[28,4,128]{2,1,0:T(4,128)S(1)}, f32[2,8,128]{2,1,0:T(8,128)S(1)}) custom-call(s32[4]{0:T(128)S(1)} %copy-done.3, s32[4]{0:T(128)S(1)} %copy-done.4, f32[16,28]{1,0:T(8,128)S(1)} %bitcast.6, bf16[64,1024]{1,0:T(8,128)(2,1)S(1)} %copy-done), custom_call_target="tpu_custom_call" | custom-call | tf_op jit(solution)/shard_map/pallas_call | solution.py:475
  9.9 0.0 collective-permute-done.2.refs_3_
  9.9 1.2 %collective-permute-done.1.refs_2_ = s32[4,128]{1,0:T(4,128)S(1)} collective-permute-done((s32[4,128]{1,0:T(4,128)}, s32[4,128]{1,0:T(4,128)S(1)}, u32[]{:S(2)}, u32[]{:S(2)}) %collective-permute-start.1) | collective-permute-done | bytes 2080 | tf_op jit(solution)/shard_map/ppermute | solution.py:503
  11.1 0.0 collective-permute-done.refs_1_
  11.1 0.0 collective-permute-done.3.refs_5_
  11.1 0.0 copy-done.1
  11.1 0.0 copy-start.5
  11.1 0.9 %shard_map.78 = (bf16[64,128]{1,0:T(8,128)(2,1)S(1)}, bf16[64,128]{1,0:T(8,128)(2,1)S(1)}, bf16[64,128]{1,0:T(8,128)(2,1)S(1)}, bf16[64,128]{1,0:T(8,128)(2,1)S(1)}) custom-call(s32[4,128]{1,0:T(4,128)S(1)} %copy-done.1, s32[4,128]{1,0:T(4,128)S(1)} %collective-permute-done.refs_1_, s32[4,128]{1,0:T(4,128)S(1)} %collective-permute-done.1.refs_2_, ...), custom_call_target="tpu_custom_call" | custom-call | tf_op jit(solution)/shard_map/pallas_call | solution.py:475
  12.1 1.9 %collective-permute-start.4 = (bf16[64,128]{1,0:T(8,128)(2,1)S(1)}, bf16[64,128]{1,0:T(8,128)(2,1)S(1)}, u32[]{:S(2)}, u32[]{:S(2)}) collective-permute-start(bf16[64,128]{1,0:T(8,128)(2,1)S(1)} %get-tuple-element.16), channel_id=1, source_target_pairs={{0,25},{1,24},{2,27},{3,26},{4,29},{5,28},{6,31},{7,30},{8,17},{9,... | collective-permute-start | bytes 49160 | tf_op jit(solution)/shard_map/ppermute | solution.py:503
  14.0 0.0 collective-permute-start.5
  14.0 2.0 %collective-permute-start.6 = (bf16[64,128]{1,0:T(8,128)(2,1)S(1)}, bf16[64,128]{1,0:T(8,128)(2,1)S(1)}, u32[]{:S(2)}, u32[]{:S(2)}) collective-permute-start(bf16[64,128]{1,0:T(8,128)(2,1)S(1)} %get-tuple-element.18), channel_id=1, source_target_pairs={{0,9},{1,8},{2,11},{3,10},{4,13},{5,12},{6,15},{7,14},{8,1},{9,0},... | collective-permute-start | bytes 49160 | tf_op jit(solution)/shard_map/ppermute | solution.py:503
  16.0 0.0 copy-done.5
  16.0 0.1 reshape.13
  16.1 0.1 reshape.14.refs_9_
  16.2 0.4 %shard_map.79 = (bf16[512,512]{1,0:T(8,128)(2,1)S(1)}, f32[4,128]{1,0:T(4,128)S(1)}) custom-call(s32[4,128]{1,0:T(4,128)S(1)} %copy-done.1, bf16[64,128]{1,0:T(8,128)(2,1)S(1)} %get-tuple-element.19.after_ref.refs_3_), custom_call_target="tpu_custom_call" | custom-call | tf_op jit(solution)/shard_map/pallas_call | solution.py:475
  16.5 0.6 %collective-permute-done.4.refs_0_ = bf16[64,128]{1,0:T(8,128)(2,1)S(1)} collective-permute-done((bf16[64,128]{1,0:T(8,128)(2,1)S(1)}, bf16[64,128]{1,0:T(8,128)(2,1)S(1)}, u32[]{:S(2)}, u32[]{:S(2)}) %collective-permute-start.4) | collective-permute-done | bytes 16416 | tf_op jit(solution)/shard_map/ppermute | solution.py:503
  17.1 1.6 %collective-permute-done.5.refs_1_ = bf16[64,128]{1,0:T(8,128)(2,1)S(1)} collective-permute-done((bf16[64,128]{1,0:T(8,128)(2,1)S(1)}, bf16[64,128]{1,0:T(8,128)(2,1)S(1)}, u32[]{:S(2)}, u32[]{:S(2)}) %collective-permute-start.5) | collective-permute-done | bytes 16416 | tf_op jit(solution)/shard_map/ppermute | solution.py:503
  18.7 0.0 collective-permute-done.6.refs_2_
  18.7 2.3 %shard_map.80 = (f32[3,8,128]{2,1,0:T(8,128)S(1)}, f32[8,2,16,128]{3,2,1,0:T(8,128)S(1)}) custom-call(bf16[64,128]{1,0:T(8,128)(2,1)S(1)} %collective-permute-done.4.refs_0_, bf16[64,128]{1,0:T(8,128)(2,1)S(1)} %collective-permute-done.5.refs_1_, bf16[64,128]{1,0:T(8,128)(2,1)S(1)} %collective-permute-done.6.refs_2_, ...), custom_call_target="tpu_custom_call" | custom-call | tf_op jit(solution)/shard_map/pallas_call | solution.py:475
  21.0 10.8 %all_to_all.5.recv_ref = f32[16,16,128]{2,1,0:T(8,128)S(1)} all-to-all(f32[16,16,128]{2,1,0:T(8,128)S(1)} %bitcast.5), channel_id=1, replica_groups={{0,2,4,6,8,10,12,14,17,19,21,23,25,27,29,31},{1,3,5,7,9,11,13,15,16,18,..., dimensions={0} | all-to-all | bytes 262144 | tf_op jit(solution)/shard_map/all_to_all | solution.py:523
  31.7 0.8 %collective-permute-start.7 = (f32[16,16,128]{2,1,0:T(8,128)S(1)}, f32[16,16,128]{2,1,0:T(8,128)S(1)}, u32[]{:S(2)}, u32[]{:S(2)}) collective-permute-start(f32[16,16,128]{2,1,0:T(8,128)S(1)} %all_to_all.5.recv_ref), channel_id=1, source_target_pairs={{0,1},{1,0},{2,3},{3,2},{4,5},{5,4},{6,7},{7,6},{8,9},{9,8},{10,11... | collective-permute-start | bytes 393224 | tf_op jit(solution)/shard_map/ppermute | solution.py:486
  32.6 0.9 %shard_map.81.sum_ref = f32[80,1024]{1,0:T(8,128)S(1)} custom-call(f32[16,16,128]{2,1,0:T(8,128)S(1)} %all_to_all.5.recv_ref), custom_call_target="tpu_custom_call" | custom-call | tf_op jit(solution)/shard_map/pallas_call | solution.py:475
  33.5 0.1 collective-permute-done.7.recv_ref
  33.6 1.6 %shard_map.82 = (f32[64,1024]{1,0:T(8,128)}, f32[3,4,256]{2,1,0:T(4,128)}) custom-call(f32[16,16,128]{2,1,0:T(8,128)S(1)} %collective-permute-done.7.recv_ref, f32[80,1024]{1,0:T(8,128)S(1)} %shard_map.81.sum_ref, f32[3,8,128]{2,1,0:T(8,128)S(1)} %get-tuple-element.25.spread_ref), custom_call_target="tpu_custom_call" | custom-call | tf_op jit(solution)/shard_map/pallas_call | solution.py:475
  (1 shorter events, 0.0 us)
Async XLA Ops:
  0.6 6.9 %copy-start.4 = (s32[4]{0:T(128)S(1)}, s32[4]{0:T(128)}, u32[]{:S(2)}) copy-start(s32[4]{0:T(128)} %cam_index_ref.1) | copy-start | bytes 52
  0.6 6.8 %copy-start.3 = (s32[4]{0:T(128)S(1)}, s32[4]{0:T(128)}, u32[]{:S(2)}) copy-start(s32[4]{0:T(128)} %tile_pos_ref.1) | copy-start | bytes 52
  0.7 10.5 %collective-permute-start.3 = (bf16[64,1024]{1,0:T(8,128)(2,1)}, bf16[64,1024]{1,0:T(8,128)(2,1)S(1)}, u32[]{:S(2)}, u32[]{:S(2)}) collective-permute-start(bf16[64,1024]{1,0:T(8,128)(2,1)} %params_ref.1), channel_id=1, source_target_pairs={{0,4},{4,0},{8,12},{12,8},{16,20},{20,16},{24,28},{28,24},{1,5},{5... | collective-permute-start | bytes 393224 | tf_op jit(solution)/shard_map/ppermute | solution.py:486
  3.7 6.2 %collective-permute-start.2 = (s32[4,128]{1,0:T(4,128)}, s32[4,128]{1,0:T(4,128)S(1)}, u32[]{:S(2)}, u32[]{:S(2)}) collective-permute-start(s32[4,128]{1,0:T(4,128)} %refs_4_.1), channel_id=1, source_target_pairs={{0,25},{1,24},{2,27},{3,26},{4,29},{5,28},{6,31},{7,30},{8,17},{9,... | collective-permute-start | bytes 6152 | tf_op jit(solution)/shard_map/ppermute | solution.py:503
  6.4 4.7 %collective-permute-start.1 = (s32[4,128]{1,0:T(4,128)}, s32[4,128]{1,0:T(4,128)S(1)}, u32[]{:S(2)}, u32[]{:S(2)}) collective-permute-start(s32[4,128]{1,0:T(4,128)} %refs_4_.1), channel_id=1, source_target_pairs={{0,16},{1,17},{2,18},{3,19},{4,20},{5,21},{6,22},{7,23},{8,24},{9,... | collective-permute-start | bytes 6152 | tf_op jit(solution)/shard_map/ppermute | solution.py:503
  6.4 4.7 %collective-permute-start = (s32[4,128]{1,0:T(4,128)}, s32[4,128]{1,0:T(4,128)S(1)}, u32[]{:S(2)}, u32[]{:S(2)}) collective-permute-start(s32[4,128]{1,0:T(4,128)} %refs_4_.1), channel_id=1, source_target_pairs={{0,9},{1,8},{2,11},{3,10},{4,13},{5,12},{6,15},{7,14},{8,1},{9,0},... | collective-permute-start | bytes 6152 | tf_op jit(solution)/shard_map/ppermute | solution.py:503
  7.5 0.9 %copy-start = (bf16[64,1024]{1,0:T(8,128)(2,1)S(1)}, bf16[64,1024]{1,0:T(8,128)(2,1)}, u32[]{:S(2)}) copy-start(bf16[64,1024]{1,0:T(8,128)(2,1)} %params_ref.1) | copy-start | bytes 393220
  8.4 0.7 %copy-start.2 = (f32[28,16]{0,1:T(8,128)S(1)}, f32[28,16]{0,1:T(8,128)}, u32[]{:S(2)}) copy-start(f32[28,16]{0,1:T(8,128)} %param.10) | copy-start | bytes 5380
  9.1 2.0 %copy-start.1 = (s32[4,128]{1,0:T(4,128)S(1)}, s32[4,128]{1,0:T(4,128)}, u32[]{:S(2)}) copy-start(s32[4,128]{1,0:T(4,128)} %refs_4_.1) | copy-start | bytes 6148
  11.1 4.9 %copy-start.5 = (f32[3,4,256]{2,1,0:T(4,128)S(1)}, f32[3,4,256]{2,1,0:T(4,128)}, u32[]{:S(2)}) copy-start(f32[3,4,256]{2,1,0:T(4,128)} %param.11) | copy-start | bytes 36868
  12.1 5.0 %collective-permute-start.4 = (bf16[64,128]{1,0:T(8,128)(2,1)S(1)}, bf16[64,128]{1,0:T(8,128)(2,1)S(1)}, u32[]{:S(2)}, u32[]{:S(2)}) collective-permute-start(bf16[64,128]{1,0:T(8,128)(2,1)S(1)} %get-tuple-element.16), channel_id=1, source_target_pairs={{0,25},{1,24},{2,27},{3,26},{4,29},{5,28},{6,31},{7,30},{8,17},{9,... | collective-permute-start | bytes 49160 | tf_op jit(solution)/shard_map/ppermute | solution.py:503
  14.0 4.7 %collective-permute-start.5 = (bf16[64,128]{1,0:T(8,128)(2,1)S(1)}, bf16[64,128]{1,0:T(8,128)(2,1)S(1)}, u32[]{:S(2)}, u32[]{:S(2)}) collective-permute-start(bf16[64,128]{1,0:T(8,128)(2,1)S(1)} %get-tuple-element.17), channel_id=1, source_target_pairs={{0,16},{1,17},{2,18},{3,19},{4,20},{5,21},{6,22},{7,23},{8,24},{9,... | collective-permute-start | bytes 49160 | tf_op jit(solution)/shard_map/ppermute | solution.py:503
  14.0 4.7 %collective-permute-start.6 = (bf16[64,128]{1,0:T(8,128)(2,1)S(1)}, bf16[64,128]{1,0:T(8,128)(2,1)S(1)}, u32[]{:S(2)}, u32[]{:S(2)}) collective-permute-start(bf16[64,128]{1,0:T(8,128)(2,1)S(1)} %get-tuple-element.18), channel_id=1, source_target_pairs={{0,9},{1,8},{2,11},{3,10},{4,13},{5,12},{6,15},{7,14},{8,1},{9,0},... | collective-permute-start | bytes 49160 | tf_op jit(solution)/shard_map/ppermute | solution.py:503
  31.7 1.8 %collective-permute-start.7 = (f32[16,16,128]{2,1,0:T(8,128)S(1)}, f32[16,16,128]{2,1,0:T(8,128)S(1)}, u32[]{:S(2)}, u32[]{:S(2)}) collective-permute-start(f32[16,16,128]{2,1,0:T(8,128)S(1)} %all_to_all.5.recv_ref), channel_id=1, source_target_pairs={{0,1},{1,0},{2,3},{3,2},{4,5},{5,4},{6,7},{7,6},{8,9},{9,8},{10,11... | collective-permute-start | bytes 393224 | tf_op jit(solution)/shard_map/ppermute | solution.py:486

commit v9 on v8

--- a/solution.py
+++ b/solution.py
@@ -407,12 +407,15 @@
     terms = jnp.concatenate([jnp.ones_like(dir_z)] + terms, axis=0)
     rows = [values] + [terms * values[11 + k : 12 + k] for k in range(3)]
     parts = split(jnp.concatenate(rows, axis=0), 2)
-    return jnp.concatenate(parts, axis=0), values[21:22].astype(jnp.int32)
+    first = 21 // high * cap
+    names = recv_ref[:, 21 % high, first : first + cap].T
+    names = jnp.concatenate([names[:, b : b + 1] for b in range(blocks)], axis=0)
+    return jnp.concatenate(parts, axis=0), names.astype(jnp.int32)
 
 
 def scatter(rows, where, first, count):
-    hot = one_hot(iota((count, where.shape[1]), 0) + first == where)
-    total = dot(rows, hot, 1, 1)
+    hot = one_hot(iota((where.shape[0], count), 1) + first == where)
+    total = dot(rows, hot)
     half = total.shape[0] // 2
     return total[:half] + total[half:]
 
@@ -490,18 +493,21 @@
     return int(owner >= owners // 2)
 
 
+def reach(x, step, flip):
+    owners, views = lax.axis_size("gauss"), lax.axis_size("view")
+    flip = flip if views % 2 == 0 else 0
+    pairs = [
+        (g * views + v, (g ^ step) * views + (v ^ flip))
+        for g in range(owners)
+        for v in range(views)
+    ]
+    return lax.ppermute(x, ("gauss", "view"), pairs)
+
+
 def far_first(blocks):
-    owners, views = lax.axis_size("gauss"), lax.axis_size("view")
     last = len(blocks) - 1
-    out = []
-    for i, block in enumerate(blocks):
-        k = 2 * (last - i)
-        pairs = []
-        for g in range(owners):
-            flip = k // 2 % 2 if views % 2 == 0 else 0
-            pairs += [(g * views + v, (g ^ k) * views + (v ^ flip)) for v in range(views)]
-        out.append(lax.ppermute(block, ("gauss", "view"), pairs) if k else block)
-    return out
+    peers = range(last, 0, -1)
+    return [reach(b, 2 * k, k % 2) for b, k in zip(blocks, peers)] + [blocks[last]]
 
 
 def exchange(x):
@@ -552,7 +558,7 @@
     wide = views % 2 == 0 and owners * views <= 32
 
     if paired:
-        other = swap(params, "gauss", 1)
+        other = reach(params, 1, 1)
         all_lists = far_first([lists] * peers)
     params_copy, cam, pixel = call(
         prepare_kernel,

time: 35.5 us -> 35.5 us (level)
  waiting for transfers between devices: 3.45 us -> 4.13 us
  blocking collectives: 10.8 us -> 10.3 us
    ppermute x2 -> x1, starting transfers between devices: 3.85 us -> 0.86 us  [swap(): lax.ppermute(x, axis, [(i, i ^ k) for i in range(lax.axis_size(axis))])]
    ppermute x6 -> x7, starting transfers between devices: 7.74 us -> 10.5 us  [reach(): return lax.ppermute(x, ('gauss', 'view'), pairs)]
    ppermute x6 -> x7, waiting for transfers between devices: 3.38 us -> 4.12 us  [reach(): return lax.ppermute(x, ('gauss', 'view'), pairs)]
    all_to_all x1, blocking collectives: 10.8 us -> 10.3 us  [exchange_wide(): lax.all_to_all(blocks, ('gauss', 'view'), split_axis=0, concat_axis=0, ax...]
  transfers between devices with their start and end apart: 8 -> 8, of which waited for: 4 -> 3; matrix products, arithmetic and copies ran while one was open for 1% -> 1% of each run, Pallas kernels for 6% -> 6%
where the time goes in v9:
time: 35.5 us; the launch traced here: 35.3 us
  starting transfers between devices  11.4 us (32%)
  blocking collectives  10.3 us (29%)
  Pallas kernels  6.97 us (20%)
  waiting for transfers between devices  4.13 us (12%)
  local copies, waits for them, and re-layouts  1.8 us (5%)
  between operations  0.72 us (2%)
    ppermute x7, starting transfers between devices, reach(): return lax.ppermute(x, ('gauss', 'view'), pairs)  10.5 us
    all_to_all x1, blocking collectives, exchange_wide(): lax.all_to_all(blocks, ('gauss', 'view'), split_axis=0, concat_axis=0, ax...  10.3 us
    pallas_call x6, Pallas kernels, call(): pl.pallas_call(kernel, out_shape=out_shape, in_specs=in_specs, out_specs=...  6.97 us
    ppermute x7, waiting for transfers between devices, reach(): return lax.ppermute(x, ('gauss', 'view'), pairs)  4.12 us
    unnamed x12, local copies, waits for them, and re-layouts  1.62 us
    ppermute x1, starting transfers between devices, swap(): lax.ppermute(x, axis, [(i, i ^ k) for i in range(lax.axis_size(axis))])  0.86 us
  transfers between devices with their start and end apart: 8, of which 3 were waited for; matrix products, arithmetic and copies ran while one was open for 1% of the time, Pallas kernels for 6%

profile of v9, /device:TPU:0, one launch (start us, length us, event | category | flops | bytes accessed | tf_op | source)
XLA Modules:
  0.0 35.3 jit_solution(9217272412914579457)
XLA Ops:
  0.6 0.0 copy-start.4
  0.6 0.0 copy-start.3
  0.7 2.4 %collective-permute-start.3 = (bf16[64,1024]{1,0:T(8,128)(2,1)}, bf16[64,1024]{1,0:T(8,128)(2,1)S(1)}, u32[]{:S(2)}, u32[]{:S(2)}) collective-permute-start(bf16[64,1024]{1,0:T(8,128)(2,1)} %params_ref.1), channel_id=1, source_target_pairs={{0,5},{1,4},{2,7},{3,6},{4,1},{5,0},{6,3},{7,2},{8,13},{9,12},{10,... | collective-permute-start | bytes 393224 | tf_op jit(solution)/shard_map/ppermute | solution.py:504
  3.1 3.9 %collective-permute-start.2 = (s32[4,128]{1,0:T(4,128)}, s32[4,128]{1,0:T(4,128)S(1)}, u32[]{:S(2)}, u32[]{:S(2)}) collective-permute-start(s32[4,128]{1,0:T(4,128)} %refs_4_.1), channel_id=1, source_target_pairs={{0,25},{1,24},{2,27},{3,26},{4,29},{5,28},{6,31},{7,30},{8,17},{9,... | collective-permute-start | bytes 6152 | tf_op jit(solution)/shard_map/ppermute | solution.py:504
  7.0 0.0 collective-permute-start.1
  7.0 0.3 collective-permute-start
  7.3 0.0 copy-done.4
  7.3 0.0 copy-done.3
  7.3 0.0 copy-start
  7.3 0.9 %copy-done = bf16[64,1024]{1,0:T(8,128)(2,1)S(1)} copy-done((bf16[64,1024]{1,0:T(8,128)(2,1)S(1)}, bf16[64,1024]{1,0:T(8,128)(2,1)}, u32[]{:S(2)}) %copy-start) | copy-done | bytes 131096
  8.2 0.0 copy-start.2
  8.2 0.7 %copy-done.2 = f32[28,16]{0,1:T(8,128)S(1)} copy-done((f32[28,16]{0,1:T(8,128)S(1)}, f32[28,16]{0,1:T(8,128)}, u32[]{:S(2)}) %copy-start.2) | copy-done | bytes 1816
  8.9 0.0 copy-start.1
  8.9 0.8 %shard_map.77 = (bf16[64,1024]{1,0:T(8,128)(2,1)S(1)}, f32[28,4,128]{2,1,0:T(4,128)S(1)}, f32[2,8,128]{2,1,0:T(8,128)S(1)}) custom-call(s32[4]{0:T(128)S(1)} %copy-done.3, s32[4]{0:T(128)S(1)} %copy-done.4, f32[16,28]{1,0:T(8,128)S(1)} %bitcast.6, bf16[64,1024]{1,0:T(8,128)(2,1)S(1)} %copy-done), custom_call_target="tpu_custom_call" | custom-call | tf_op jit(solution)/shard_map/pallas_call | solution.py:478
  9.6 0.0 collective-permute-done.2.refs_3_
  9.7 2.0 %collective-permute-done.1.refs_2_ = s32[4,128]{1,0:T(4,128)S(1)} collective-permute-done((s32[4,128]{1,0:T(4,128)}, s32[4,128]{1,0:T(4,128)S(1)}, u32[]{:S(2)}, u32[]{:S(2)}) %collective-permute-start.1) | collective-permute-done | bytes 2080 | tf_op jit(solution)/shard_map/ppermute | solution.py:504
  11.7 0.0 collective-permute-done.refs_1_
  11.7 0.0 collective-permute-done.3.refs_5_
  11.7 0.0 copy-done.1
  11.7 0.0 copy-start.5
  11.7 0.9 %shard_map.78 = (bf16[64,128]{1,0:T(8,128)(2,1)S(1)}, bf16[64,128]{1,0:T(8,128)(2,1)S(1)}, bf16[64,128]{1,0:T(8,128)(2,1)S(1)}, bf16[64,128]{1,0:T(8,128)(2,1)S(1)}) custom-call(s32[4,128]{1,0:T(4,128)S(1)} %copy-done.1, s32[4,128]{1,0:T(4,128)S(1)} %collective-permute-done.refs_1_, s32[4,128]{1,0:T(4,128)S(1)} %collective-permute-done.1.refs_2_, ...), custom_call_target="tpu_custom_call" | custom-call | tf_op jit(solution)/shard_map/pallas_call | solution.py:478
  12.6 1.9 %collective-permute-start.4 = (bf16[64,128]{1,0:T(8,128)(2,1)S(1)}, bf16[64,128]{1,0:T(8,128)(2,1)S(1)}, u32[]{:S(2)}, u32[]{:S(2)}) collective-permute-start(bf16[64,128]{1,0:T(8,128)(2,1)S(1)} %get-tuple-element.16), channel_id=1, source_target_pairs={{0,25},{1,24},{2,27},{3,26},{4,29},{5,28},{6,31},{7,30},{8,17},{9,... | collective-permute-start | bytes 49160 | tf_op jit(solution)/shard_map/ppermute | solution.py:504
  14.5 0.0 collective-permute-start.5
  14.5 2.0 %collective-permute-start.6 = (bf16[64,128]{1,0:T(8,128)(2,1)S(1)}, bf16[64,128]{1,0:T(8,128)(2,1)S(1)}, u32[]{:S(2)}, u32[]{:S(2)}) collective-permute-start(bf16[64,128]{1,0:T(8,128)(2,1)S(1)} %get-tuple-element.18), channel_id=1, source_target_pairs={{0,9},{1,8},{2,11},{3,10},{4,13},{5,12},{6,15},{7,14},{8,1},{9,0},... | collective-permute-start | bytes 49160 | tf_op jit(solution)/shard_map/ppermute | solution.py:504
  16.5 0.0 copy-done.5
  16.5 0.1 reshape.13
  16.6 0.1 reshape.14.refs_9_
  16.7 0.4 %shard_map.79 = (bf16[512,512]{1,0:T(8,128)(2,1)S(1)}, f32[4,128]{1,0:T(4,128)S(1)}) custom-call(s32[4,128]{1,0:T(4,128)S(1)} %copy-done.1, bf16[64,128]{1,0:T(8,128)(2,1)S(1)} %get-tuple-element.19.after_ref.refs_3_), custom_call_target="tpu_custom_call" | custom-call | tf_op jit(solution)/shard_map/pallas_call | solution.py:478
  17.1 0.6 %collective-permute-done.4.refs_0_ = bf16[64,128]{1,0:T(8,128)(2,1)S(1)} collective-permute-done((bf16[64,128]{1,0:T(8,128)(2,1)S(1)}, bf16[64,128]{1,0:T(8,128)(2,1)S(1)}, u32[]{:S(2)}, u32[]{:S(2)}) %collective-permute-start.4) | collective-permute-done | bytes 16416 | tf_op jit(solution)/shard_map/ppermute | solution.py:504
  17.7 1.5 %collective-permute-done.5.refs_1_ = bf16[64,128]{1,0:T(8,128)(2,1)S(1)} collective-permute-done((bf16[64,128]{1,0:T(8,128)(2,1)S(1)}, bf16[64,128]{1,0:T(8,128)(2,1)S(1)}, u32[]{:S(2)}, u32[]{:S(2)}) %collective-permute-start.5) | collective-permute-done | bytes 16416 | tf_op jit(solution)/shard_map/ppermute | solution.py:504
  19.2 0.0 collective-permute-done.6.refs_2_
  19.2 2.3 %shard_map.80 = (f32[3,8,128]{2,1,0:T(8,128)S(1)}, f32[8,2,16,128]{3,2,1,0:T(8,128)S(1)}) custom-call(bf16[64,128]{1,0:T(8,128)(2,1)S(1)} %collective-permute-done.4.refs_0_, bf16[64,128]{1,0:T(8,128)(2,1)S(1)} %collective-permute-done.5.refs_1_, bf16[64,128]{1,0:T(8,128)(2,1)S(1)} %collective-permute-done.6.refs_2_, ...), custom_call_target="tpu_custom_call" | custom-call | tf_op jit(solution)/shard_map/pallas_call | solution.py:478
  21.5 10.3 %all_to_all.5.recv_ref = f32[16,16,128]{2,1,0:T(8,128)S(1)} all-to-all(f32[16,16,128]{2,1,0:T(8,128)S(1)} %bitcast.5), channel_id=1, replica_groups={{0,2,4,6,8,10,12,14,17,19,21,23,25,27,29,31},{1,3,5,7,9,11,13,15,16,18,..., dimensions={0} | all-to-all | bytes 262144 | tf_op jit(solution)/shard_map/all_to_all | solution.py:529
  31.7 0.9 %collective-permute-start.7 = (f32[16,16,128]{2,1,0:T(8,128)S(1)}, f32[16,16,128]{2,1,0:T(8,128)S(1)}, u32[]{:S(2)}, u32[]{:S(2)}) collective-permute-start(f32[16,16,128]{2,1,0:T(8,128)S(1)} %all_to_all.5.recv_ref), channel_id=1, source_target_pairs={{0,1},{1,0},{2,3},{3,2},{4,5},{5,4},{6,7},{7,6},{8,9},{9,8},{10,11... | collective-permute-start | bytes 393224 | tf_op jit(solution)/shard_map/ppermute | solution.py:489
  32.6 1.0 %shard_map.81.sum_ref = f32[80,1024]{1,0:T(8,128)S(1)} custom-call(f32[16,16,128]{2,1,0:T(8,128)S(1)} %all_to_all.5.recv_ref), custom_call_target="tpu_custom_call" | custom-call | tf_op jit(solution)/shard_map/pallas_call | solution.py:478
  33.6 0.0 collective-permute-done.7.recv_ref
  33.6 1.7 %shard_map.82 = (f32[64,1024]{1,0:T(8,128)}, f32[3,4,256]{2,1,0:T(4,128)}) custom-call(f32[16,16,128]{2,1,0:T(8,128)S(1)} %collective-permute-done.7.recv_ref, f32[80,1024]{1,0:T(8,128)S(1)} %shard_map.81.sum_ref, f32[3,8,128]{2,1,0:T(8,128)S(1)} %get-tuple-element.25.spread_ref), custom_call_target="tpu_custom_call" | custom-call | tf_op jit(solution)/shard_map/pallas_call | solution.py:478
  (1 shorter events, 0.0 us)
Async XLA Ops:
  0.6 6.6 %copy-start.4 = (s32[4]{0:T(128)S(1)}, s32[4]{0:T(128)}, u32[]{:S(2)}) copy-start(s32[4]{0:T(128)} %cam_index_ref.1) | copy-start | bytes 52
  0.6 6.6 %copy-start.3 = (s32[4]{0:T(128)S(1)}, s32[4]{0:T(128)}, u32[]{:S(2)}) copy-start(s32[4]{0:T(128)} %tile_pos_ref.1) | copy-start | bytes 52
  0.7 11.0 %collective-permute-start.3 = (bf16[64,1024]{1,0:T(8,128)(2,1)}, bf16[64,1024]{1,0:T(8,128)(2,1)S(1)}, u32[]{:S(2)}, u32[]{:S(2)}) collective-permute-start(bf16[64,1024]{1,0:T(8,128)(2,1)} %params_ref.1), channel_id=1, source_target_pairs={{0,5},{1,4},{2,7},{3,6},{4,1},{5,0},{6,3},{7,2},{8,13},{9,12},{10,... | collective-permute-start | bytes 393224 | tf_op jit(solution)/shard_map/ppermute | solution.py:504
  3.1 6.6 %collective-permute-start.2 = (s32[4,128]{1,0:T(4,128)}, s32[4,128]{1,0:T(4,128)S(1)}, u32[]{:S(2)}, u32[]{:S(2)}) collective-permute-start(s32[4,128]{1,0:T(4,128)} %refs_4_.1), channel_id=1, source_target_pairs={{0,25},{1,24},{2,27},{3,26},{4,29},{5,28},{6,31},{7,30},{8,17},{9,... | collective-permute-start | bytes 6152 | tf_op jit(solution)/shard_map/ppermute | solution.py:504
  7.0 4.7 %collective-permute-start.1 = (s32[4,128]{1,0:T(4,128)}, s32[4,128]{1,0:T(4,128)S(1)}, u32[]{:S(2)}, u32[]{:S(2)}) collective-permute-start(s32[4,128]{1,0:T(4,128)} %refs_4_.1), channel_id=1, source_target_pairs={{0,16},{1,17},{2,18},{3,19},{4,20},{5,21},{6,22},{7,23},{8,24},{9,... | collective-permute-start | bytes 6152 | tf_op jit(solution)/shard_map/ppermute | solution.py:504
  7.0 4.7 %collective-permute-start = (s32[4,128]{1,0:T(4,128)}, s32[4,128]{1,0:T(4,128)S(1)}, u32[]{:S(2)}, u32[]{:S(2)}) collective-permute-start(s32[4,128]{1,0:T(4,128)} %refs_4_.1), channel_id=1, source_target_pairs={{0,9},{1,8},{2,11},{3,10},{4,13},{5,12},{6,15},{7,14},{8,1},{9,0},... | collective-permute-start | bytes 6152 | tf_op jit(solution)/shard_map/ppermute | solution.py:504
  7.3 0.9 %copy-start = (bf16[64,1024]{1,0:T(8,128)(2,1)S(1)}, bf16[64,1024]{1,0:T(8,128)(2,1)}, u32[]{:S(2)}) copy-start(bf16[64,1024]{1,0:T(8,128)(2,1)} %params_ref.1) | copy-start | bytes 393220
  8.2 0.7 %copy-start.2 = (f32[28,16]{0,1:T(8,128)S(1)}, f32[28,16]{0,1:T(8,128)}, u32[]{:S(2)}) copy-start(f32[28,16]{0,1:T(8,128)} %param.10) | copy-start | bytes 5380
  8.9 2.8 %copy-start.1 = (s32[4,128]{1,0:T(4,128)S(1)}, s32[4,128]{1,0:T(4,128)}, u32[]{:S(2)}) copy-start(s32[4,128]{1,0:T(4,128)} %refs_4_.1) | copy-start | bytes 6148
  11.7 4.9 %copy-start.5 = (f32[3,4,256]{2,1,0:T(4,128)S(1)}, f32[3,4,256]{2,1,0:T(4,128)}, u32[]{:S(2)}) copy-start(f32[3,4,256]{2,1,0:T(4,128)} %param.11) | copy-start | bytes 36868
  12.6 5.0 %collective-permute-start.4 = (bf16[64,128]{1,0:T(8,128)(2,1)S(1)}, bf16[64,128]{1,0:T(8,128)(2,1)S(1)}, u32[]{:S(2)}, u32[]{:S(2)}) collective-permute-start(bf16[64,128]{1,0:T(8,128)(2,1)S(1)} %get-tuple-element.16), channel_id=1, source_target_pairs={{0,25},{1,24},{2,27},{3,26},{4,29},{5,28},{6,31},{7,30},{8,17},{9,... | collective-permute-start | bytes 49160 | tf_op jit(solution)/shard_map/ppermute | solution.py:504
  14.5 4.6 %collective-permute-start.5 = (bf16[64,128]{1,0:T(8,128)(2,1)S(1)}, bf16[64,128]{1,0:T(8,128)(2,1)S(1)}, u32[]{:S(2)}, u32[]{:S(2)}) collective-permute-start(bf16[64,128]{1,0:T(8,128)(2,1)S(1)} %get-tuple-element.17), channel_id=1, source_target_pairs={{0,16},{1,17},{2,18},{3,19},{4,20},{5,21},{6,22},{7,23},{8,24},{9,... | collective-permute-start | bytes 49160 | tf_op jit(solution)/shard_map/ppermute | solution.py:504
  14.5 4.6 %collective-permute-start.6 = (bf16[64,128]{1,0:T(8,128)(2,1)S(1)}, bf16[64,128]{1,0:T(8,128)(2,1)S(1)}, u32[]{:S(2)}, u32[]{:S(2)}) collective-permute-start(bf16[64,128]{1,0:T(8,128)(2,1)S(1)} %get-tuple-element.18), channel_id=1, source_target_pairs={{0,9},{1,8},{2,11},{3,10},{4,13},{5,12},{6,15},{7,14},{8,1},{9,0},... | collective-permute-start | bytes 49160 | tf_op jit(solution)/shard_map/ppermute | solution.py:504
  31.7 1.8 %collective-permute-start.7 = (f32[16,16,128]{2,1,0:T(8,128)S(1)}, f32[16,16,128]{2,1,0:T(8,128)S(1)}, u32[]{:S(2)}, u32[]{:S(2)}) collective-permute-start(f32[16,16,128]{2,1,0:T(8,128)S(1)} %all_to_all.5.recv_ref), channel_id=1, source_target_pairs={{0,1},{1,0},{2,3},{3,2},{4,5},{5,4},{6,7},{7,6},{8,9},{9,8},{10,11... | collective-permute-start | bytes 393224 | tf_op jit(solution)/shard_map/ppermute | solution.py:489

commit v10 on v9

--- a/solution.py
+++ b/solution.py
@@ -270,23 +270,17 @@
         (-0.5 * LOG2E) * con_c,
         jnp.where(live, opacity, 0.0),
     ] + colors
-    count = len(attrs)
-    blocks = []
-    for value in attrs:
-        parts = [p.astype(F32) for p in split(value, 3)]
-        parts.append(jnp.zeros((16 - 3 * tiles, length), F32))
-        blocks.append(jnp.concatenate(parts, axis=0))
-    stacked = jnp.concatenate(blocks, axis=1)
-    lane_tile = iota((16, LANES), 1) // share
-    row_index = iota((16, LANES), 0)
-    spread = one_hot((row_index % tiles == lane_tile) & (row_index < 3 * tiles))
-    table = dot(stacked.T.astype(BF16), spread)
+    table = [
+        jnp.concatenate(
+            [jnp.broadcast_to(value[t : t + 1, :], (share, length)) for t in range(tiles)], axis=0
+        ).T
+        for value in attrs
+    ]
     pixel_x, pixel_y = pixel_ref[0, :1, :], pixel_ref[1]
-    dx = pixel_x - table[:length]
-    table_ref[0:length, :] = table[2 * length : 3 * length] * dx * dx
-    table_ref[length : 2 * length, :] = table[3 * length : 4 * length] * dx
-    table_ref[2 * length : 3 * length, :] = table[length : 2 * length]
-    table_ref[3 * length :, :] = table[4 * length :]
+    dx = pixel_x - table[0]
+    columns = [table[2] * dx * dx, table[3] * dx, table[1]] + table[4:]
+    for index, column in enumerate(columns):
+        table_ref[index * length : (index + 1) * length, :] = column
 
     def row(index, l):
         return table_ref[index * length + l : index * length + l + 1, :]
@@ -407,15 +401,12 @@
     terms = jnp.concatenate([jnp.ones_like(dir_z)] + terms, axis=0)
     rows = [values] + [terms * values[11 + k : 12 + k] for k in range(3)]
     parts = split(jnp.concatenate(rows, axis=0), 2)
-    first = 21 // high * cap
-    names = recv_ref[:, 21 % high, first : first + cap].T
-    names = jnp.concatenate([names[:, b : b + 1] for b in range(blocks)], axis=0)
-    return jnp.concatenate(parts, axis=0), names.astype(jnp.int32)
+    return jnp.concatenate(parts, axis=0), values[21:22].astype(jnp.int32)
 
 
 def scatter(rows, where, first, count):
-    hot = one_hot(iota((where.shape[0], count), 1) + first == where)
-    total = dot(rows, hot)
+    hot = one_hot(iota((count, where.shape[1]), 0) + first == where)
+    total = dot(rows, hot, 1, 1)
     half = total.shape[0] // 2
     return total[:half] + total[half:]
 

time: 35.5 us -> 35.3 us (level)
  transfers between devices with their start and end apart: 8 -> 8, of which waited for: 3 -> 4; matrix products, arithmetic and copies ran while one was open for 1% -> 1% of each run, Pallas kernels for 6% -> 6%
where the time goes in v10:
time: 35.3 us; the launch traced here: 35 us
  starting transfers between devices  11.4 us (32%)
  blocking collectives  10.3 us (29%)
  Pallas kernels  6.72 us (19%)
  waiting for transfers between devices  4.18 us (12%)
  local copies, waits for them, and re-layouts  1.8 us (5%)
  between operations  0.72 us (2%)
    ppermute x7, starting transfers between devices, reach(): return lax.ppermute(x, ('gauss', 'view'), pairs)  10.5 us
    all_to_all x1, blocking collectives, exchange_wide(): lax.all_to_all(blocks, ('gauss', 'view'), split_axis=0, concat_axis=0, ax...  10.3 us
    pallas_call x6, Pallas kernels, call(): pl.pallas_call(kernel, out_shape=out_shape, in_specs=in_specs, out_specs=...  6.72 us
    ppermute x7, waiting for transfers between devices, reach(): return lax.ppermute(x, ('gauss', 'view'), pairs)  4.12 us
    unnamed x12, local copies, waits for them, and re-layouts  1.62 us
    ppermute x1, starting transfers between devices, swap(): lax.ppermute(x, axis, [(i, i ^ k) for i in range(lax.axis_size(axis))])  0.86 us
  transfers between devices with their start and end apart: 8, of which 4 were waited for; matrix products, arithmetic and copies ran while one was open for 1% of the time, Pallas kernels for 6%

profile of v10, /device:TPU:0, one launch (start us, length us, event | category | flops | bytes accessed | tf_op | source)
XLA Modules:
  0.0 35.0 jit_solution(4842909927742465125)
XLA Ops:
  0.6 0.0 copy-start.4
  0.6 0.0 copy-start.3
  0.7 2.4 %collective-permute-start.3 = (bf16[64,1024]{1,0:T(8,128)(2,1)}, bf16[64,1024]{1,0:T(8,128)(2,1)S(1)}, u32[]{:S(2)}, u32[]{:S(2)}) collective-permute-start(bf16[64,1024]{1,0:T(8,128)(2,1)} %params_ref.1), channel_id=1, source_target_pairs={{0,5},{1,4},{2,7},{3,6},{4,1},{5,0},{6,3},{7,2},{8,13},{9,12},{10,... | collective-permute-start | bytes 393224 | tf_op jit(solution)/shard_map/ppermute | solution.py:495
  3.1 3.9 %collective-permute-start.2 = (s32[4,128]{1,0:T(4,128)}, s32[4,128]{1,0:T(4,128)S(1)}, u32[]{:S(2)}, u32[]{:S(2)}) collective-permute-start(s32[4,128]{1,0:T(4,128)} %refs_4_.1), channel_id=1, source_target_pairs={{0,25},{1,24},{2,27},{3,26},{4,29},{5,28},{6,31},{7,30},{8,17},{9,... | collective-permute-start | bytes 6152 | tf_op jit(solution)/shard_map/ppermute | solution.py:495
  7.0 0.0 collective-permute-start.1
  7.0 0.3 collective-permute-start
  7.3 0.0 copy-done.4
  7.3 0.0 copy-done.3
  7.3 0.0 copy-start
  7.3 0.9 %copy-done = bf16[64,1024]{1,0:T(8,128)(2,1)S(1)} copy-done((bf16[64,1024]{1,0:T(8,128)(2,1)S(1)}, bf16[64,1024]{1,0:T(8,128)(2,1)}, u32[]{:S(2)}) %copy-start) | copy-done | bytes 131096
  8.2 0.0 copy-start.2
  8.2 0.7 %copy-done.2 = f32[28,16]{0,1:T(8,128)S(1)} copy-done((f32[28,16]{0,1:T(8,128)S(1)}, f32[28,16]{0,1:T(8,128)}, u32[]{:S(2)}) %copy-start.2) | copy-done | bytes 1816
  8.9 0.0 copy-start.1
  8.9 0.8 %shard_map.77 = (bf16[64,1024]{1,0:T(8,128)(2,1)S(1)}, f32[28,4,128]{2,1,0:T(4,128)S(1)}, f32[2,8,128]{2,1,0:T(8,128)S(1)}) custom-call(s32[4]{0:T(128)S(1)} %copy-done.3, s32[4]{0:T(128)S(1)} %copy-done.4, f32[16,28]{1,0:T(8,128)S(1)} %bitcast.6, bf16[64,1024]{1,0:T(8,128)(2,1)S(1)} %copy-done), custom_call_target="tpu_custom_call" | custom-call | tf_op jit(solution)/shard_map/pallas_call | solution.py:469
  9.6 0.0 collective-permute-done.2.refs_3_
  9.7 2.0 %collective-permute-done.1.refs_2_ = s32[4,128]{1,0:T(4,128)S(1)} collective-permute-done((s32[4,128]{1,0:T(4,128)}, s32[4,128]{1,0:T(4,128)S(1)}, u32[]{:S(2)}, u32[]{:S(2)}) %collective-permute-start.1) | collective-permute-done | bytes 2080 | tf_op jit(solution)/shard_map/ppermute | solution.py:495
  11.7 0.0 collective-permute-done.refs_1_
  11.7 0.0 collective-permute-done.3.refs_5_
  11.7 0.0 copy-done.1
  11.7 0.0 copy-start.5
  11.7 0.9 %shard_map.78 = (bf16[64,128]{1,0:T(8,128)(2,1)S(1)}, bf16[64,128]{1,0:T(8,128)(2,1)S(1)}, bf16[64,128]{1,0:T(8,128)(2,1)S(1)}, bf16[64,128]{1,0:T(8,128)(2,1)S(1)}) custom-call(s32[4,128]{1,0:T(4,128)S(1)} %copy-done.1, s32[4,128]{1,0:T(4,128)S(1)} %collective-permute-done.refs_1_, s32[4,128]{1,0:T(4,128)S(1)} %collective-permute-done.1.refs_2_, ...), custom_call_target="tpu_custom_call" | custom-call | tf_op jit(solution)/shard_map/pallas_call | solution.py:469
  12.6 1.9 %collective-permute-start.4 = (bf16[64,128]{1,0:T(8,128)(2,1)S(1)}, bf16[64,128]{1,0:T(8,128)(2,1)S(1)}, u32[]{:S(2)}, u32[]{:S(2)}) collective-permute-start(bf16[64,128]{1,0:T(8,128)(2,1)S(1)} %get-tuple-element.16), channel_id=1, source_target_pairs={{0,25},{1,24},{2,27},{3,26},{4,29},{5,28},{6,31},{7,30},{8,17},{9,... | collective-permute-start | bytes 49160 | tf_op jit(solution)/shard_map/ppermute | solution.py:495
  14.5 0.0 collective-permute-start.5
  14.5 2.0 %collective-permute-start.6 = (bf16[64,128]{1,0:T(8,128)(2,1)S(1)}, bf16[64,128]{1,0:T(8,128)(2,1)S(1)}, u32[]{:S(2)}, u32[]{:S(2)}) collective-permute-start(bf16[64,128]{1,0:T(8,128)(2,1)S(1)} %get-tuple-element.18), channel_id=1, source_target_pairs={{0,9},{1,8},{2,11},{3,10},{4,13},{5,12},{6,15},{7,14},{8,1},{9,0},... | collective-permute-start | bytes 49160 | tf_op jit(solution)/shard_map/ppermute | solution.py:495
  16.5 0.0 copy-done.5
  16.5 0.1 reshape.13
  16.6 0.1 reshape.14.refs_9_
  16.7 0.4 %shard_map.79 = (bf16[512,512]{1,0:T(8,128)(2,1)S(1)}, f32[4,128]{1,0:T(4,128)S(1)}) custom-call(s32[4,128]{1,0:T(4,128)S(1)} %copy-done.1, bf16[64,128]{1,0:T(8,128)(2,1)S(1)} %get-tuple-element.19.after_ref.refs_3_), custom_call_target="tpu_custom_call" | custom-call | tf_op jit(solution)/shard_map/pallas_call | solution.py:469
  17.1 0.6 %collective-permute-done.4.refs_0_ = bf16[64,128]{1,0:T(8,128)(2,1)S(1)} collective-permute-done((bf16[64,128]{1,0:T(8,128)(2,1)S(1)}, bf16[64,128]{1,0:T(8,128)(2,1)S(1)}, u32[]{:S(2)}, u32[]{:S(2)}) %collective-permute-start.4) | collective-permute-done | bytes 16416 | tf_op jit(solution)/shard_map/ppermute | solution.py:495
  17.7 1.5 %collective-permute-done.5.refs_1_ = bf16[64,128]{1,0:T(8,128)(2,1)S(1)} collective-permute-done((bf16[64,128]{1,0:T(8,128)(2,1)S(1)}, bf16[64,128]{1,0:T(8,128)(2,1)S(1)}, u32[]{:S(2)}, u32[]{:S(2)}) %collective-permute-start.5) | collective-permute-done | bytes 16416 | tf_op jit(solution)/shard_map/ppermute | solution.py:495
  19.2 0.0 collective-permute-done.6.refs_2_
  19.2 2.1 %shard_map.80 = (f32[3,8,128]{2,1,0:T(8,128)S(1)}, f32[8,2,16,128]{3,2,1,0:T(8,128)S(1)}) custom-call(bf16[64,128]{1,0:T(8,128)(2,1)S(1)} %collective-permute-done.4.refs_0_, bf16[64,128]{1,0:T(8,128)(2,1)S(1)} %collective-permute-done.5.refs_1_, bf16[64,128]{1,0:T(8,128)(2,1)S(1)} %collective-permute-done.6.refs_2_, ...), custom_call_target="tpu_custom_call" | custom-call | tf_op jit(solution)/shard_map/pallas_call | solution.py:469
  21.3 10.3 %all_to_all.5.recv_ref = f32[16,16,128]{2,1,0:T(8,128)S(1)} all-to-all(f32[16,16,128]{2,1,0:T(8,128)S(1)} %bitcast.5), channel_id=1, replica_groups={{0,2,4,6,8,10,12,14,17,19,21,23,25,27,29,31},{1,3,5,7,9,11,13,15,16,18,..., dimensions={0} | all-to-all | bytes 262144 | tf_op jit(solution)/shard_map/all_to_all | solution.py:520
  31.6 0.9 %collective-permute-start.7 = (f32[16,16,128]{2,1,0:T(8,128)S(1)}, f32[16,16,128]{2,1,0:T(8,128)S(1)}, u32[]{:S(2)}, u32[]{:S(2)}) collective-permute-start(f32[16,16,128]{2,1,0:T(8,128)S(1)} %all_to_all.5.recv_ref), channel_id=1, source_target_pairs={{0,1},{1,0},{2,3},{3,2},{4,5},{5,4},{6,7},{7,6},{8,9},{9,8},{10,11... | collective-permute-start | bytes 393224 | tf_op jit(solution)/shard_map/ppermute | solution.py:480
  32.4 0.9 %shard_map.81.sum_ref = f32[80,1024]{1,0:T(8,128)S(1)} custom-call(f32[16,16,128]{2,1,0:T(8,128)S(1)} %all_to_all.5.recv_ref), custom_call_target="tpu_custom_call" | custom-call | tf_op jit(solution)/shard_map/pallas_call | solution.py:469
  33.4 0.1 collective-permute-done.7.recv_ref
  33.4 1.6 %shard_map.82 = (f32[64,1024]{1,0:T(8,128)}, f32[3,4,256]{2,1,0:T(4,128)}) custom-call(f32[16,16,128]{2,1,0:T(8,128)S(1)} %collective-permute-done.7.recv_ref, f32[80,1024]{1,0:T(8,128)S(1)} %shard_map.81.sum_ref, f32[3,8,128]{2,1,0:T(8,128)S(1)} %get-tuple-element.25.spread_ref), custom_call_target="tpu_custom_call" | custom-call | tf_op jit(solution)/shard_map/pallas_call | solution.py:469
  (1 shorter events, 0.0 us)
Async XLA Ops:
  0.6 6.6 %copy-start.4 = (s32[4]{0:T(128)S(1)}, s32[4]{0:T(128)}, u32[]{:S(2)}) copy-start(s32[4]{0:T(128)} %cam_index_ref.1) | copy-start | bytes 52
  0.6 6.6 %copy-start.3 = (s32[4]{0:T(128)S(1)}, s32[4]{0:T(128)}, u32[]{:S(2)}) copy-start(s32[4]{0:T(128)} %tile_pos_ref.1) | copy-start | bytes 52
  0.7 11.0 %collective-permute-start.3 = (bf16[64,1024]{1,0:T(8,128)(2,1)}, bf16[64,1024]{1,0:T(8,128)(2,1)S(1)}, u32[]{:S(2)}, u32[]{:S(2)}) collective-permute-start(bf16[64,1024]{1,0:T(8,128)(2,1)} %params_ref.1), channel_id=1, source_target_pairs={{0,5},{1,4},{2,7},{3,6},{4,1},{5,0},{6,3},{7,2},{8,13},{9,12},{10,... | collective-permute-start | bytes 393224 | tf_op jit(solution)/shard_map/ppermute | solution.py:495
  3.1 6.6 %collective-permute-start.2 = (s32[4,128]{1,0:T(4,128)}, s32[4,128]{1,0:T(4,128)S(1)}, u32[]{:S(2)}, u32[]{:S(2)}) collective-permute-start(s32[4,128]{1,0:T(4,128)} %refs_4_.1), channel_id=1, source_target_pairs={{0,25},{1,24},{2,27},{3,26},{4,29},{5,28},{6,31},{7,30},{8,17},{9,... | collective-permute-start | bytes 6152 | tf_op jit(solution)/shard_map/ppermute | solution.py:495
  7.0 4.7 %collective-permute-start.1 = (s32[4,128]{1,0:T(4,128)}, s32[4,128]{1,0:T(4,128)S(1)}, u32[]{:S(2)}, u32[]{:S(2)}) collective-permute-start(s32[4,128]{1,0:T(4,128)} %refs_4_.1), channel_id=1, source_target_pairs={{0,16},{1,17},{2,18},{3,19},{4,20},{5,21},{6,22},{7,23},{8,24},{9,... | collective-permute-start | bytes 6152 | tf_op jit(solution)/shard_map/ppermute | solution.py:495
  7.0 4.7 %collective-permute-start = (s32[4,128]{1,0:T(4,128)}, s32[4,128]{1,0:T(4,128)S(1)}, u32[]{:S(2)}, u32[]{:S(2)}) collective-permute-start(s32[4,128]{1,0:T(4,128)} %refs_4_.1), channel_id=1, source_target_pairs={{0,9},{1,8},{2,11},{3,10},{4,13},{5,12},{6,15},{7,14},{8,1},{9,0},... | collective-permute-start | bytes 6152 | tf_op jit(solution)/shard_map/ppermute | solution.py:495
  7.3 0.9 %copy-start = (bf16[64,1024]{1,0:T(8,128)(2,1)S(1)}, bf16[64,1024]{1,0:T(8,128)(2,1)}, u32[]{:S(2)}) copy-start(bf16[64,1024]{1,0:T(8,128)(2,1)} %params_ref.1) | copy-start | bytes 393220
  8.2 0.7 %copy-start.2 = (f32[28,16]{0,1:T(8,128)S(1)}, f32[28,16]{0,1:T(8,128)}, u32[]{:S(2)}) copy-start(f32[28,16]{0,1:T(8,128)} %param.10) | copy-start | bytes 5380
  8.9 2.8 %copy-start.1 = (s32[4,128]{1,0:T(4,128)S(1)}, s32[4,128]{1,0:T(4,128)}, u32[]{:S(2)}) copy-start(s32[4,128]{1,0:T(4,128)} %refs_4_.1) | copy-start | bytes 6148
  11.7 4.9 %copy-start.5 = (f32[3,4,256]{2,1,0:T(4,128)S(1)}, f32[3,4,256]{2,1,0:T(4,128)}, u32[]{:S(2)}) copy-start(f32[3,4,256]{2,1,0:T(4,128)} %param.11) | copy-start | bytes 36868
  12.6 5.0 %collective-permute-start.4 = (bf16[64,128]{1,0:T(8,128)(2,1)S(1)}, bf16[64,128]{1,0:T(8,128)(2,1)S(1)}, u32[]{:S(2)}, u32[]{:S(2)}) collective-permute-start(bf16[64,128]{1,0:T(8,128)(2,1)S(1)} %get-tuple-element.16), channel_id=1, source_target_pairs={{0,25},{1,24},{2,27},{3,26},{4,29},{5,28},{6,31},{7,30},{8,17},{9,... | collective-permute-start | bytes 49160 | tf_op jit(solution)/shard_map/ppermute | solution.py:495
  14.5 4.6 %collective-permute-start.5 = (bf16[64,128]{1,0:T(8,128)(2,1)S(1)}, bf16[64,128]{1,0:T(8,128)(2,1)S(1)}, u32[]{:S(2)}, u32[]{:S(2)}) collective-permute-start(bf16[64,128]{1,0:T(8,128)(2,1)S(1)} %get-tuple-element.17), channel_id=1, source_target_pairs={{0,16},{1,17},{2,18},{3,19},{4,20},{5,21},{6,22},{7,23},{8,24},{9,... | collective-permute-start | bytes 49160 | tf_op jit(solution)/shard_map/ppermute | solution.py:495
  14.5 4.6 %collective-permute-start.6 = (bf16[64,128]{1,0:T(8,128)(2,1)S(1)}, bf16[64,128]{1,0:T(8,128)(2,1)S(1)}, u32[]{:S(2)}, u32[]{:S(2)}) collective-permute-start(bf16[64,128]{1,0:T(8,128)(2,1)S(1)} %get-tuple-element.18), channel_id=1, source_target_pairs={{0,9},{1,8},{2,11},{3,10},{4,13},{5,12},{6,15},{7,14},{8,1},{9,0},... | collective-permute-start | bytes 49160 | tf_op jit(solution)/shard_map/ppermute | solution.py:495
  31.6 1.8 %collective-permute-start.7 = (f32[16,16,128]{2,1,0:T(8,128)S(1)}, f32[16,16,128]{2,1,0:T(8,128)S(1)}, u32[]{:S(2)}, u32[]{:S(2)}) collective-permute-start(f32[16,16,128]{2,1,0:T(8,128)S(1)} %all_to_all.5.recv_ref), channel_id=1, source_target_pairs={{0,1},{1,0},{2,3},{3,2},{4,5},{5,4},{6,7},{7,6},{8,9},{9,8},{10,11... | collective-permute-start | bytes 393224 | tf_op jit(solution)/shard_map/ppermute | solution.py:480

commit v11 on v10

--- a/solution.py
+++ b/solution.py
@@ -336,12 +336,17 @@
     sums = [down(index) for index in range(6)]
     g_x = sums[0] * dx
     sums = sums + [g_x, g_x * dx, sums[1] * dx]
-    wide = jnp.concatenate([jnp.concatenate(split(s, 2), axis=1) for s in sums], axis=0)
-    gather = one_hot(iota((8, 2 * LANES), 0) == (iota((8, 2 * LANES), 1) % LANES) // share)
-    reduced = dot(gather, wide, 1, 1)
-    g_0, g_y, g_yy, s_0, s_1, s_2, g_x, g_xx, g_xy = [
-        reduced[:tiles, q * length : (q + 1) * length] for q in range(len(sums))
-    ]
+    def over_lanes(x):
+        x = x.T
+        return jnp.concatenate(
+            [
+                jnp.sum(x[t * share : (t + 1) * share], axis=0, keepdims=True)
+                for t in range(tiles)
+            ],
+            axis=0,
+        )
+
+    g_0, g_y, g_yy, s_0, s_1, s_2, g_x, g_xx, g_xy = [over_lanes(s) for s in sums]
 
     d_colors = [s_0, s_1, s_2]
     d_terms = []

time: 35.3 us -> 35.2 us (level)
  no operation moved by 1% of the time
where the time goes in v11:
time: 35.2 us; the launch traced here: 34.9 us
  starting transfers between devices  11.4 us (32%)
  blocking collectives  10.3 us (29%)
  Pallas kernels  6.62 us (19%)
  waiting for transfers between devices  4.18 us (12%)
  local copies, waits for them, and re-layouts  1.8 us (5%)
  between operations  0.72 us (2%)
    ppermute x7, starting transfers between devices, reach(): return lax.ppermute(x, ('gauss', 'view'), pairs)  10.5 us
    all_to_all x1, blocking collectives, exchange_wide(): lax.all_to_all(blocks, ('gauss', 'view'), split_axis=0, concat_axis=0, ax...  10.3 us
    pallas_call x6, Pallas kernels, call(): pl.pallas_call(kernel, out_shape=out_shape, in_specs=in_specs, out_specs=...  6.62 us
    ppermute x7, waiting for transfers between devices, reach(): return lax.ppermute(x, ('gauss', 'view'), pairs)  4.12 us
    unnamed x12, local copies, waits for them, and re-layouts  1.62 us
    ppermute x1, starting transfers between devices, swap(): lax.ppermute(x, axis, [(i, i ^ k) for i in range(lax.axis_size(axis))])  0.86 us
  transfers between devices with their start and end apart: 8, of which 4 were waited for; matrix products, arithmetic and copies ran while one was open for 1% of the time, Pallas kernels for 6%

profile of v11, /device:TPU:0, one launch (start us, length us, event | category | flops | bytes accessed | tf_op | source)
XLA Modules:
  0.0 34.9 jit_solution(4643995821004049530)
XLA Ops:
  0.6 0.0 copy-start.4
  0.6 0.0 copy-start.3
  0.7 2.4 %collective-permute-start.3 = (bf16[64,1024]{1,0:T(8,128)(2,1)}, bf16[64,1024]{1,0:T(8,128)(2,1)S(1)}, u32[]{:S(2)}, u32[]{:S(2)}) collective-permute-start(bf16[64,1024]{1,0:T(8,128)(2,1)} %params_ref.1), channel_id=1, source_target_pairs={{0,5},{1,4},{2,7},{3,6},{4,1},{5,0},{6,3},{7,2},{8,13},{9,12},{10,... | collective-permute-start | bytes 393224 | tf_op jit(solution)/shard_map/ppermute | solution.py:500
  3.1 3.9 %collective-permute-start.2 = (s32[4,128]{1,0:T(4,128)}, s32[4,128]{1,0:T(4,128)S(1)}, u32[]{:S(2)}, u32[]{:S(2)}) collective-permute-start(s32[4,128]{1,0:T(4,128)} %refs_4_.1), channel_id=1, source_target_pairs={{0,25},{1,24},{2,27},{3,26},{4,29},{5,28},{6,31},{7,30},{8,17},{9,... | collective-permute-start | bytes 6152 | tf_op jit(solution)/shard_map/ppermute | solution.py:500
  7.0 0.0 collective-permute-start.1
  7.0 0.3 collective-permute-start
  7.3 0.0 copy-done.4
  7.3 0.0 copy-done.3
  7.3 0.0 copy-start
  7.3 0.9 %copy-done = bf16[64,1024]{1,0:T(8,128)(2,1)S(1)} copy-done((bf16[64,1024]{1,0:T(8,128)(2,1)S(1)}, bf16[64,1024]{1,0:T(8,128)(2,1)}, u32[]{:S(2)}) %copy-start) | copy-done | bytes 131096
  8.2 0.0 copy-start.2
  8.2 0.7 %copy-done.2 = f32[28,16]{0,1:T(8,128)S(1)} copy-done((f32[28,16]{0,1:T(8,128)S(1)}, f32[28,16]{0,1:T(8,128)}, u32[]{:S(2)}) %copy-start.2) | copy-done | bytes 1816
  8.9 0.0 copy-start.1
  8.9 0.8 %shard_map.77 = (bf16[64,1024]{1,0:T(8,128)(2,1)S(1)}, f32[28,4,128]{2,1,0:T(4,128)S(1)}, f32[2,8,128]{2,1,0:T(8,128)S(1)}) custom-call(s32[4]{0:T(128)S(1)} %copy-done.3, s32[4]{0:T(128)S(1)} %copy-done.4, f32[16,28]{1,0:T(8,128)S(1)} %bitcast.6, bf16[64,1024]{1,0:T(8,128)(2,1)S(1)} %copy-done), custom_call_target="tpu_custom_call" | custom-call | tf_op jit(solution)/shard_map/pallas_call | solution.py:474
  9.6 0.0 collective-permute-done.2.refs_3_
  9.7 2.0 %collective-permute-done.1.refs_2_ = s32[4,128]{1,0:T(4,128)S(1)} collective-permute-done((s32[4,128]{1,0:T(4,128)}, s32[4,128]{1,0:T(4,128)S(1)}, u32[]{:S(2)}, u32[]{:S(2)}) %collective-permute-start.1) | collective-permute-done | bytes 2080 | tf_op jit(solution)/shard_map/ppermute | solution.py:500
  11.7 0.0 collective-permute-done.refs_1_
  11.7 0.0 collective-permute-done.3.refs_5_
  11.7 0.0 copy-done.1
  11.7 0.0 copy-start.5
  11.7 0.9 %shard_map.78 = (bf16[64,128]{1,0:T(8,128)(2,1)S(1)}, bf16[64,128]{1,0:T(8,128)(2,1)S(1)}, bf16[64,128]{1,0:T(8,128)(2,1)S(1)}, bf16[64,128]{1,0:T(8,128)(2,1)S(1)}) custom-call(s32[4,128]{1,0:T(4,128)S(1)} %copy-done.1, s32[4,128]{1,0:T(4,128)S(1)} %collective-permute-done.refs_1_, s32[4,128]{1,0:T(4,128)S(1)} %collective-permute-done.1.refs_2_, ...), custom_call_target="tpu_custom_call" | custom-call | tf_op jit(solution)/shard_map/pallas_call | solution.py:474
  12.6 1.9 %collective-permute-start.4 = (bf16[64,128]{1,0:T(8,128)(2,1)S(1)}, bf16[64,128]{1,0:T(8,128)(2,1)S(1)}, u32[]{:S(2)}, u32[]{:S(2)}) collective-permute-start(bf16[64,128]{1,0:T(8,128)(2,1)S(1)} %get-tuple-element.16), channel_id=1, source_target_pairs={{0,25},{1,24},{2,27},{3,26},{4,29},{5,28},{6,31},{7,30},{8,17},{9,... | collective-permute-start | bytes 49160 | tf_op jit(solution)/shard_map/ppermute | solution.py:500
  14.5 0.0 collective-permute-start.5
  14.5 2.0 %collective-permute-start.6 = (bf16[64,128]{1,0:T(8,128)(2,1)S(1)}, bf16[64,128]{1,0:T(8,128)(2,1)S(1)}, u32[]{:S(2)}, u32[]{:S(2)}) collective-permute-start(bf16[64,128]{1,0:T(8,128)(2,1)S(1)} %get-tuple-element.18), channel_id=1, source_target_pairs={{0,9},{1,8},{2,11},{3,10},{4,13},{5,12},{6,15},{7,14},{8,1},{9,0},... | collective-permute-start | bytes 49160 | tf_op jit(solution)/shard_map/ppermute | solution.py:500
  16.5 0.0 copy-done.5
  16.5 0.1 reshape.13
  16.6 0.1 reshape.14.refs_9_
  16.7 0.4 %shard_map.79 = (bf16[512,512]{1,0:T(8,128)(2,1)S(1)}, f32[4,128]{1,0:T(4,128)S(1)}) custom-call(s32[4,128]{1,0:T(4,128)S(1)} %copy-done.1, bf16[64,128]{1,0:T(8,128)(2,1)S(1)} %get-tuple-element.19.after_ref.refs_3_), custom_call_target="tpu_custom_call" | custom-call | tf_op jit(solution)/shard_map/pallas_call | solution.py:474
  17.1 0.6 %collective-permute-done.4.refs_0_ = bf16[64,128]{1,0:T(8,128)(2,1)S(1)} collective-permute-done((bf16[64,128]{1,0:T(8,128)(2,1)S(1)}, bf16[64,128]{1,0:T(8,128)(2,1)S(1)}, u32[]{:S(2)}, u32[]{:S(2)}) %collective-permute-start.4) | collective-permute-done | bytes 16416 | tf_op jit(solution)/shard_map/ppermute | solution.py:500
  17.7 1.5 %collective-permute-done.5.refs_1_ = bf16[64,128]{1,0:T(8,128)(2,1)S(1)} collective-permute-done((bf16[64,128]{1,0:T(8,128)(2,1)S(1)}, bf16[64,128]{1,0:T(8,128)(2,1)S(1)}, u32[]{:S(2)}, u32[]{:S(2)}) %collective-permute-start.5) | collective-permute-done | bytes 16416 | tf_op jit(solution)/shard_map/ppermute | solution.py:500
  19.2 0.0 collective-permute-done.6.refs_2_
  19.2 2.0 %shard_map.80 = (f32[3,8,128]{2,1,0:T(8,128)S(1)}, f32[8,2,16,128]{3,2,1,0:T(8,128)S(1)}) custom-call(bf16[64,128]{1,0:T(8,128)(2,1)S(1)} %collective-permute-done.4.refs_0_, bf16[64,128]{1,0:T(8,128)(2,1)S(1)} %collective-permute-done.5.refs_1_, bf16[64,128]{1,0:T(8,128)(2,1)S(1)} %collective-permute-done.6.refs_2_, ...), custom_call_target="tpu_custom_call" | custom-call | tf_op jit(solution)/shard_map/pallas_call | solution.py:474
  21.2 10.3 %all_to_all.5.recv_ref = f32[16,16,128]{2,1,0:T(8,128)S(1)} all-to-all(f32[16,16,128]{2,1,0:T(8,128)S(1)} %bitcast.5), channel_id=1, replica_groups={{0,2,4,6,8,10,12,14,17,19,21,23,25,27,29,31},{1,3,5,7,9,11,13,15,16,18,..., dimensions={0} | all-to-all | bytes 262144 | tf_op jit(solution)/shard_map/all_to_all | solution.py:525
  31.5 0.9 %collective-permute-start.7 = (f32[16,16,128]{2,1,0:T(8,128)S(1)}, f32[16,16,128]{2,1,0:T(8,128)S(1)}, u32[]{:S(2)}, u32[]{:S(2)}) collective-permute-start(f32[16,16,128]{2,1,0:T(8,128)S(1)} %all_to_all.5.recv_ref), channel_id=1, source_target_pairs={{0,1},{1,0},{2,3},{3,2},{4,5},{5,4},{6,7},{7,6},{8,9},{9,8},{10,11... | collective-permute-start | bytes 393224 | tf_op jit(solution)/shard_map/ppermute | solution.py:485
  32.3 0.9 %shard_map.81.sum_ref = f32[80,1024]{1,0:T(8,128)S(1)} custom-call(f32[16,16,128]{2,1,0:T(8,128)S(1)} %all_to_all.5.recv_ref), custom_call_target="tpu_custom_call" | custom-call | tf_op jit(solution)/shard_map/pallas_call | solution.py:474
  33.3 0.1 collective-permute-done.7.recv_ref
  33.3 1.6 %shard_map.82 = (f32[64,1024]{1,0:T(8,128)}, f32[3,4,256]{2,1,0:T(4,128)}) custom-call(f32[16,16,128]{2,1,0:T(8,128)S(1)} %collective-permute-done.7.recv_ref, f32[80,1024]{1,0:T(8,128)S(1)} %shard_map.81.sum_ref, f32[3,8,128]{2,1,0:T(8,128)S(1)} %get-tuple-element.25.spread_ref), custom_call_target="tpu_custom_call" | custom-call | tf_op jit(solution)/shard_map/pallas_call | solution.py:474
  (1 shorter events, 0.0 us)
Async XLA Ops:
  0.6 6.6 %copy-start.4 = (s32[4]{0:T(128)S(1)}, s32[4]{0:T(128)}, u32[]{:S(2)}) copy-start(s32[4]{0:T(128)} %cam_index_ref.1) | copy-start | bytes 52
  0.6 6.6 %copy-start.3 = (s32[4]{0:T(128)S(1)}, s32[4]{0:T(128)}, u32[]{:S(2)}) copy-start(s32[4]{0:T(128)} %tile_pos_ref.1) | copy-start | bytes 52
  0.7 11.0 %collective-permute-start.3 = (bf16[64,1024]{1,0:T(8,128)(2,1)}, bf16[64,1024]{1,0:T(8,128)(2,1)S(1)}, u32[]{:S(2)}, u32[]{:S(2)}) collective-permute-start(bf16[64,1024]{1,0:T(8,128)(2,1)} %params_ref.1), channel_id=1, source_target_pairs={{0,5},{1,4},{2,7},{3,6},{4,1},{5,0},{6,3},{7,2},{8,13},{9,12},{10,... | collective-permute-start | bytes 393224 | tf_op jit(solution)/shard_map/ppermute | solution.py:500
  3.1 6.6 %collective-permute-start.2 = (s32[4,128]{1,0:T(4,128)}, s32[4,128]{1,0:T(4,128)S(1)}, u32[]{:S(2)}, u32[]{:S(2)}) collective-permute-start(s32[4,128]{1,0:T(4,128)} %refs_4_.1), channel_id=1, source_target_pairs={{0,25},{1,24},{2,27},{3,26},{4,29},{5,28},{6,31},{7,30},{8,17},{9,... | collective-permute-start | bytes 6152 | tf_op jit(solution)/shard_map/ppermute | solution.py:500
  7.0 4.7 %collective-permute-start.1 = (s32[4,128]{1,0:T(4,128)}, s32[4,128]{1,0:T(4,128)S(1)}, u32[]{:S(2)}, u32[]{:S(2)}) collective-permute-start(s32[4,128]{1,0:T(4,128)} %refs_4_.1), channel_id=1, source_target_pairs={{0,16},{1,17},{2,18},{3,19},{4,20},{5,21},{6,22},{7,23},{8,24},{9,... | collective-permute-start | bytes 6152 | tf_op jit(solution)/shard_map/ppermute | solution.py:500
  7.0 4.7 %collective-permute-start = (s32[4,128]{1,0:T(4,128)}, s32[4,128]{1,0:T(4,128)S(1)}, u32[]{:S(2)}, u32[]{:S(2)}) collective-permute-start(s32[4,128]{1,0:T(4,128)} %refs_4_.1), channel_id=1, source_target_pairs={{0,9},{1,8},{2,11},{3,10},{4,13},{5,12},{6,15},{7,14},{8,1},{9,0},... | collective-permute-start | bytes 6152 | tf_op jit(solution)/shard_map/ppermute | solution.py:500
  7.3 0.9 %copy-start = (bf16[64,1024]{1,0:T(8,128)(2,1)S(1)}, bf16[64,1024]{1,0:T(8,128)(2,1)}, u32[]{:S(2)}) copy-start(bf16[64,1024]{1,0:T(8,128)(2,1)} %params_ref.1) | copy-start | bytes 393220
  8.2 0.7 %copy-start.2 = (f32[28,16]{0,1:T(8,128)S(1)}, f32[28,16]{0,1:T(8,128)}, u32[]{:S(2)}) copy-start(f32[28,16]{0,1:T(8,128)} %param.10) | copy-start | bytes 5380
  8.9 2.8 %copy-start.1 = (s32[4,128]{1,0:T(4,128)S(1)}, s32[4,128]{1,0:T(4,128)}, u32[]{:S(2)}) copy-start(s32[4,128]{1,0:T(4,128)} %refs_4_.1) | copy-start | bytes 6148
  11.7 4.9 %copy-start.5 = (f32[3,4,256]{2,1,0:T(4,128)S(1)}, f32[3,4,256]{2,1,0:T(4,128)}, u32[]{:S(2)}) copy-start(f32[3,4,256]{2,1,0:T(4,128)} %param.11) | copy-start | bytes 36868
  12.6 5.0 %collective-permute-start.4 = (bf16[64,128]{1,0:T(8,128)(2,1)S(1)}, bf16[64,128]{1,0:T(8,128)(2,1)S(1)}, u32[]{:S(2)}, u32[]{:S(2)}) collective-permute-start(bf16[64,128]{1,0:T(8,128)(2,1)S(1)} %get-tuple-element.16), channel_id=1, source_target_pairs={{0,25},{1,24},{2,27},{3,26},{4,29},{5,28},{6,31},{7,30},{8,17},{9,... | collective-permute-start | bytes 49160 | tf_op jit(solution)/shard_map/ppermute | solution.py:500
  14.5 4.6 %collective-permute-start.5 = (bf16[64,128]{1,0:T(8,128)(2,1)S(1)}, bf16[64,128]{1,0:T(8,128)(2,1)S(1)}, u32[]{:S(2)}, u32[]{:S(2)}) collective-permute-start(bf16[64,128]{1,0:T(8,128)(2,1)S(1)} %get-tuple-element.17), channel_id=1, source_target_pairs={{0,16},{1,17},{2,18},{3,19},{4,20},{5,21},{6,22},{7,23},{8,24},{9,... | collective-permute-start | bytes 49160 | tf_op jit(solution)/shard_map/ppermute | solution.py:500
  14.5 4.6 %collective-permute-start.6 = (bf16[64,128]{1,0:T(8,128)(2,1)S(1)}, bf16[64,128]{1,0:T(8,128)(2,1)S(1)}, u32[]{:S(2)}, u32[]{:S(2)}) collective-permute-start(bf16[64,128]{1,0:T(8,128)(2,1)S(1)} %get-tuple-element.18), channel_id=1, source_target_pairs={{0,9},{1,8},{2,11},{3,10},{4,13},{5,12},{6,15},{7,14},{8,1},{9,0},... | collective-permute-start | bytes 49160 | tf_op jit(solution)/shard_map/ppermute | solution.py:500
  31.5 1.8 %collective-permute-start.7 = (f32[16,16,128]{2,1,0:T(8,128)S(1)}, f32[16,16,128]{2,1,0:T(8,128)S(1)}, u32[]{:S(2)}, u32[]{:S(2)}) collective-permute-start(f32[16,16,128]{2,1,0:T(8,128)S(1)} %all_to_all.5.recv_ref), channel_id=1, source_target_pairs={{0,1},{1,0},{2,3},{3,2},{4,5},{5,4},{6,7},{7,6},{8,9},{9,8},{10,11... | collective-permute-start | bytes 393224 | tf_op jit(solution)/shard_map/ppermute | solution.py:485

commit v12 on v11

--- a/solution.py
+++ b/solution.py
@@ -372,13 +372,13 @@
         rows_ref[pl.ds(v, tiles, stride=width), :] = values[v]
     by_slot = jnp.concatenate(
         [
-            jnp.concatenate(split(rows_ref[t * width : t * width + SENT, :], 3), axis=0)
+            jnp.concatenate(split(rows_ref[t * width : t * width + SENT, :], 2), axis=0)
             for t in range(tiles)
         ],
         axis=1,
     )
     by_slot = dot(by_slot, hot, 1, 1)
-    by_slot = by_slot[:SENT] + by_slot[SENT : 2 * SENT] + by_slot[2 * SENT :]
+    by_slot = by_slot[:SENT] + by_slot[SENT:]
     owners, copies, high, _ = send_ref.shape
     cap = hot.shape[0] // owners
     for o in range(owners):
@@ -617,7 +617,7 @@
         total = call(
             functools.partial(first_kernel, cap), shape((SENT + 48, g_dev), F32), (received,)
         )
-        parts = 4
+        parts = 2
         grads, pictures = call(
             functools.partial(last_kernel, cap),
             [shape((width, g_dev), F32), shape(targets.shape, F32)],

time: 35.2 us -> 35.2 us (level)
  no operation moved by 1% of the time
where the time goes in v12:
time: 35.2 us; the launch traced here: 34.9 us
  starting transfers between devices  11.4 us (32%)
  blocking collectives  10.3 us (29%)
  Pallas kernels  6.61 us (19%)
  waiting for transfers between devices  4.18 us (12%)
  local copies, waits for them, and re-layouts  1.8 us (5%)
  between operations  0.72 us (2%)
    ppermute x7, starting transfers between devices, reach(): return lax.ppermute(x, ('gauss', 'view'), pairs)  10.5 us
    all_to_all x1, blocking collectives, exchange_wide(): lax.all_to_all(blocks, ('gauss', 'view'), split_axis=0, concat_axis=0, ax...  10.3 us
    pallas_call x6, Pallas kernels, call(): pl.pallas_call(kernel, out_shape=out_shape, in_specs=in_specs, out_specs=...  6.61 us
    ppermute x7, waiting for transfers between devices, reach(): return lax.ppermute(x, ('gauss', 'view'), pairs)  4.12 us
    unnamed x12, local copies, waits for them, and re-layouts  1.62 us
    ppermute x1, starting transfers between devices, swap(): lax.ppermute(x, axis, [(i, i ^ k) for i in range(lax.axis_size(axis))])  0.86 us
  transfers between devices with their start and end apart: 8, of which 4 were waited for; matrix products, arithmetic and copies ran while one was open for 1% of the time, Pallas kernels for 6%

profile of v12, /device:TPU:0, one launch (start us, length us, event | category | flops | bytes accessed | tf_op | source)
XLA Modules:
  0.0 34.9 jit_solution(12769957649070168576)
XLA Ops:
  0.6 0.0 copy-start.4
  0.6 0.0 copy-start.3
  0.7 2.4 %collective-permute-start.3 = (bf16[64,1024]{1,0:T(8,128)(2,1)}, bf16[64,1024]{1,0:T(8,128)(2,1)S(1)}, u32[]{:S(2)}, u32[]{:S(2)}) collective-permute-start(bf16[64,1024]{1,0:T(8,128)(2,1)} %params_ref.1), channel_id=1, source_target_pairs={{0,5},{1,4},{2,7},{3,6},{4,1},{5,0},{6,3},{7,2},{8,13},{9,12},{10,... | collective-permute-start | bytes 393224 | tf_op jit(solution)/shard_map/ppermute | solution.py:500
  3.1 3.9 %collective-permute-start.2 = (s32[4,128]{1,0:T(4,128)}, s32[4,128]{1,0:T(4,128)S(1)}, u32[]{:S(2)}, u32[]{:S(2)}) collective-permute-start(s32[4,128]{1,0:T(4,128)} %refs_4_.1), channel_id=1, source_target_pairs={{0,25},{1,24},{2,27},{3,26},{4,29},{5,28},{6,31},{7,30},{8,17},{9,... | collective-permute-start | bytes 6152 | tf_op jit(solution)/shard_map/ppermute | solution.py:500
  7.0 0.0 collective-permute-start.1
  7.0 0.3 collective-permute-start
  7.3 0.0 copy-done.4
  7.3 0.0 copy-done.3
  7.3 0.0 copy-start
  7.3 0.9 %copy-done = bf16[64,1024]{1,0:T(8,128)(2,1)S(1)} copy-done((bf16[64,1024]{1,0:T(8,128)(2,1)S(1)}, bf16[64,1024]{1,0:T(8,128)(2,1)}, u32[]{:S(2)}) %copy-start) | copy-done | bytes 131096
  8.2 0.0 copy-start.2
  8.2 0.7 %copy-done.2 = f32[28,16]{0,1:T(8,128)S(1)} copy-done((f32[28,16]{0,1:T(8,128)S(1)}, f32[28,16]{0,1:T(8,128)}, u32[]{:S(2)}) %copy-start.2) | copy-done | bytes 1816
  8.9 0.0 copy-start.1
  8.9 0.8 %shard_map.77 = (bf16[64,1024]{1,0:T(8,128)(2,1)S(1)}, f32[28,4,128]{2,1,0:T(4,128)S(1)}, f32[2,8,128]{2,1,0:T(8,128)S(1)}) custom-call(s32[4]{0:T(128)S(1)} %copy-done.3, s32[4]{0:T(128)S(1)} %copy-done.4, f32[16,28]{1,0:T(8,128)S(1)} %bitcast.6, bf16[64,1024]{1,0:T(8,128)(2,1)S(1)} %copy-done), custom_call_target="tpu_custom_call" | custom-call | tf_op jit(solution)/shard_map/pallas_call | solution.py:474
  9.6 0.0 collective-permute-done.2.refs_3_
  9.7 2.0 %collective-permute-done.1.refs_2_ = s32[4,128]{1,0:T(4,128)S(1)} collective-permute-done((s32[4,128]{1,0:T(4,128)}, s32[4,128]{1,0:T(4,128)S(1)}, u32[]{:S(2)}, u32[]{:S(2)}) %collective-permute-start.1) | collective-permute-done | bytes 2080 | tf_op jit(solution)/shard_map/ppermute | solution.py:500
  11.7 0.0 collective-permute-done.refs_1_
  11.7 0.0 collective-permute-done.3.refs_5_
  11.7 0.0 copy-done.1
  11.7 0.0 copy-start.5
  11.7 0.9 %shard_map.78 = (bf16[64,128]{1,0:T(8,128)(2,1)S(1)}, bf16[64,128]{1,0:T(8,128)(2,1)S(1)}, bf16[64,128]{1,0:T(8,128)(2,1)S(1)}, bf16[64,128]{1,0:T(8,128)(2,1)S(1)}) custom-call(s32[4,128]{1,0:T(4,128)S(1)} %copy-done.1, s32[4,128]{1,0:T(4,128)S(1)} %collective-permute-done.refs_1_, s32[4,128]{1,0:T(4,128)S(1)} %collective-permute-done.1.refs_2_, ...), custom_call_target="tpu_custom_call" | custom-call | tf_op jit(solution)/shard_map/pallas_call | solution.py:474
  12.6 1.9 %collective-permute-start.4 = (bf16[64,128]{1,0:T(8,128)(2,1)S(1)}, bf16[64,128]{1,0:T(8,128)(2,1)S(1)}, u32[]{:S(2)}, u32[]{:S(2)}) collective-permute-start(bf16[64,128]{1,0:T(8,128)(2,1)S(1)} %get-tuple-element.16), channel_id=1, source_target_pairs={{0,25},{1,24},{2,27},{3,26},{4,29},{5,28},{6,31},{7,30},{8,17},{9,... | collective-permute-start | bytes 49160 | tf_op jit(solution)/shard_map/ppermute | solution.py:500
  14.5 0.0 collective-permute-start.5
  14.5 2.0 %collective-permute-start.6 = (bf16[64,128]{1,0:T(8,128)(2,1)S(1)}, bf16[64,128]{1,0:T(8,128)(2,1)S(1)}, u32[]{:S(2)}, u32[]{:S(2)}) collective-permute-start(bf16[64,128]{1,0:T(8,128)(2,1)S(1)} %get-tuple-element.18), channel_id=1, source_target_pairs={{0,9},{1,8},{2,11},{3,10},{4,13},{5,12},{6,15},{7,14},{8,1},{9,0},... | collective-permute-start | bytes 49160 | tf_op jit(solution)/shard_map/ppermute | solution.py:500
  16.5 0.0 copy-done.5
  16.5 0.1 reshape.13
  16.6 0.1 reshape.14.refs_9_
  16.7 0.4 %shard_map.79 = (bf16[512,512]{1,0:T(8,128)(2,1)S(1)}, f32[4,128]{1,0:T(4,128)S(1)}) custom-call(s32[4,128]{1,0:T(4,128)S(1)} %copy-done.1, bf16[64,128]{1,0:T(8,128)(2,1)S(1)} %get-tuple-element.19.after_ref.refs_3_), custom_call_target="tpu_custom_call" | custom-call | tf_op jit(solution)/shard_map/pallas_call | solution.py:474
  17.1 0.6 %collective-permute-done.4.refs_0_ = bf16[64,128]{1,0:T(8,128)(2,1)S(1)} collective-permute-done((bf16[64,128]{1,0:T(8,128)(2,1)S(1)}, bf16[64,128]{1,0:T(8,128)(2,1)S(1)}, u32[]{:S(2)}, u32[]{:S(2)}) %collective-permute-start.4) | collective-permute-done | bytes 16416 | tf_op jit(solution)/shard_map/ppermute | solution.py:500
  17.7 1.5 %collective-permute-done.5.refs_1_ = bf16[64,128]{1,0:T(8,128)(2,1)S(1)} collective-permute-done((bf16[64,128]{1,0:T(8,128)(2,1)S(1)}, bf16[64,128]{1,0:T(8,128)(2,1)S(1)}, u32[]{:S(2)}, u32[]{:S(2)}) %collective-permute-start.5) | collective-permute-done | bytes 16416 | tf_op jit(solution)/shard_map/ppermute | solution.py:500
  19.2 0.0 collective-permute-done.6.refs_2_
  19.2 2.0 %shard_map.80 = (f32[3,8,128]{2,1,0:T(8,128)S(1)}, f32[8,2,16,128]{3,2,1,0:T(8,128)S(1)}) custom-call(bf16[64,128]{1,0:T(8,128)(2,1)S(1)} %collective-permute-done.4.refs_0_, bf16[64,128]{1,0:T(8,128)(2,1)S(1)} %collective-permute-done.5.refs_1_, bf16[64,128]{1,0:T(8,128)(2,1)S(1)} %collective-permute-done.6.refs_2_, ...), custom_call_target="tpu_custom_call" | custom-call | tf_op jit(solution)/shard_map/pallas_call | solution.py:474
  21.2 10.3 %all_to_all.5.recv_ref = f32[16,16,128]{2,1,0:T(8,128)S(1)} all-to-all(f32[16,16,128]{2,1,0:T(8,128)S(1)} %bitcast.5), channel_id=1, replica_groups={{0,2,4,6,8,10,12,14,17,19,21,23,25,27,29,31},{1,3,5,7,9,11,13,15,16,18,..., dimensions={0} | all-to-all | bytes 262144 | tf_op jit(solution)/shard_map/all_to_all | solution.py:525
  31.5 0.9 %collective-permute-start.7 = (f32[16,16,128]{2,1,0:T(8,128)S(1)}, f32[16,16,128]{2,1,0:T(8,128)S(1)}, u32[]{:S(2)}, u32[]{:S(2)}) collective-permute-start(f32[16,16,128]{2,1,0:T(8,128)S(1)} %all_to_all.5.recv_ref), channel_id=1, source_target_pairs={{0,1},{1,0},{2,3},{3,2},{4,5},{5,4},{6,7},{7,6},{8,9},{9,8},{10,11... | collective-permute-start | bytes 393224 | tf_op jit(solution)/shard_map/ppermute | solution.py:485
  32.3 0.9 %shard_map.81.sum_ref = f32[80,1024]{1,0:T(8,128)S(1)} custom-call(f32[16,16,128]{2,1,0:T(8,128)S(1)} %all_to_all.5.recv_ref), custom_call_target="tpu_custom_call" | custom-call | tf_op jit(solution)/shard_map/pallas_call | solution.py:474
  33.2 0.1 collective-permute-done.7.recv_ref
  33.3 1.6 %shard_map.82 = (f32[64,1024]{1,0:T(8,128)}, f32[3,4,256]{2,1,0:T(4,128)}) custom-call(f32[16,16,128]{2,1,0:T(8,128)S(1)} %collective-permute-done.7.recv_ref, f32[80,1024]{1,0:T(8,128)S(1)} %shard_map.81.sum_ref, f32[3,8,128]{2,1,0:T(8,128)S(1)} %get-tuple-element.25.spread_ref), custom_call_target="tpu_custom_call" | custom-call | tf_op jit(solution)/shard_map/pallas_call | solution.py:474
  (1 shorter events, 0.0 us)
Async XLA Ops:
  0.6 6.6 %copy-start.4 = (s32[4]{0:T(128)S(1)}, s32[4]{0:T(128)}, u32[]{:S(2)}) copy-start(s32[4]{0:T(128)} %cam_index_ref.1) | copy-start | bytes 52
  0.6 6.6 %copy-start.3 = (s32[4]{0:T(128)S(1)}, s32[4]{0:T(128)}, u32[]{:S(2)}) copy-start(s32[4]{0:T(128)} %tile_pos_ref.1) | copy-start | bytes 52
  0.7 11.0 %collective-permute-start.3 = (bf16[64,1024]{1,0:T(8,128)(2,1)}, bf16[64,1024]{1,0:T(8,128)(2,1)S(1)}, u32[]{:S(2)}, u32[]{:S(2)}) collective-permute-start(bf16[64,1024]{1,0:T(8,128)(2,1)} %params_ref.1), channel_id=1, source_target_pairs={{0,5},{1,4},{2,7},{3,6},{4,1},{5,0},{6,3},{7,2},{8,13},{9,12},{10,... | collective-permute-start | bytes 393224 | tf_op jit(solution)/shard_map/ppermute | solution.py:500
  3.1 6.6 %collective-permute-start.2 = (s32[4,128]{1,0:T(4,128)}, s32[4,128]{1,0:T(4,128)S(1)}, u32[]{:S(2)}, u32[]{:S(2)}) collective-permute-start(s32[4,128]{1,0:T(4,128)} %refs_4_.1), channel_id=1, source_target_pairs={{0,25},{1,24},{2,27},{3,26},{4,29},{5,28},{6,31},{7,30},{8,17},{9,... | collective-permute-start | bytes 6152 | tf_op jit(solution)/shard_map/ppermute | solution.py:500
  7.0 4.7 %collective-permute-start.1 = (s32[4,128]{1,0:T(4,128)}, s32[4,128]{1,0:T(4,128)S(1)}, u32[]{:S(2)}, u32[]{:S(2)}) collective-permute-start(s32[4,128]{1,0:T(4,128)} %refs_4_.1), channel_id=1, source_target_pairs={{0,16},{1,17},{2,18},{3,19},{4,20},{5,21},{6,22},{7,23},{8,24},{9,... | collective-permute-start | bytes 6152 | tf_op jit(solution)/shard_map/ppermute | solution.py:500
  7.0 4.7 %collective-permute-start = (s32[4,128]{1,0:T(4,128)}, s32[4,128]{1,0:T(4,128)S(1)}, u32[]{:S(2)}, u32[]{:S(2)}) collective-permute-start(s32[4,128]{1,0:T(4,128)} %refs_4_.1), channel_id=1, source_target_pairs={{0,9},{1,8},{2,11},{3,10},{4,13},{5,12},{6,15},{7,14},{8,1},{9,0},... | collective-permute-start | bytes 6152 | tf_op jit(solution)/shard_map/ppermute | solution.py:500
  7.3 0.9 %copy-start = (bf16[64,1024]{1,0:T(8,128)(2,1)S(1)}, bf16[64,1024]{1,0:T(8,128)(2,1)}, u32[]{:S(2)}) copy-start(bf16[64,1024]{1,0:T(8,128)(2,1)} %params_ref.1) | copy-start | bytes 393220
  8.2 0.7 %copy-start.2 = (f32[28,16]{0,1:T(8,128)S(1)}, f32[28,16]{0,1:T(8,128)}, u32[]{:S(2)}) copy-start(f32[28,16]{0,1:T(8,128)} %param.10) | copy-start | bytes 5380
  8.9 2.8 %copy-start.1 = (s32[4,128]{1,0:T(4,128)S(1)}, s32[4,128]{1,0:T(4,128)}, u32[]{:S(2)}) copy-start(s32[4,128]{1,0:T(4,128)} %refs_4_.1) | copy-start | bytes 6148
  11.7 4.9 %copy-start.5 = (f32[3,4,256]{2,1,0:T(4,128)S(1)}, f32[3,4,256]{2,1,0:T(4,128)}, u32[]{:S(2)}) copy-start(f32[3,4,256]{2,1,0:T(4,128)} %param.11) | copy-start | bytes 36868
  12.6 5.0 %collective-permute-start.4 = (bf16[64,128]{1,0:T(8,128)(2,1)S(1)}, bf16[64,128]{1,0:T(8,128)(2,1)S(1)}, u32[]{:S(2)}, u32[]{:S(2)}) collective-permute-start(bf16[64,128]{1,0:T(8,128)(2,1)S(1)} %get-tuple-element.16), channel_id=1, source_target_pairs={{0,25},{1,24},{2,27},{3,26},{4,29},{5,28},{6,31},{7,30},{8,17},{9,... | collective-permute-start | bytes 49160 | tf_op jit(solution)/shard_map/ppermute | solution.py:500
  14.5 4.6 %collective-permute-start.5 = (bf16[64,128]{1,0:T(8,128)(2,1)S(1)}, bf16[64,128]{1,0:T(8,128)(2,1)S(1)}, u32[]{:S(2)}, u32[]{:S(2)}) collective-permute-start(bf16[64,128]{1,0:T(8,128)(2,1)S(1)} %get-tuple-element.17), channel_id=1, source_target_pairs={{0,16},{1,17},{2,18},{3,19},{4,20},{5,21},{6,22},{7,23},{8,24},{9,... | collective-permute-start | bytes 49160 | tf_op jit(solution)/shard_map/ppermute | solution.py:500
  14.5 4.6 %collective-permute-start.6 = (bf16[64,128]{1,0:T(8,128)(2,1)S(1)}, bf16[64,128]{1,0:T(8,128)(2,1)S(1)}, u32[]{:S(2)}, u32[]{:S(2)}) collective-permute-start(bf16[64,128]{1,0:T(8,128)(2,1)S(1)} %get-tuple-element.18), channel_id=1, source_target_pairs={{0,9},{1,8},{2,11},{3,10},{4,13},{5,12},{6,15},{7,14},{8,1},{9,0},... | collective-permute-start | bytes 49160 | tf_op jit(solution)/shard_map/ppermute | solution.py:500
  31.5 1.8 %collective-permute-start.7 = (f32[16,16,128]{2,1,0:T(8,128)S(1)}, f32[16,16,128]{2,1,0:T(8,128)S(1)}, u32[]{:S(2)}, u32[]{:S(2)}) collective-permute-start(f32[16,16,128]{2,1,0:T(8,128)S(1)} %all_to_all.5.recv_ref), channel_id=1, source_target_pairs={{0,1},{1,0},{2,3},{3,2},{4,5},{5,4},{6,7},{7,6},{8,9},{9,8},{10,11... | collective-permute-start | bytes 393224 | tf_op jit(solution)/shard_map/ppermute | solution.py:485
